TPU v7x, 256 devices: a whole 4x4x8 slice. The times are simulated.
256 devices in a mesh: dp: 4 (over y), seq: 64 (over z, x, core).
Axes of the slice: x: 4, y: 4, z: 8, core: 2. Of those that a mesh axis runs over, the one named last changes fastest.
Arguments:
- query_rows: bfloat16 [4, 16384, 2048], P('dp', 'seq'), may hold values from -12 to 12
- key_rows: bfloat16 [4, 16384, 2048], P('dp', 'seq'), may hold values from -12 to 12
- value_rows: bfloat16 [4, 16384, 2048], P('dp', 'seq'), may hold values from -6 to 6
- output_grad: bfloat16 [4, 16384, 2048], P('dp', 'seq'), may hold values from -6 to 6
- query_gain: float32 [16, 128], replicated, may hold values from 0.5 to 6
- key_gain: float32 [16, 128], replicated, may hold values from 0.5 to 6
- block_list: int32 [4, 16, 128, 8], P('dp'), may hold values from 0 to 127, as said below
- block_count: int32 [4, 16, 128], P('dp'), may hold values from 1 to 8, as said below
Outputs:
- attended: bfloat16 [4, 16384, 2048], P('dp', 'seq')
- query_grad: bfloat16 [4, 16384, 2048], P('dp', 'seq')
- key_grad: bfloat16 [4, 16384, 2048], P('dp', 'seq')
- value_grad: bfloat16 [4, 16384, 2048], P('dp', 'seq')
- query_gain_grad: float32 [16, 128], replicated
- key_gain_grad: float32 [16, 128], replicated
Inputs may be any that keep to these rules, and one draw needn't show every extreme that they name: `block_list`: for every sample, head and query block the 8 entries are distinct block numbers, and the first is the query block itself. Only the first block_count entries of a list are used. In every sample and head some query block uses all 8.
All inputs are finite; a program needn't handle non-finite values.
Results may differ from a plain program's by a relative error of at most 0.03.
The roundings to bfloat16 on the way count: a program that leaves them out, or rounds other values in their place, can miss the bound.
Values may be sent and summed in bfloat16 or wider, within the bound.
No kernel may reach another device: no remote copies, remote signals or barrier semaphores. Data moves between devices by JAX's collectives and lax.ppermute only.
A program may use at most 128 MiB of HBM per device.

v0:
```python
import math

import jax
import jax.numpy as jnp
from jax import lax
from jax.sharding import PartitionSpec as P

HEADS = 16
HEAD_DIM = 128
BLOCK = 128
MOST = 8


EPS = 1e-06


def inverse_root(wide_rows):
    return lax.rsqrt(jnp.mean(wide_rows * wide_rows, axis=-1, keepdims=True) + EPS)


def norm_backward(wide_rows, row_scale, gain_row, upstream_grad):
    weighted = upstream_grad * gain_row
    inner_mean = jnp.mean(weighted * wide_rows, axis=-1, keepdims=True)
    return row_scale * weighted - wide_rows * (row_scale * row_scale * row_scale) * inner_mean


def to_pieces(token_block, set_count, group_count, local_heads):
    tok_rows = token_block.shape[0]
    shaped = token_block.reshape(
        set_count, tok_rows // set_count, group_count, local_heads, HEAD_DIM
    )
    shaped = jnp.transpose(shaped, (2, 0, 1, 3, 4))
    return shaped.reshape(group_count * set_count, tok_rows // set_count, local_heads, HEAD_DIM)


def from_pieces(pieces, set_count, group_count):
    set_rows = pieces.shape[1]
    local_heads = pieces.shape[2]
    shaped = pieces.reshape(group_count, set_count, set_rows, local_heads, HEAD_DIM)
    shaped = jnp.transpose(shaped, (1, 2, 0, 3, 4))
    return shaped.reshape(set_count * set_rows, group_count * local_heads * HEAD_DIM)


def repeated(token_block, set_count, group_count, local_heads):
    tok_rows = token_block.shape[0]
    shaped = jnp.transpose(
        token_block.reshape(tok_rows, group_count, local_heads, HEAD_DIM), (1, 0, 2, 3)
    )
    shaped = jnp.broadcast_to(
        shaped[:, None], (group_count, set_count, tok_rows, local_heads, HEAD_DIM)
    )
    return shaped.reshape(group_count * set_count, tok_rows, local_heads, HEAD_DIM)


def pick_blocks(block_table, chosen):
    picked = jax.vmap(lambda one_table, one_list: one_table[one_list], in_axes=(0, 1), out_axes=1)(
        block_table, chosen
    )
    return picked.reshape(chosen.shape[0], chosen.shape[1], MOST * BLOCK, HEAD_DIM)


def add_blocks(block_table, chosen, update):
    shaped = update.reshape(update.shape[0], update.shape[1], MOST, BLOCK, HEAD_DIM)
    return jax.vmap(
        lambda one_table, one_list, one_update: one_table.at[one_list].add(one_update),
        in_axes=(0, 1, 1),
    )(block_table, chosen, shaped)


def body(
    query_rows, key_rows, value_rows, output_grad, query_gain, key_gain, block_list, block_count
):
    seq_count = lax.axis_size("seq")
    tok_rows = query_rows.shape[1]
    local_heads = max(1, HEADS // seq_count)
    set_count = max(1, seq_count // HEADS)
    group_count = HEADS // local_heads
    set_rows = tok_rows // set_count
    seq_total = tok_rows * seq_count
    block_total = seq_total // BLOCK
    position = lax.axis_index("seq")
    my_set = position % set_count
    my_group = position // set_count
    inv_root = 1.0 / math.sqrt(HEAD_DIM)
    query_flat = query_rows[0]
    key_flat = key_rows[0]
    value_flat = value_rows[0]
    grad_flat = output_grad[0]
    query_send = to_pieces(query_flat, set_count, group_count, local_heads)
    grad_send = to_pieces(grad_flat, set_count, group_count, local_heads)
    query_head, grad_head, key_dup, value_dup = (
        lax.all_to_all(query_send, "seq", split_axis=0, concat_axis=0, tiled=True),
        lax.all_to_all(grad_send, "seq", split_axis=0, concat_axis=0, tiled=True),
        lax.all_to_all(
            repeated(key_flat, set_count, group_count, local_heads),
            "seq",
            split_axis=0,
            concat_axis=0,
            tiled=True,
        ),
        lax.all_to_all(
            repeated(value_flat, set_count, group_count, local_heads),
            "seq",
            split_axis=0,
            concat_axis=0,
            tiled=True,
        ),
    )
    key_all = key_dup.reshape(seq_total, local_heads, HEAD_DIM)
    value_all = value_dup.reshape(seq_total, local_heads, HEAD_DIM)
    head_start = my_group * local_heads
    gain_query = lax.dynamic_slice_in_dim(query_gain, head_start, local_heads, 0)
    gain_key = lax.dynamic_slice_in_dim(key_gain, head_start, local_heads, 0)
    key_wide_all = key_all.astype(jnp.float32)
    key_norm = (key_wide_all * inverse_root(key_wide_all) * gain_key).astype(jnp.bfloat16)
    key_table = jnp.transpose(
        key_norm.reshape(block_total, BLOCK, local_heads, HEAD_DIM), (2, 0, 1, 3)
    )
    value_table = jnp.transpose(
        value_all.reshape(block_total, BLOCK, local_heads, HEAD_DIM), (2, 0, 1, 3)
    )
    head_lists = lax.dynamic_slice_in_dim(block_list[0], head_start, local_heads, 0)
    head_counts = lax.dynamic_slice_in_dim(block_count[0], head_start, local_heads, 0)
    group_rows = math.gcd(set_rows, BLOCK)
    per_source = set_rows // group_rows
    group_total = seq_count * per_source
    per_step = math.gcd(group_total, max(1, 512 // group_rows))
    step_total = group_total // per_step
    group_index = jnp.arange(group_total, dtype=jnp.int32)
    starts = (
        group_index // per_source * tok_rows
        + my_set * set_rows
        + group_index % per_source * group_rows
    )
    block_numbers = starts // BLOCK
    chooser = (block_numbers[:, None] == jnp.arange(block_total, dtype=jnp.int32)[None, :]).astype(
        jnp.int32
    )
    group_lists = jnp.einsum("gb,hbm->ghm", chooser, head_lists)
    group_counts = jnp.einsum("gb,hb->gh", chooser, head_counts)
    query_steps = query_head.reshape(step_total, per_step, group_rows, local_heads, HEAD_DIM)
    grad_steps = grad_head.reshape(step_total, per_step, group_rows, local_heads, HEAD_DIM)
    list_steps = group_lists.reshape(step_total, per_step, local_heads, MOST)
    count_steps = group_counts.reshape(step_total, per_step, local_heads)

    def attend(carry, inputs):
        key_acc, value_acc, gain_acc = carry
        query_block, grad_block, chosen, live_count = inputs
        query_wide = query_block.astype(jnp.float32)
        query_scale = inverse_root(query_wide)
        query_hat = query_wide * query_scale
        query_norm = (query_hat * gain_query).astype(jnp.bfloat16)
        key_pick = pick_blocks(key_table, chosen)
        value_pick = pick_blocks(value_table, chosen)
        live_mask = jnp.repeat(
            jnp.arange(MOST, dtype=jnp.int32) < live_count[..., None], BLOCK, axis=-1
        )
        scores = (
            jnp.einsum("gqhe,ghke->ghqk", query_norm, key_pick, preferred_element_type=jnp.float32)
            * inv_root
        )
        scores = jnp.where(live_mask[:, :, None, :], scores, -jnp.inf)
        row_max = jnp.max(scores, axis=-1, keepdims=True)
        exp_scores = jnp.exp(scores - row_max)
        weights = (exp_scores / jnp.sum(exp_scores, axis=-1, keepdims=True)).astype(jnp.bfloat16)
        attended_block = jnp.einsum(
            "ghqk,ghke->gqhe", weights, value_pick, preferred_element_type=jnp.float32
        ).astype(jnp.bfloat16)
        weight_grad = jnp.einsum(
            "gqhe,ghke->ghqk", grad_block, value_pick, preferred_element_type=jnp.float32
        )
        row_inner = jnp.sum(
            grad_block.astype(jnp.float32) * attended_block.astype(jnp.float32), axis=-1
        )
        row_inner = jnp.transpose(row_inner, (0, 2, 1))[..., None]
        score_grad = (weights.astype(jnp.float32) * (weight_grad - row_inner)).astype(jnp.bfloat16)
        norm_grad = (
            jnp.einsum("ghqk,ghke->gqhe", score_grad, key_pick, preferred_element_type=jnp.float32)
            * inv_root
        )
        key_term = (
            jnp.einsum(
                "ghqk,gqhe->ghke", score_grad, query_norm, preferred_element_type=jnp.float32
            )
            * inv_root
        )
        value_term = jnp.einsum(
            "ghqk,gqhe->ghke", weights, grad_block, preferred_element_type=jnp.float32
        )
        key_acc = add_blocks(key_acc, chosen, key_term)
        value_acc = add_blocks(value_acc, chosen, value_term)
        gain_acc = gain_acc + jnp.sum(norm_grad * query_hat, axis=(0, 1))
        block_query_grad = norm_backward(query_wide, query_scale, gain_query, norm_grad).astype(
            jnp.bfloat16
        )
        return ((key_acc, value_acc, gain_acc), (attended_block, block_query_grad))

    start_carry = (
        jnp.zeros((local_heads, block_total, BLOCK, HEAD_DIM), jnp.float32),
        jnp.zeros((local_heads, block_total, BLOCK, HEAD_DIM), jnp.float32),
        jnp.zeros((local_heads, HEAD_DIM), jnp.float32),
    )
    final_carry, outputs = lax.scan(
        attend, start_carry, (query_steps, grad_steps, list_steps, count_steps)
    )
    key_acc, value_acc, query_gain_part = final_carry
    attended_head = outputs[0].reshape(seq_count, set_rows, local_heads, HEAD_DIM)
    query_grad_head = outputs[1].reshape(seq_count, set_rows, local_heads, HEAD_DIM)
    attended_back = lax.all_to_all(attended_head, "seq", split_axis=0, concat_axis=0, tiled=True)
    attended = from_pieces(attended_back, set_count, group_count)
    key_round = lax.optimization_barrier(key_acc.astype(jnp.bfloat16))
    value_round = lax.optimization_barrier(value_acc.astype(jnp.bfloat16))
    key_seq = jnp.transpose(key_round, (1, 2, 0, 3)).reshape(seq_total, local_heads, HEAD_DIM)
    value_seq = jnp.transpose(value_round, (1, 2, 0, 3)).reshape(seq_total, local_heads, HEAD_DIM)
    zero_gains = jnp.zeros((HEADS, HEAD_DIM), jnp.float32)
    query_gain_full = lax.dynamic_update_slice_in_dim(zero_gains, query_gain_part, head_start, 0)
    key_send = key_seq.reshape(seq_count, tok_rows, local_heads, HEAD_DIM)
    value_send = value_seq.reshape(seq_count, tok_rows, local_heads, HEAD_DIM)
    query_back, key_back, value_back = (
        lax.all_to_all(query_grad_head, "seq", split_axis=0, concat_axis=0, tiled=True),
        lax.all_to_all(key_send, "seq", split_axis=0, concat_axis=0, tiled=True),
        lax.all_to_all(value_send, "seq", split_axis=0, concat_axis=0, tiled=True),
    )
    key_sum = jnp.sum(
        key_back.astype(jnp.float32).reshape(
            group_count, set_count, tok_rows, local_heads, HEAD_DIM
        ),
        axis=1,
    )
    value_sum = jnp.sum(
        value_back.astype(jnp.float32).reshape(
            group_count, set_count, tok_rows, local_heads, HEAD_DIM
        ),
        axis=1,
    )
    key_total = jnp.transpose(key_sum, (1, 0, 2, 3)).reshape(tok_rows, HEADS, HEAD_DIM)
    value_grad = (
        jnp.transpose(value_sum, (1, 0, 2, 3))
        .reshape(tok_rows, HEADS * HEAD_DIM)
        .astype(jnp.bfloat16)
    )
    key_broadened = key_flat.astype(jnp.float32).reshape(tok_rows, HEADS, HEAD_DIM)
    key_scale = inverse_root(key_broadened)
    key_grad = (
        norm_backward(key_broadened, key_scale, key_gain, key_total)
        .astype(jnp.bfloat16)
        .reshape(tok_rows, HEADS * HEAD_DIM)
    )
    key_gain_full = jnp.sum(key_total * key_broadened * key_scale, axis=0)
    query_grad = from_pieces(query_back, set_count, group_count)
    query_gain_grad, key_gain_grad = lax.psum((query_gain_full, key_gain_full), ("dp", "seq"))
    return (
        attended[None],
        query_grad[None],
        key_grad[None],
        value_grad[None],
        query_gain_grad,
        key_gain_grad,
    )


def solution(mesh):
    return jax.shard_map(
        body,
        mesh=mesh,
        in_specs=(
            P("dp", "seq", None),
            P("dp", "seq", None),
            P("dp", "seq", None),
            P("dp", "seq", None),
            P(),
            P(),
            P("dp", None, None, None),
            P("dp", None, None),
        ),
        out_specs=(
            P("dp", "seq", None),
            P("dp", "seq", None),
            P("dp", "seq", None),
            P("dp", "seq", None),
            P(),
            P(),
        ),
        check_vma=False,
    )
```

profile of v0, /device:TPU:16, one launch (start us, length us, event | category | flops | bytes accessed | tf_op | source)
XLA Modules:
  0.0 1059.5 jit_solution(1371810830710295593)
XLA Ops:
  3.4 11.9 %all-to-all-start = ((bf16[64,64,1,128]{3,1,2,0:T(8,128)(2,1)}), bf16[64,64,1,128]{3,1,2,0:T(8,128)(2,1)S(1)}, u32[]{:S(2)}, u32[]{:S(2)}) async-start(bf16[64,64,1,128]{3,1,2,0:T(8,128)(2,1)} %bitcast.12), calls=%async_computation | async-start | bytes 2097152 | tf_op jit(solution)/shard_map/all_to_all | solution.py:92
  16.8 27.4 %all-to-all-done = bf16[64,64,1,128]{3,1,2,0:T(8,128)(2,1)S(1)} async-done(((bf16[64,64,1,128]{3,1,2,0:T(8,128)(2,1)}), bf16[64,64,1,128]{3,1,2,0:T(8,128)(2,1)S(1)}, u32[]{:S(2)}, u32[]{:S(2)}) %all-to-all-start) | async-done | bytes 1048608 | tf_op jit(solution)/shard_map/all_to_all | solution.py:92
  44.2 5.6 all-to-all-start.2
  50.3 28.4 %all-to-all-done.2 = bf16[64,64,1,128]{3,1,2,0:T(8,128)(2,1)S(1)} async-done(((bf16[64,64,1,128]{3,1,2,0:T(8,128)(2,1)}), bf16[64,64,1,128]{3,1,2,0:T(8,128)(2,1)S(1)}, u32[]{:S(2)}, u32[]{:S(2)}) %all-to-all-start.2) | async-done | bytes 1048608 | tf_op jit(solution)/shard_map/all_to_all | solution.py:93
  81.7 6.0 all-to-all-start.1
  88.2 95.7 %all-to-all-done.1 = bf16[64,256,1,128]{3,1,2,0:T(8,128)(2,1)} async-done(((bf16[64,256,1,128]{3,1,2,0:T(8,128)(2,1)}), bf16[64,256,1,128]{3,1,2,0:T(8,128)(2,1)}, u32[]{:S(2)}, u32[]{:S(2)}) %all-to-all-start.1) | async-done | bytes 4194336 | tf_op jit(solution)/shard_map/all_to_all | solution.py:94
  186.8 6.0 all-to-all-start.3
  195.0 4.4 multiply_reduce_fusion
  199.5 5.8 multiply_convert_fusion.1
  205.3 83.6 %all-to-all-done.3 = bf16[64,256,1,128]{3,1,2,0:T(8,128)(2,1)} async-done(((bf16[64,256,1,128]{3,1,2,0:T(8,128)(2,1)}), bf16[64,256,1,128]{3,1,2,0:T(8,128)(2,1)}, u32[]{:S(2)}, u32[]{:S(2)}) %all-to-all-start.3) | async-done | bytes 4194336 | tf_op jit(solution)/shard_map/all_to_all | solution.py:101
  288.9 4.3 broadcast.339
  293.1 4.3 broadcast.339.clone
  297.4 409.7 %while.19 = (s32[]{:T(128)}, f32[1,128,128,128]{3,2,1,0:T(8,128)}, f32[1,128,128,128]{3,2,1,0:T(8,128)}, f32[1,128]{1,0:T(1,128)S(1)}, bf16[8,8,64,1,128]{4,2,1,...) while((s32[]{:T(128)}, f32[1,128,128,128]{3,2,1,0:T(8,128)}, ...), condition=%wide.region_10.11_spmd.clone, body=%wide.region_1.10_spmd.clone.sunk | while | flops 815729600 | bytes 97584952 | solution.py:203
  298.4 3.1 gather_fusion
  305.9 3.1 gather_fusion.1
  318.0 13.4 %scatter_fusion = f32[128,128,128]{2,1,0:T(8,128)} fusion(f32[128,128,128]{2,1,0:T(8,128)} %bitcast.314, s32[64]{0:T(128)S(1)} %reshape.648, f32[64,128,128]{2,1,0:T(8,128)} %bitcast.310), kind=kCustom, calls=%fused_computation.2.clone.clone.1 | custom fusion | flops 1048576 | bytes 12583168 | tf_op jit(solution)/shard_map/while/body/eval_jaxpr/vmap()/scatter-add | solution.py:65
  331.4 3.7 fusion.110
  335.1 13.5 %scatter_fusion.1 = f32[128,128,128]{2,1,0:T(8,128)} fusion(f32[128,128,128]{2,1,0:T(8,128)} %bitcast.316, s32[64]{0:T(128)S(1)} %reshape.648, f32[64,128,128]{2,1,0:T(8,128)} %bitcast.311), kind=kCustom, calls=%fused_computation.3.clone.clone.1 | custom fusion | flops 1048576 | bytes 12583168 | tf_op jit(solution)/shard_map/while/body/eval_jaxpr/vmap()/scatter-add | solution.py:65
  349.6 3.1 gather_fusion
  357.0 3.1 gather_fusion.1
  369.1 13.5 %scatter_fusion = f32[128,128,128]{2,1,0:T(8,128)} fusion(f32[128,128,128]{2,1,0:T(8,128)} %bitcast.314, s32[64]{0:T(128)S(1)} %reshape.648, f32[64,128,128]{2,1,0:T(8,128)} %bitcast.310), kind=kCustom, calls=%fused_computation.2.clone.clone.1 | custom fusion | flops 1048576 | bytes 12583168 | tf_op jit(solution)/shard_map/while/body/eval_jaxpr/vmap()/scatter-add | solution.py:65
  382.6 3.7 fusion.110
  386.3 13.5 %scatter_fusion.1 = f32[128,128,128]{2,1,0:T(8,128)} fusion(f32[128,128,128]{2,1,0:T(8,128)} %bitcast.316, s32[64]{0:T(128)S(1)} %reshape.648, f32[64,128,128]{2,1,0:T(8,128)} %bitcast.311), kind=kCustom, calls=%fused_computation.3.clone.clone.1 | custom fusion | flops 1048576 | bytes 12583168 | tf_op jit(solution)/shard_map/while/body/eval_jaxpr/vmap()/scatter-add | solution.py:65
  400.8 3.1 gather_fusion
  408.3 3.1 gather_fusion.1
  420.4 13.5 %scatter_fusion = f32[128,128,128]{2,1,0:T(8,128)} fusion(f32[128,128,128]{2,1,0:T(8,128)} %bitcast.314, s32[64]{0:T(128)S(1)} %reshape.648, f32[64,128,128]{2,1,0:T(8,128)} %bitcast.310), kind=kCustom, calls=%fused_computation.2.clone.clone.1 | custom fusion | flops 1048576 | bytes 12583168 | tf_op jit(solution)/shard_map/while/body/eval_jaxpr/vmap()/scatter-add | solution.py:65
  433.9 3.7 fusion.110
  437.5 13.5 %scatter_fusion.1 = f32[128,128,128]{2,1,0:T(8,128)} fusion(f32[128,128,128]{2,1,0:T(8,128)} %bitcast.316, s32[64]{0:T(128)S(1)} %reshape.648, f32[64,128,128]{2,1,0:T(8,128)} %bitcast.311), kind=kCustom, calls=%fused_computation.3.clone.clone.1 | custom fusion | flops 1048576 | bytes 12583168 | tf_op jit(solution)/shard_map/while/body/eval_jaxpr/vmap()/scatter-add | solution.py:65
  452.0 3.1 gather_fusion
  459.5 3.1 gather_fusion.1
  471.6 13.4 %scatter_fusion = f32[128,128,128]{2,1,0:T(8,128)} fusion(f32[128,128,128]{2,1,0:T(8,128)} %bitcast.314, s32[64]{0:T(128)S(1)} %reshape.648, f32[64,128,128]{2,1,0:T(8,128)} %bitcast.310), kind=kCustom, calls=%fused_computation.2.clone.clone.1 | custom fusion | flops 1048576 | bytes 12583168 | tf_op jit(solution)/shard_map/while/body/eval_jaxpr/vmap()/scatter-add | solution.py:65
  485.1 3.7 fusion.110
  488.8 13.4 %scatter_fusion.1 = f32[128,128,128]{2,1,0:T(8,128)} fusion(f32[128,128,128]{2,1,0:T(8,128)} %bitcast.316, s32[64]{0:T(128)S(1)} %reshape.648, f32[64,128,128]{2,1,0:T(8,128)} %bitcast.311), kind=kCustom, calls=%fused_computation.3.clone.clone.1 | custom fusion | flops 1048576 | bytes 12583168 | tf_op jit(solution)/shard_map/while/body/eval_jaxpr/vmap()/scatter-add | solution.py:65
  503.2 3.1 gather_fusion
  510.6 3.1 gather_fusion.1
  522.7 13.5 %scatter_fusion = f32[128,128,128]{2,1,0:T(8,128)} fusion(f32[128,128,128]{2,1,0:T(8,128)} %bitcast.314, s32[64]{0:T(128)S(1)} %reshape.648, f32[64,128,128]{2,1,0:T(8,128)} %bitcast.310), kind=kCustom, calls=%fused_computation.2.clone.clone.1 | custom fusion | flops 1048576 | bytes 12583168 | tf_op jit(solution)/shard_map/while/body/eval_jaxpr/vmap()/scatter-add | solution.py:65
  536.2 3.7 fusion.110
  539.9 13.6 %scatter_fusion.1 = f32[128,128,128]{2,1,0:T(8,128)} fusion(f32[128,128,128]{2,1,0:T(8,128)} %bitcast.316, s32[64]{0:T(128)S(1)} %reshape.648, f32[64,128,128]{2,1,0:T(8,128)} %bitcast.311), kind=kCustom, calls=%fused_computation.3.clone.clone.1 | custom fusion | flops 1048576 | bytes 12583168 | tf_op jit(solution)/shard_map/while/body/eval_jaxpr/vmap()/scatter-add | solution.py:65
  554.5 3.1 gather_fusion
  562.0 3.1 gather_fusion.1
  574.1 13.5 %scatter_fusion = f32[128,128,128]{2,1,0:T(8,128)} fusion(f32[128,128,128]{2,1,0:T(8,128)} %bitcast.314, s32[64]{0:T(128)S(1)} %reshape.648, f32[64,128,128]{2,1,0:T(8,128)} %bitcast.310), kind=kCustom, calls=%fused_computation.2.clone.clone.1 | custom fusion | flops 1048576 | bytes 12583168 | tf_op jit(solution)/shard_map/while/body/eval_jaxpr/vmap()/scatter-add | solution.py:65
  587.6 3.7 fusion.110
  591.3 13.5 %scatter_fusion.1 = f32[128,128,128]{2,1,0:T(8,128)} fusion(f32[128,128,128]{2,1,0:T(8,128)} %bitcast.316, s32[64]{0:T(128)S(1)} %reshape.648, f32[64,128,128]{2,1,0:T(8,128)} %bitcast.311), kind=kCustom, calls=%fused_computation.3.clone.clone.1 | custom fusion | flops 1048576 | bytes 12583168 | tf_op jit(solution)/shard_map/while/body/eval_jaxpr/vmap()/scatter-add | solution.py:65
  605.7 3.1 gather_fusion
  613.2 3.1 gather_fusion.1
  625.3 13.5 %scatter_fusion = f32[128,128,128]{2,1,0:T(8,128)} fusion(f32[128,128,128]{2,1,0:T(8,128)} %bitcast.314, s32[64]{0:T(128)S(1)} %reshape.648, f32[64,128,128]{2,1,0:T(8,128)} %bitcast.310), kind=kCustom, calls=%fused_computation.2.clone.clone.1 | custom fusion | flops 1048576 | bytes 12583168 | tf_op jit(solution)/shard_map/while/body/eval_jaxpr/vmap()/scatter-add | solution.py:65
  638.8 3.7 fusion.110
  642.5 13.4 %scatter_fusion.1 = f32[128,128,128]{2,1,0:T(8,128)} fusion(f32[128,128,128]{2,1,0:T(8,128)} %bitcast.316, s32[64]{0:T(128)S(1)} %reshape.648, f32[64,128,128]{2,1,0:T(8,128)} %bitcast.311), kind=kCustom, calls=%fused_computation.3.clone.clone.1 | custom fusion | flops 1048576 | bytes 12583168 | tf_op jit(solution)/shard_map/while/body/eval_jaxpr/vmap()/scatter-add | solution.py:65
  656.9 3.1 gather_fusion
  664.4 3.1 gather_fusion.1
  676.5 13.4 %scatter_fusion = f32[128,128,128]{2,1,0:T(8,128)} fusion(f32[128,128,128]{2,1,0:T(8,128)} %bitcast.314, s32[64]{0:T(128)S(1)} %reshape.648, f32[64,128,128]{2,1,0:T(8,128)} %bitcast.310), kind=kCustom, calls=%fused_computation.2.clone.clone.1 | custom fusion | flops 1048576 | bytes 12583168 | tf_op jit(solution)/shard_map/while/body/eval_jaxpr/vmap()/scatter-add | solution.py:65
  689.9 3.7 fusion.110
  693.6 13.4 %scatter_fusion.1 = f32[128,128,128]{2,1,0:T(8,128)} fusion(f32[128,128,128]{2,1,0:T(8,128)} %bitcast.316, s32[64]{0:T(128)S(1)} %reshape.648, f32[64,128,128]{2,1,0:T(8,128)} %bitcast.311), kind=kCustom, calls=%fused_computation.3.clone.clone.1 | custom fusion | flops 1048576 | bytes 12583168 | tf_op jit(solution)/shard_map/while/body/eval_jaxpr/vmap()/scatter-add | solution.py:65
  707.1 34.7 %all_to_all.40 = bf16[64,64,1,128]{3,1,2,0:T(8,128)(2,1)} all-to-all(bf16[64,64,1,128]{3,1,2,0:T(8,128)(2,1)} %bitcast.340), channel_id=1, replica_groups=mesh['dp'=4,'seq'=64] {'seq'}, dimensions={0} | all-to-all | bytes 2097152 | tf_op jit(solution)/shard_map/all_to_all | solution.py:209
  741.8 5.6 all-to-all-start.5
  747.4 6.3 convert_element_type.165
  753.7 22.5 %all-to-all-done.5 = bf16[64,64,1,128]{3,1,2,0:T(8,128)(2,1)S(1)} async-done(((bf16[64,64,1,128]{3,1,2,0:T(8,128)(2,1)}), bf16[64,64,1,128]{3,1,2,0:T(8,128)(2,1)S(1)}, u32[]{:S(2)}, u32[]{:S(2)}) %all-to-all-start.5) | async-done | bytes 1048608 | tf_op jit(solution)/shard_map/all_to_all | solution.py:220
  776.3 5.8 all-to-all-start.6
  782.1 6.3 convert_element_type.168
  788.4 89.9 %all-to-all-done.6 = bf16[64,256,1,128]{3,1,2,0:T(8,128)(2,1)} async-done(((bf16[64,256,1,128]{3,1,2,0:T(8,128)(2,1)}), bf16[64,256,1,128]{3,1,2,0:T(8,128)(2,1)}, u32[]{:S(2)}, u32[]{:S(2)}) %all-to-all-start.6) | async-done | bytes 4194336 | tf_op jit(solution)/shard_map/all_to_all | solution.py:221
  878.4 5.8 all-to-all-start.7
  892.9 3.1 convert_reduce_fusion
  902.5 77.9 %all-to-all-done.7 = bf16[64,256,1,128]{3,1,2,0:T(8,128)(2,1)} async-done(((bf16[64,256,1,128]{3,1,2,0:T(8,128)(2,1)}), bf16[64,256,1,128]{3,1,2,0:T(8,128)(2,1)}, u32[]{:S(2)}, u32[]{:S(2)}) %all-to-all-start.7) | async-done | bytes 4194336 | tf_op jit(solution)/shard_map/all_to_all | solution.py:222
  985.4 74.1 %all-reduce = (f32[16,128]{1,0:T(8,128)}, f32[16,128]{1,0:T(8,128)}) all-reduce(f32[16,128]{1,0:T(8,128)S(1)} %dynamic_update_slice.10, f32[16,128]{1,0:T(8,128)S(1)} %get-tuple-element.197), channel_id=1, replica_groups=mesh['dp'=4,'seq'=64] {'dp','seq'}, use_global_device_ids=true, to_apply=%region_15.16 | all-reduce | flops 4096 | bytes 32768 | tf_op jit(solution)/shard_map/psum | solution.py:251
  (312 shorter events, 146.5 us)
Async XLA Ops:
  0.6 193.0 %copy-start = (s32[1,16,128,8]{2,3,1,0:T(8,128)S(1)}, s32[1,16,128,8]{2,3,1,0:T(8,128)}, u32[]{:S(2)}) copy-start(s32[1,16,128,8]{2,3,1,0:T(8,128)} %param.16) | copy-start | bytes 196612
  2.1 13.2 %copy-start.12 = (bf16[1,256,2048]{2,1,0:T(8,128)(2,1)S(1)}, bf16[1,256,2048]{2,1,0:T(8,128)(2,1)}, u32[]{:S(2)}) copy-start(bf16[1,256,2048]{2,1,0:T(8,128)(2,1)} %param.13) | copy-start | bytes 3145732
  3.4 40.8 %all-to-all-start = ((bf16[64,64,1,128]{3,1,2,0:T(8,128)(2,1)}), bf16[64,64,1,128]{3,1,2,0:T(8,128)(2,1)S(1)}, u32[]{:S(2)}, u32[]{:S(2)}) async-start(bf16[64,64,1,128]{3,1,2,0:T(8,128)(2,1)} %bitcast.12), calls=%async_computation | async-start | bytes 2097152 | tf_op jit(solution)/shard_map/all_to_all | solution.py:92
  15.6 34.2 %copy-start.9 = (bf16[1,256,2048]{2,1,0:T(8,128)(2,1)S(1)}, bf16[1,256,2048]{2,1,0:T(8,128)(2,1)}, u32[]{:S(2)}) copy-start(bf16[1,256,2048]{2,1,0:T(8,128)(2,1)} %param.11) | copy-start | bytes 3145732
  44.2 34.5 %all-to-all-start.2 = ((bf16[64,64,1,128]{3,1,2,0:T(8,128)(2,1)}), bf16[64,64,1,128]{3,1,2,0:T(8,128)(2,1)S(1)}, u32[]{:S(2)}, u32[]{:S(2)}) async-start(bf16[64,64,1,128]{3,1,2,0:T(8,128)(2,1)} %bitcast.330), calls=%async_computation.2 | async-start | bytes 2097152 | tf_op jit(solution)/shard_map/all_to_all | solution.py:93
  81.7 6.0 copy-start.13
  81.7 102.2 %all-to-all-start.1 = ((bf16[64,256,1,128]{3,1,2,0:T(8,128)(2,1)}), bf16[64,256,1,128]{3,1,2,0:T(8,128)(2,1)}, u32[]{:S(2)}, u32[]{:S(2)}) async-start(bf16[64,256,1,128]{3,1,2,0:T(8,128)(2,1)} %bitcast.322), calls=%async_computation.1 | async-start | bytes 8388608 | tf_op jit(solution)/shard_map/all_to_all | solution.py:94
  186.8 6.1 copy-start.14
  186.8 102.0 %all-to-all-start.3 = ((bf16[64,256,1,128]{3,1,2,0:T(8,128)(2,1)}), bf16[64,256,1,128]{3,1,2,0:T(8,128)(2,1)}, u32[]{:S(2)}, u32[]{:S(2)}) async-start(bf16[64,256,1,128]{3,1,2,0:T(8,128)(2,1)} %bitcast.321), calls=%async_computation.3 | async-start | bytes 8388608 | tf_op jit(solution)/shard_map/all_to_all | solution.py:101
  297.4 1.0 copy-start.6
  297.4 4.2 copy-start.4
  301.5 2.4 copy-start.2
  310.5 1.9 copy-start.3
  312.4 1.6 copy-start.5
  335.1 13.5 %copy-start.7 = (bf16[8,8,64,1,128]{4,2,1,3,0:T(8,128)(2,1)S(1)}, bf16[8,8,64,1,128]{4,2,1,3,0:T(8,128)(2,1)}, u32[]{:S(2)}) copy-start(bf16[8,8,64,1,128]{4,2,1,3,0:T(8,128)(2,1)} %copy-done.6) | copy-start | bytes 3145732 | tf_op jit(solution)/shard_map/while
  348.6 1.0 copy-start.6
  348.6 4.2 copy-start.4
  352.7 2.4 copy-start.2
  361.7 1.9 copy-start.3
  363.6 1.6 copy-start.5
  386.3 13.5 %copy-start.7 = (bf16[8,8,64,1,128]{4,2,1,3,0:T(8,128)(2,1)S(1)}, bf16[8,8,64,1,128]{4,2,1,3,0:T(8,128)(2,1)}, u32[]{:S(2)}) copy-start(bf16[8,8,64,1,128]{4,2,1,3,0:T(8,128)(2,1)} %copy-done.6) | copy-start | bytes 3145732 | tf_op jit(solution)/shard_map/while
  399.8 1.0 copy-start.6
  399.8 4.2 copy-start.4
  403.9 2.4 copy-start.2
  412.9 1.9 copy-start.3
  414.8 1.6 copy-start.5
  437.5 13.5 %copy-start.7 = (bf16[8,8,64,1,128]{4,2,1,3,0:T(8,128)(2,1)S(1)}, bf16[8,8,64,1,128]{4,2,1,3,0:T(8,128)(2,1)}, u32[]{:S(2)}) copy-start(bf16[8,8,64,1,128]{4,2,1,3,0:T(8,128)(2,1)} %copy-done.6) | copy-start | bytes 3145732 | tf_op jit(solution)/shard_map/while
  451.1 1.0 copy-start.6
  451.1 4.2 copy-start.4
  455.2 2.4 copy-start.2
  464.1 1.9 copy-start.3
  466.1 1.6 copy-start.5
  488.8 13.4 %copy-start.7 = (bf16[8,8,64,1,128]{4,2,1,3,0:T(8,128)(2,1)S(1)}, bf16[8,8,64,1,128]{4,2,1,3,0:T(8,128)(2,1)}, u32[]{:S(2)}) copy-start(bf16[8,8,64,1,128]{4,2,1,3,0:T(8,128)(2,1)} %copy-done.6) | copy-start | bytes 3145732 | tf_op jit(solution)/shard_map/while
  502.2 1.0 copy-start.6
  502.2 4.2 copy-start.4
  506.3 2.4 copy-start.2
  515.3 1.9 copy-start.3
  517.2 1.6 copy-start.5
  539.9 13.6 %copy-start.7 = (bf16[8,8,64,1,128]{4,2,1,3,0:T(8,128)(2,1)S(1)}, bf16[8,8,64,1,128]{4,2,1,3,0:T(8,128)(2,1)}, u32[]{:S(2)}) copy-start(bf16[8,8,64,1,128]{4,2,1,3,0:T(8,128)(2,1)} %copy-done.6) | copy-start | bytes 3145732 | tf_op jit(solution)/shard_map/while
  553.5 1.0 copy-start.6
  553.5 4.2 copy-start.4
  557.6 2.4 copy-start.2
  566.6 1.9 copy-start.3
  568.5 1.6 copy-start.5
  591.3 13.5 %copy-start.7 = (bf16[8,8,64,1,128]{4,2,1,3,0:T(8,128)(2,1)S(1)}, bf16[8,8,64,1,128]{4,2,1,3,0:T(8,128)(2,1)}, u32[]{:S(2)}) copy-start(bf16[8,8,64,1,128]{4,2,1,3,0:T(8,128)(2,1)} %copy-done.6) | copy-start | bytes 3145732 | tf_op jit(solution)/shard_map/while
  604.8 1.0 copy-start.6
  604.8 4.2 copy-start.4
  608.9 2.4 copy-start.2
  617.8 1.9 copy-start.3
  619.8 1.6 copy-start.5
  642.5 13.5 %copy-start.7 = (bf16[8,8,64,1,128]{4,2,1,3,0:T(8,128)(2,1)S(1)}, bf16[8,8,64,1,128]{4,2,1,3,0:T(8,128)(2,1)}, u32[]{:S(2)}) copy-start(bf16[8,8,64,1,128]{4,2,1,3,0:T(8,128)(2,1)} %copy-done.6) | copy-start | bytes 3145732 | tf_op jit(solution)/shard_map/while
  656.0 1.0 copy-start.6
  656.0 4.2 copy-start.4
  660.1 2.4 copy-start.2
  669.0 1.9 copy-start.3
  670.9 1.6 copy-start.5
  693.6 13.5 %copy-start.7 = (bf16[8,8,64,1,128]{4,2,1,3,0:T(8,128)(2,1)S(1)}, bf16[8,8,64,1,128]{4,2,1,3,0:T(8,128)(2,1)}, u32[]{:S(2)}) copy-start(bf16[8,8,64,1,128]{4,2,1,3,0:T(8,128)(2,1)} %copy-done.6) | copy-start | bytes 3145732 | tf_op jit(solution)/shard_map/while
  741.8 34.5 %all-to-all-start.5 = ((bf16[64,64,1,128]{3,1,2,0:T(8,128)(2,1)}), bf16[64,64,1,128]{3,1,2,0:T(8,128)(2,1)S(1)}, u32[]{:S(2)}, u32[]{:S(2)}) async-start(bf16[64,64,1,128]{3,1,2,0:T(8,128)(2,1)} %bitcast.31), calls=%async_computation.5 | async-start | bytes 2097152 | tf_op jit(solution)/shard_map/all_to_all | solution.py:220
  776.3 102.1 %all-to-all-start.6 = ((bf16[64,256,1,128]{3,1,2,0:T(8,128)(2,1)}), bf16[64,256,1,128]{3,1,2,0:T(8,128)(2,1)}, u32[]{:S(2)}, u32[]{:S(2)}) async-start(bf16[64,256,1,128]{3,1,2,0:T(8,128)(2,1)} %bitcast.320), calls=%async_computation.6 | async-start | bytes 8388608 | tf_op jit(solution)/shard_map/all_to_all | solution.py:221
  878.4 5.8 copy-start.10
  878.4 102.0 %all-to-all-start.7 = ((bf16[64,256,1,128]{3,1,2,0:T(8,128)(2,1)}), bf16[64,256,1,128]{3,1,2,0:T(8,128)(2,1)}, u32[]{:S(2)}, u32[]{:S(2)}) async-start(bf16[64,256,1,128]{3,1,2,0:T(8,128)(2,1)} %bitcast.319), calls=%async_computation.7 | async-start | bytes 8388608 | tf_op jit(solution)/shard_map/all_to_all | solution.py:222
  884.7 2.3 copy-start.11
  897.9 2.7 copy-start.8
  983.5 76.0 %copy-start.1 = (s32[1,16,128,8]{2,3,1,0:T(8,128)S(1)}, s32[1,16,128,8]{2,3,1,0:T(8,128)}, u32[]{:S(2)}) copy-start(s32[1,16,128,8]{2,3,1,0:T(8,128)} %param.16) | copy-start | bytes 196612
where the time goes:
time: 1070 us; the launch traced here: 1060 us
  waiting for transfers between devices  425 us (40%)
  other arithmetic  272 us (25%)
  matrix products  112 us (10%)
  blocking collectives  109 us (10%)
  local copies, waits for them, and re-layouts  91.8 us (9%)
  starting transfers between devices  46.6 us (4%)
    scatter-add x24, other arithmetic, add_blocks(): one_table.at[one_list].add(one_update)  216 us
    all_to_all x1, waiting for transfers between devices, body(): lax.all_to_all(repeated(key_flat, set_count, group_count, local_heads), '...  95.7 us
    all_to_all x1, waiting for transfers between devices, body(): lax.all_to_all(key_send, 'seq', split_axis=0, concat_axis=0, tiled=True)  89.9 us
    all_to_all x1, waiting for transfers between devices, body(): lax.all_to_all(repeated(value_flat, set_count, group_count, local_heads),...  83.6 us
    all_to_all x1, waiting for transfers between devices, body(): lax.all_to_all(value_send, 'seq', split_axis=0, concat_axis=0, tiled=True)  77.9 us
    psum x1, blocking collectives, body(): lax.psum((query_gain_full, key_gain_full), ('dp', 'seq'))  74.1 us
    gather x16, local copies, waits for them, and re-layouts, pick_blocks(): one_table[one_list]  50.2 us
    all_to_all x1, blocking collectives, body(): lax.all_to_all(attended_head, 'seq', split_axis=0, concat_axis=0, tiled=T...  34.7 us
  transfers between devices with their start and end apart: 7, of which 7 were waited for; matrix products, arithmetic and copies ran while one was open for 4% of the time, Pallas kernels for 0%

commit v1 on v0

v1 whole, which is shorter than its diff:
```python
import functools, math
import jax
import jax.numpy as jnp
from jax import lax
from jax.experimental import pallas as pl
from jax.experimental.pallas import tpu as pltpu
from jax.sharding import PartitionSpec as P

HEAD_DIM = 128
EPS = 1e-06
INV_ROOT = 1.0 / math.sqrt(HEAD_DIM)
NT = (((1,), (1,)), ((), ()))
TN = (((0,), (0,)), ((), ()))
NN = (((1,), (0,)), ((), ()))


def dot(a, b, dims):
    return lax.dot_general(a, b, dims, preferred_element_type=jnp.float32)


def attend_kernel(order_ref, count_ref, list_ref, bound_ref, kv0, kv1, kv2, kv3, qg_ref, gains_ref,
                  og_ref, p0, p1, p2, p3, gain_ref, ktab, vtab, acck, accv, sems, *, per_step, buckets):
    pieces = (kv0, kv1, kv2, kv3)
    copies = []
    for i, piece in enumerate(pieces):
        where = pl.ds((i % 2) * 64, 64)
        rows = pl.ds((i // 2) * 64, 64)
        for j, table in enumerate((ktab, vtab)):
            copies.append(pltpu.make_async_copy(piece.at[:, j], table.at[where, rows], sems.at[2 * i + j]))
    for copy in copies:
        copy.start()

    @pl.loop(0, 128)
    def _(t):
        acck[t] = jnp.zeros((128, 128), jnp.float32)
        accv[t] = jnp.zeros((128, 128), jnp.float32)

    gain_query = gains_ref[0:1, :]
    gain_key = gains_ref[1:2, :]
    gain_ref[...] = jnp.zeros_like(gain_ref)
    for copy in copies:
        copy.wait()

    @pl.loop(0, 128, unroll=2)
    def _(t):
        wide = ktab[t].astype(jnp.float32)
        scale = lax.rsqrt(jnp.mean(wide * wide, axis=-1, keepdims=True) + EPS)
        ktab[t] = (wide * scale * gain_key).astype(jnp.bfloat16)

    def one_group(i, most):
        g = order_ref[i]
        live = count_ref[i]
        spots = [list_ref[i * 8 + j] for j in range(most)]
        wide = qg_ref[g, 0].astype(jnp.float32)
        grad = qg_ref[g, 1]
        scale = lax.rsqrt(jnp.mean(wide * wide, axis=-1, keepdims=True) + EPS)
        hat = wide * scale
        normed = (hat * gain_query).astype(jnp.bfloat16)
        keys = [ktab[t] for t in spots]
        values = [vtab[t] for t in spots]
        scores = []
        for j in range(most):
            s = dot(normed, keys[j], NT) * INV_ROOT
            if j:
                s = jnp.where(j < live, s, -jnp.inf)
            scores.append(s)
        top = jnp.max(functools.reduce(jnp.maximum, scores), axis=-1, keepdims=True)
        exps = [jnp.exp(s - top) for s in scores]
        total = jnp.sum(functools.reduce(jnp.add, exps), axis=-1, keepdims=True)
        inverse = 1.0 / total
        weights = [(e * inverse).astype(jnp.bfloat16) for e in exps]
        attended = functools.reduce(jnp.add, [dot(w, v, NN) for w, v in zip(weights, values)]).astype(jnp.bfloat16)
        og_ref[g, 0] = attended
        inner = jnp.sum(grad.astype(jnp.float32) * attended.astype(jnp.float32), axis=-1, keepdims=True)
        score_grads = []
        for j in range(most):
            wg = dot(grad, values[j], NT)
            score_grads.append((weights[j].astype(jnp.float32) * (wg - inner)).astype(jnp.bfloat16))
        norm_grad = functools.reduce(jnp.add, [dot(s, k, NN) for s, k in zip(score_grads, keys)]) * INV_ROOT
        for j in range(most):
            acck[spots[j]] += dot(score_grads[j], normed, TN)
            accv[spots[j]] += dot(weights[j], grad, TN)
        gain_ref[0:1, :] += jnp.sum(norm_grad * hat, axis=0, keepdims=True)
        weighted = norm_grad * gain_query
        mean = jnp.mean(weighted * wide, axis=-1, keepdims=True)
        og_ref[g, 1] = (scale * weighted - wide * (scale * scale * scale) * mean).astype(jnp.bfloat16)

    start = 0
    for which, most in enumerate(buckets):
        stop = bound_ref[which]

        @pl.loop(start, stop)
        def _(step, most=most):
            for u in range(per_step):
                one_group(step * per_step + u, most)

        start = stop

    outs = (p0, p1, p2, p3)

    @pl.loop(0, 64)
    def _(s):
        for x in range(2):
            k = acck[x * 64 + s] * INV_ROOT
            v = accv[x * 64 + s]
            for c in range(2):
                outs[2 * c + x][s, 0] = k[c * 64:(c + 1) * 64].astype(jnp.bfloat16)
                outs[2 * c + x][s, 1] = v[c * 64:(c + 1) * 64].astype(jnp.bfloat16)


def attend(order, counts, lists, bounds, kv0, kv1, kv2, kv3, qg, gains, per_step=2, buckets=(8, 6, 4, 2)):
    smem = pl.BlockSpec(memory_space=pltpu.SMEM)
    vmem = pl.BlockSpec(memory_space=pltpu.VMEM)
    hbm = pl.BlockSpec(memory_space=pl.ANY)
    piece = jax.ShapeDtypeStruct((64, 2, 64, 128), jnp.bfloat16)
    return pl.pallas_call(
        functools.partial(attend_kernel, per_step=per_step, buckets=buckets),
        out_shape=(piece, piece, piece, piece, piece, jax.ShapeDtypeStruct((8, 128), jnp.float32)),
        in_specs=[smem] * 4 + [hbm] * 4 + [vmem] * 2,
        out_specs=(vmem,) * 6,
        scratch_shapes=[
            pltpu.VMEM((128, 128, 128), jnp.bfloat16),
            pltpu.VMEM((128, 128, 128), jnp.bfloat16),
            pltpu.VMEM((128, 128, 128), jnp.float32),
            pltpu.VMEM((128, 128, 128), jnp.float32),
            pltpu.SemaphoreType.DMA((8,)),
        ],
        compiler_params=pltpu.CompilerParams(vmem_limit_bytes=56 * 1024 * 1024),
    )(order, counts, lists, bounds, kv0, kv1, kv2, kv3, qg, gains)


def sorted_tables(counts, lists, per_step, buckets):
    index = jnp.arange(64, dtype=jnp.int32)
    ahead = (counts[None, :] > counts[:, None]) | ((counts[None, :] == counts[:, None]) & (index[None, :] < index[:, None]))
    rank = jnp.sum(ahead.astype(jnp.int32), axis=1)
    place = (rank[None, :] == index[:, None]).astype(jnp.int32)
    order = jnp.sum(place * index[None, :], axis=1)
    sorted_counts = jnp.sum(place * counts[None, :], axis=1)
    sorted_lists = jnp.sum(place[:, :, None] * lists[None, :, :], axis=1)
    bounds = [(jnp.sum((counts > b).astype(jnp.int32)) + per_step - 1) // per_step for b in buckets[1:]]
    bounds = jnp.stack(bounds + [jnp.int32(64 // per_step)])
    return order, sorted_counts, sorted_lists.reshape(-1), bounds


HEADS = 16
MOST = 8
PER_STEP = 2
BUCKETS = (8, 6, 4, 2)


def to_send(rows):
    return jnp.transpose(rows.reshape(4, 64, HEADS, HEAD_DIM), (2, 0, 1, 3)).reshape(64, 64, HEAD_DIM)


def from_back(pieces):
    return jnp.transpose(pieces.reshape(HEADS, 4, 64, HEAD_DIM), (1, 2, 0, 3)).reshape(1, 256, HEADS * HEAD_DIM)


def exchange(array):
    return lax.all_to_all(array, "seq", split_axis=0, concat_axis=0, tiled=True)


def across(array, flip):
    return lax.ppermute(array, "seq", [(i, i ^ flip) for i in range(64)])


def body(query_rows, key_rows, value_rows, output_grad, query_gain, key_gain, block_list, block_count):
    position = lax.axis_index("seq")
    head = position // 4
    chip = position // 2 % 2
    lists = lax.dynamic_slice_in_dim(block_list[0], head, 1, 0).reshape(64, 2, MOST)
    counts = lax.dynamic_slice_in_dim(block_count[0], head, 1, 0).reshape(64, 2)
    lists = jnp.where(chip == 0, lists[:, 0], lists[:, 1])
    counts = jnp.where(chip == 0, counts[:, 0], counts[:, 1])
    lists = (lists % 2 ^ chip) * 64 + lists // 2
    order, counts, lists, bounds = sorted_tables(counts, lists, PER_STEP, BUCKETS)
    gain_query = lax.dynamic_slice_in_dim(query_gain, head, 1, 0)
    gain_key = lax.dynamic_slice_in_dim(key_gain, head, 1, 0)
    gains = jnp.concatenate([gain_query, gain_key], axis=0)

    with jax.named_scope("gather"):
        kv_own = exchange(jnp.stack([to_send(key_rows[0]), to_send(value_rows[0])], axis=1))
        query_rows, output_grad, kv_own = lax.optimization_barrier((query_rows, output_grad, kv_own))
        kv_chip = across(kv_own, 2)
        query_grad_pair = exchange(jnp.stack([to_send(query_rows[0]), to_send(output_grad[0])], axis=1))
        kv_core = across(kv_own, 1)
        kv_far = across(kv_chip, 1)
    with jax.named_scope("attend"):
        outs = attend(order, counts, lists, bounds, kv_own, kv_chip, kv_core, kv_far, query_grad_pair, gains, PER_STEP, BUCKETS)
    front, part_own, part_chip, part_core, part_far, query_gain_rows = outs
    with jax.named_scope("return"):
        far = part_chip.astype(jnp.float32) + across(part_far, 1).astype(jnp.float32)
        far = across(far.astype(jnp.bfloat16), 2)
        front_back = exchange(front)
        near = part_own.astype(jnp.float32) + across(part_core, 1).astype(jnp.float32)
        total = near + far.astype(jnp.float32)
        key_total, value_total = total[:, 0], total[:, 1]
        wide = kv_own[:, 0].astype(jnp.float32)
        scale = lax.rsqrt(jnp.mean(wide * wide, axis=-1, keepdims=True) + EPS)
        weighted = key_total * gain_key
        inner = jnp.mean(weighted * wide, axis=-1, keepdims=True)
        key_grad = scale * weighted - wide * (scale * scale * scale) * inner
        key_gain_row = jnp.sum(key_total * (wide * scale), axis=(0, 1))
        back = exchange(jnp.stack([key_grad, value_total], axis=1).astype(jnp.bfloat16))
    with jax.named_scope("gains"):
        mine = jnp.stack([query_gain_rows[0], key_gain_row])
        for flip in (1, 2):
            mine = mine + lax.ppermute(mine, "dp", [(i, i ^ flip) for i in range(4)])
        for flip in (1, 2):
            mine = mine + across(mine, flip)
        gathered = mine[None]
        for step, flip in enumerate((4, 8, 16, 32)):
            other = across(gathered, flip)
            low = (position // flip) % 2 == 0
            gathered = jnp.where(low, jnp.concatenate([gathered, other]), jnp.concatenate([other, gathered]))
    return (
        from_back(front_back[:, 0]),
        from_back(front_back[:, 1]),
        from_back(back[:, 0]),
        from_back(back[:, 1]),
        gathered[:, 0],
        gathered[:, 1],
    )


def solution(mesh):
    rows = P("dp", "seq", None)
    return jax.shard_map(
        body,
        mesh=mesh,
        in_specs=(rows, rows, rows, rows, P(), P(), P("dp", None, None, None), P("dp", None, None)),
        out_specs=(rows, rows, rows, rows, P(), P()),
        check_vma=False,
    )
```

time: 1070 us -> 383 us (0.36)
  waiting for transfers between devices: 425 us -> 164 us
  other arithmetic: 272 us -> 16 us
  matrix products: 112 us -> 0 us
  local copies, waits for them, and re-layouts: 91.8 us -> 17.7 us
  Pallas kernels: 0 us -> 70.2 us
  blocking collectives: 109 us -> 63.2 us
    all_to_all x7 -> x3, waiting for transfers between devices: 425 us -> 0.01 us  [exchange(): return lax.all_to_all(array, 'seq', split_axis=0, concat_axis=0, tiled=True)]
    scatter-add x24 -> x0, other arithmetic: 216 us -> none  [add_blocks(): one_table.at[one_list].add(one_update)]
    ppermute x0 -> x14, waiting for transfers between devices: none -> 164 us  [the longest x12 156 us: across(): return lax.ppermute(array, 'seq', [(i, i ^ flip) for i in range(64)])]
    dot_general x42 -> x0, matrix products: 93.9 us -> none  [the longest x8 29.5 us: attend(): jnp.einsum('ghqk,gqhe->ghke', weights, grad_block, preferred_element_type...]
    psum x1 -> x0, blocking collectives: 74.1 us -> none  [body(): lax.psum((query_gain_full, key_gain_full), ('dp', 'seq'))]
    pallas_call x0 -> x1, Pallas kernels: none -> 70.2 us  [attend(): pl.pallas_call(functools.partial(attend_kernel, per_step=per_step, bucket...]
    gather x16 -> x0, local copies, waits for them, and re-layouts: 50.2 us -> none  [pick_blocks(): one_table[one_list]]
    convert_element_type x12 -> x2, other arithmetic: 33.9 us -> 3.32 us  [the longest x1 3.31 us: body(): far = across(far.astype(jnp.bfloat16), 2)]
  transfers between devices with their start and end apart: 7 -> 17, of which waited for: 7 -> 9; matrix products, arithmetic and copies ran while one was open for 4% -> 6% of each run, Pallas kernels for 0% -> 0%
where the time goes in v1:
time: 383 us
  waiting for transfers between devices  164 us (43%)
  Pallas kernels  70.2 us (18%)
  blocking collectives  63.2 us (17%)
  starting transfers between devices  48.8 us (13%)
  local copies, waits for them, and re-layouts  17.7 us (5%)
  other arithmetic  16 us (4%)
    ppermute x12, waiting for transfers between devices, across(): return lax.ppermute(array, 'seq', [(i, i ^ flip) for i in range(64)])  156 us
    pallas_call x1, Pallas kernels, attend(): pl.pallas_call(functools.partial(attend_kernel, per_step=per_step, bucket...  70.2 us
    all_to_all x1, blocking collectives, exchange(): return lax.all_to_all(array, 'seq', split_axis=0, concat_axis=0, tiled=True)  63.2 us
    all_to_all x3, starting transfers between devices, exchange(): return lax.all_to_all(array, 'seq', split_axis=0, concat_axis=0, tiled=True)  32.6 us
    ppermute x12, starting transfers between devices, across(): return lax.ppermute(array, 'seq', [(i, i ^ flip) for i in range(64)])  15.5 us
    ppermute x2, waiting for transfers between devices, body(): mine = mine + lax.ppermute(mine, 'dp', [(i, i ^ flip) for i in range(4)])  7.98 us
  transfers between devices with their start and end apart: 17, of which 9 were waited for; matrix products, arithmetic and copies ran while one was open for 6% of the time, Pallas kernels for 0%

profile of v1, /device:TPU:16, one launch (start us, length us, event | category | flops | bytes accessed | tf_op | source)
XLA Modules:
  0.0 382.9 jit_solution(12190872457817394220)
XLA Ops:
  0.7 1.5 copy.51
  2.2 0.3 copy.43
  2.5 0.2 copy.52
  2.7 0.3 copy.44
  3.0 0.2 pad_maximum_fusion
  3.2 63.2 %all_to_all.20.kv0 = bf16[64,2,64,128]{3,2,1,0:T(8,128)(2,1)S(1)} all-to-all(bf16[64,2,64,128]{3,2,1,0:T(8,128)(2,1)S(1)} %pad_maximum_fusion), channel_id=1, replica_groups=mesh['dp'=4,'seq'=64] {'seq'}, dimensions={0} | all-to-all | bytes 4194304 | tf_op jit(solution)/shard_map/gather/all_to_all | solution.py:160
  66.5 1.5 collective-permute-start
  67.9 0.2 copy.53
  68.2 0.3 copy.45
  68.4 0.7 copy-done.7
  69.2 0.2 copy.54
  69.4 0.3 copy.46
  69.7 1.5 pad_maximum_fusion.1
  71.2 5.6 %all-to-all-start.1 = ((bf16[64,2,64,128]{3,2,1,0:T(8,128)(2,1)}), bf16[64,2,64,128]{3,2,1,0:T(8,128)(2,1)}, u32[]{:S(2)}, u32[]{:S(2)}) async-start(bf16[64,2,64,128]{3,2,1,0:T(8,128)(2,1)} %pad_maximum_fusion.1), calls=%async_computation.1 | async-start | bytes 4194304 | tf_op jit(solution)/shard_map/gather/all_to_all | solution.py:160
  76.8 56.7 %collective-permute-done.kv1 = bf16[64,2,64,128]{3,2,1,0:T(8,128)(2,1)} collective-permute-done((bf16[64,2,64,128]{3,2,1,0:T(8,128)(2,1)S(1)}, bf16[64,2,64,128]{3,2,1,0:T(8,128)(2,1)}, u32[]{:S(2)}, u32[]{:S(2)}) %collective-permute-start) | collective-permute-done | bytes 2097184 | tf_op jit(solution)/shard_map/gather/ppermute | solution.py:164
  133.5 0.7 fusion.22
  134.4 0.2 fusion.10
  134.6 0.7 fusion.23
  137.5 0.2 convert_reduce_fusion
  137.7 1.2 multiply_reduce_fusion
  138.9 0.7 reshape.141.list_ref
  139.5 0.6 pad_add_fusion.bound_ref
  140.1 0.7 constant_dynamic-slice_fusion
  140.8 0.6 pad_maximum_fusion.3.gains_ref
  141.4 0.6 select_reduce_fusion
  142.0 70.2 %attend.1 = (bf16[64,2,64,128]{3,2,1,0:T(8,128)(2,1)}, bf16[64,2,64,128]{3,2,1,0:T(8,128)(2,1)}, bf16[64,2,64,128]{3,2,1,0:T(8,128)(2,1)}, bf16[64,2,64,128]{3,2...) custom-call(s32[64]{0:T(128)} %get-tuple-element.30.order_ref, s32[64]{0:T(128)} %get-tuple-element.29.count_ref, ...), custom_call_target="tpu_custom_call" | custom-call | tf_op jit(solution)/shard_map/attend/pallas_call | solution.py:116
  212.3 0.6 collective-permute-start.4
  212.9 16.8 %all-to-all-start.2 = ((bf16[64,2,64,128]{3,2,1,0:T(8,128)(2,1)}), bf16[64,2,64,128]{3,2,1,0:T(8,128)(2,1)S(1)}, u32[]{:S(2)}, u32[]{:S(2)}) async-start(bf16[64,2,64,128]{3,2,1,0:T(8,128)(2,1)} %get-tuple-element.18), calls=%async_computation.2 | async-start | bytes 4194304 | tf_op jit(solution)/shard_map/return/all_to_all | solution.py:160
  229.7 0.1 collective-permute-start.3
  229.8 3.3 add_convert_fusion
  233.2 1.8 collective-permute-start.5
  234.9 0.6 fusion.3
  235.6 63.9 %collective-permute-done.5 = bf16[64,2,64,128]{3,2,1,0:T(8,128)(2,1)S(1)} collective-permute-done((bf16[64,2,64,128]{3,2,1,0:T(8,128)(2,1)S(1)}, bf16[64,2,64,128]{3,2,1,0:T(8,128)(2,1)S(1)}, u32[]{:S(2)}, u32[]{:S(2)}) %collective-permute-start.5) | collective-permute-done | bytes 2097184 | tf_op jit(solution)/shard_map/return/ppermute | solution.py:164
  299.5 1.5 convert_add_fusion
  301.0 0.2 slice.83
  301.2 1.3 fusion.6
  302.6 1.9 fusion.9
  304.5 1.5 pad_maximum_fusion.2
  306.1 10.2 %all-to-all-start.3 = ((bf16[64,2,64,128]{3,2,1,0:T(8,128)(2,1)}), bf16[64,2,64,128]{3,2,1,0:T(8,128)(2,1)}, u32[]{:S(2)}, u32[]{:S(2)}) async-start(bf16[64,2,64,128]{3,2,1,0:T(8,128)(2,1)} %pad_maximum_fusion.2), calls=%async_computation.3 | async-start | bytes 4194304 | tf_op jit(solution)/shard_map/return/all_to_all | solution.py:160
  316.2 0.7 slice.54
  316.9 0.6 collective-permute-start.6
  317.6 2.9 collective-permute-done.6
  320.6 5.1 %collective-permute-done.7 = f32[2,128]{1,0:T(2,128)S(1)} collective-permute-done((f32[2,128]{1,0:T(2,128)S(1)}, f32[2,128]{1,0:T(2,128)S(1)}, u32[]{:S(2)}, u32[]{:S(2)}) %collective-permute-start.7) | collective-permute-done | bytes 1056 | tf_op jit(solution)/shard_map/gains/ppermute | solution.py:208
  325.8 1.1 collective-permute-done.8
  326.9 1.5 collective-permute-start.9
  328.4 2.1 collective-permute-done.9
  330.5 3.0 collective-permute-start.10
  333.5 2.1 collective-permute-done.10
  335.6 1.5 collective-permute-start.11
  337.1 26.3 %collective-permute-done.11 = f32[2,2,128]{2,1,0:T(2,128)S(1)} collective-permute-done((f32[2,2,128]{2,1,0:T(2,128)S(1)}, f32[2,2,128]{2,1,0:T(2,128)S(1)}, u32[]{:S(2)}, u32[]{:S(2)}) %collective-permute-start.11) | collective-permute-done | bytes 2080 | tf_op jit(solution)/shard_map/gains/ppermute | solution.py:164
  363.4 0.7 collective-permute-start.12
  364.0 3.8 %collective-permute-done.12 = f32[4,2,128]{2,1,0:T(2,128)S(1)} collective-permute-done((f32[4,2,128]{2,1,0:T(2,128)S(1)}, f32[4,2,128]{2,1,0:T(2,128)S(1)}, u32[]{:S(2)}, u32[]{:S(2)}) %collective-permute-start.12) | collective-permute-done | bytes 4128 | tf_op jit(solution)/shard_map/gains/ppermute | solution.py:164
  367.9 4.6 %collective-permute-start.13 = (f32[8,2,128]{2,1,0:T(2,128)S(1)}, f32[8,2,128]{2,1,0:T(2,128)S(1)}, u32[]{:S(2)}, u32[]{:S(2)}) collective-permute-start(f32[8,2,128]{2,1,0:T(2,128)S(1)} %maximum_select_fusion.1), channel_id=1, source_target_pairs={{0,32},{1,33},{2,34},{3,35},{4,36},{5,37},{6,38},{7,39},{8,40},{9,... | collective-permute-start | bytes 24584 | tf_op jit(solution)/shard_map/gains/ppermute | solution.py:164
  372.5 0.2 fusion.28
  372.7 0.7 copy.47
  373.4 1.3 reshape.146
  374.6 0.7 copy.48
  375.3 1.3 reshape.147
  376.6 0.6 fusion.29
  377.2 1.7 fusion.27
  379.0 0.7 copy.49
  379.6 1.3 reshape.148
  380.9 0.7 copy.50
  381.6 1.3 reshape.149
  (45 shorter events, 0.8 us)
Async XLA Ops:
  0.6 136.6 %copy-start = (s32[1,16,128,8]{2,3,1,0:T(8,128)S(1)}, s32[1,16,128,8]{2,3,1,0:T(8,128)}, u32[]{:S(2)}) copy-start(s32[1,16,128,8]{2,3,1,0:T(8,128)} %param.14) | copy-start | bytes 196612
  0.6 1.8 copy-start.5
  3.2 64.7 %copy-start.6 = (bf16[1,256,2048]{2,1,0:T(8,128)(2,1)S(1)}, bf16[1,256,2048]{2,1,0:T(8,128)(2,1)}, u32[]{:S(2)}) copy-start(bf16[1,256,2048]{2,1,0:T(8,128)(2,1)} %param.8) | copy-start | bytes 3145732
  66.5 10.3 %copy-start.2 = (bf16[64,2,64,128]{3,2,1,0:T(8,128)(2,1)}, bf16[64,2,64,128]{3,2,1,0:T(8,128)(2,1)S(1)}, u32[]{:S(2)}) copy-start(bf16[64,2,64,128]{3,2,1,0:T(8,128)(2,1)S(1)} %all_to_all.20.kv0) | copy-start | bytes 6291460
  66.5 67.1 %collective-permute-start = (bf16[64,2,64,128]{3,2,1,0:T(8,128)(2,1)S(1)}, bf16[64,2,64,128]{3,2,1,0:T(8,128)(2,1)}, u32[]{:S(2)}, u32[]{:S(2)}) collective-permute-start(bf16[64,2,64,128]{3,2,1,0:T(8,128)(2,1)S(1)} %all_to_all.20.kv0), channel_id=1, source_target_pairs={{0,2},{1,3},{2,0},{3,1},{4,6},{5,7},{6,4},{7,5},{8,10},{9,11},{10,... | collective-permute-start | bytes 6291464 | tf_op jit(solution)/shard_map/gather/ppermute | solution.py:164
  67.9 1.2 copy-start.7
  71.2 70.9 %all-to-all-start.1 = ((bf16[64,2,64,128]{3,2,1,0:T(8,128)(2,1)}), bf16[64,2,64,128]{3,2,1,0:T(8,128)(2,1)}, u32[]{:S(2)}, u32[]{:S(2)}) async-start(bf16[64,2,64,128]{3,2,1,0:T(8,128)(2,1)} %pad_maximum_fusion.1), calls=%async_computation.1 | async-start | bytes 4194304 | tf_op jit(solution)/shard_map/gather/all_to_all | solution.py:160
  76.7 65.3 %collective-permute-start.1 = (bf16[64,2,64,128]{3,2,1,0:T(8,128)(2,1)S(1)}, bf16[64,2,64,128]{3,2,1,0:T(8,128)(2,1)}, u32[]{:S(2)}, u32[]{:S(2)}) collective-permute-start(bf16[64,2,64,128]{3,2,1,0:T(8,128)(2,1)S(1)} %all_to_all.20.kv0), channel_id=1, source_target_pairs={{0,1},{1,0},{2,3},{3,2},{4,5},{5,4},{6,7},{7,6},{8,9},{9,8},{10,11... | collective-permute-start | bytes 6291464 | tf_op jit(solution)/shard_map/gather/ppermute | solution.py:164
  133.5 8.5 %collective-permute-start.2 = (bf16[64,2,64,128]{3,2,1,0:T(8,128)(2,1)}, bf16[64,2,64,128]{3,2,1,0:T(8,128)(2,1)}, u32[]{:S(2)}, u32[]{:S(2)}) collective-permute-start(bf16[64,2,64,128]{3,2,1,0:T(8,128)(2,1)} %collective-permute-done.kv1), channel_id=1, source_target_pairs={{0,1},{1,0},{2,3},{3,2},{4,5},{5,4},{6,7},{7,6},{8,9},{9,8},{10,11... | collective-permute-start | bytes 6291464 | tf_op jit(solution)/shard_map/gather/ppermute | solution.py:164
  212.3 17.6 %collective-permute-start.4 = (bf16[64,2,64,128]{3,2,1,0:T(8,128)(2,1)}, bf16[64,2,64,128]{3,2,1,0:T(8,128)(2,1)}, u32[]{:S(2)}, u32[]{:S(2)}) collective-permute-start(bf16[64,2,64,128]{3,2,1,0:T(8,128)(2,1)} %get-tuple-element.22), channel_id=1, source_target_pairs={{0,1},{1,0},{2,3},{3,2},{4,5},{5,4},{6,7},{7,6},{8,9},{9,8},{10,11... | collective-permute-start | bytes 6291464 | tf_op jit(solution)/shard_map/return/ppermute | solution.py:164
  212.9 93.2 %all-to-all-start.2 = ((bf16[64,2,64,128]{3,2,1,0:T(8,128)(2,1)}), bf16[64,2,64,128]{3,2,1,0:T(8,128)(2,1)S(1)}, u32[]{:S(2)}, u32[]{:S(2)}) async-start(bf16[64,2,64,128]{3,2,1,0:T(8,128)(2,1)} %get-tuple-element.18), calls=%async_computation.2 | async-start | bytes 4194304 | tf_op jit(solution)/shard_map/return/all_to_all | solution.py:160
  229.7 5.9 %collective-permute-start.3 = (bf16[64,2,64,128]{3,2,1,0:T(8,128)(2,1)}, bf16[64,2,64,128]{3,2,1,0:T(8,128)(2,1)S(1)}, u32[]{:S(2)}, u32[]{:S(2)}) collective-permute-start(bf16[64,2,64,128]{3,2,1,0:T(8,128)(2,1)} %get-tuple-element.20), channel_id=1, source_target_pairs={{0,1},{1,0},{2,3},{3,2},{4,5},{5,4},{6,7},{7,6},{8,9},{9,8},{10,11... | collective-permute-start | bytes 6291464 | tf_op jit(solution)/shard_map/return/ppermute | solution.py:164
  229.8 5.1 %copy-start.3 = (bf16[64,2,64,128]{3,2,1,0:T(8,128)(2,1)S(1)}, bf16[64,2,64,128]{3,2,1,0:T(8,128)(2,1)}, u32[]{:S(2)}) copy-start(bf16[64,2,64,128]{3,2,1,0:T(8,128)(2,1)} %copy-done.2) | copy-start | bytes 6291460
  229.8 69.7 %copy-start.4 = (bf16[64,2,64,128]{3,2,1,0:T(8,128)(2,1)S(1)}, bf16[64,2,64,128]{3,2,1,0:T(8,128)(2,1)}, u32[]{:S(2)}) copy-start(bf16[64,2,64,128]{3,2,1,0:T(8,128)(2,1)} %get-tuple-element.19) | copy-start | bytes 6291460
  233.2 66.4 %collective-permute-start.5 = (bf16[64,2,64,128]{3,2,1,0:T(8,128)(2,1)S(1)}, bf16[64,2,64,128]{3,2,1,0:T(8,128)(2,1)S(1)}, u32[]{:S(2)}, u32[]{:S(2)}) collective-permute-start(bf16[64,2,64,128]{3,2,1,0:T(8,128)(2,1)S(1)} %add_convert_fusion), channel_id=1, source_target_pairs={{0,2},{1,3},{2,0},{3,1},{4,6},{5,7},{6,4},{7,5},{8,10},{9,11},{10,... | collective-permute-start | bytes 6291464 | tf_op jit(solution)/shard_map/return/ppermute | solution.py:164
  306.1 71.2 %all-to-all-start.3 = ((bf16[64,2,64,128]{3,2,1,0:T(8,128)(2,1)}), bf16[64,2,64,128]{3,2,1,0:T(8,128)(2,1)}, u32[]{:S(2)}, u32[]{:S(2)}) async-start(bf16[64,2,64,128]{3,2,1,0:T(8,128)(2,1)} %pad_maximum_fusion.2), calls=%async_computation.3 | async-start | bytes 4194304 | tf_op jit(solution)/shard_map/return/all_to_all | solution.py:160
  316.9 3.6 collective-permute-start.6
  320.5 5.2 %collective-permute-start.7 = (f32[2,128]{1,0:T(2,128)S(1)}, f32[2,128]{1,0:T(2,128)S(1)}, u32[]{:S(2)}, u32[]{:S(2)}) collective-permute-start(f32[2,128]{1,0:T(2,128)S(1)} %fusion.26), channel_id=1, source_target_pairs={{0,128},{64,192},{128,0},{192,64},{1,129},{65,193},{129,1},{193,65... | collective-permute-start | bytes 3080 | tf_op jit(solution)/shard_map/gains/ppermute | solution.py:208
  325.7 1.2 collective-permute-start.8
  326.9 3.6 collective-permute-start.9
  330.5 5.1 %collective-permute-start.10 = (f32[1,2,128]{2,1,0:T(2,128)S(1)}, f32[1,2,128]{2,1,0:T(2,128)S(1)}, u32[]{:S(2)}, u32[]{:S(2)}) collective-permute-start(f32[1,2,128]{2,1,0:T(2,128)S(1)} %add_bitcast_fusion), channel_id=1, source_target_pairs={{0,4},{1,5},{2,6},{3,7},{4,0},{5,1},{6,2},{7,3},{8,12},{9,13},{10,... | collective-permute-start | bytes 3080 | tf_op jit(solution)/shard_map/gains/ppermute | solution.py:164
  335.6 27.8 %collective-permute-start.11 = (f32[2,2,128]{2,1,0:T(2,128)S(1)}, f32[2,2,128]{2,1,0:T(2,128)S(1)}, u32[]{:S(2)}, u32[]{:S(2)}) collective-permute-start(f32[2,2,128]{2,1,0:T(2,128)S(1)} %maximum_select_fusion.3), channel_id=1, source_target_pairs={{0,8},{1,9},{2,10},{3,11},{4,12},{5,13},{6,14},{7,15},{8,0},{9,1},... | collective-permute-start | bytes 6152 | tf_op jit(solution)/shard_map/gains/ppermute | solution.py:164
  363.4 4.5 %collective-permute-start.12 = (f32[4,2,128]{2,1,0:T(2,128)S(1)}, f32[4,2,128]{2,1,0:T(2,128)S(1)}, u32[]{:S(2)}, u32[]{:S(2)}) collective-permute-start(f32[4,2,128]{2,1,0:T(2,128)S(1)} %maximum_select_fusion.2), channel_id=1, source_target_pairs={{0,16},{1,17},{2,18},{3,19},{4,20},{5,21},{6,22},{7,23},{8,24},{9,... | collective-permute-start | bytes 12296 | tf_op jit(solution)/shard_map/gains/ppermute | solution.py:164
  367.9 8.7 %collective-permute-start.13 = (f32[8,2,128]{2,1,0:T(2,128)S(1)}, f32[8,2,128]{2,1,0:T(2,128)S(1)}, u32[]{:S(2)}, u32[]{:S(2)}) collective-permute-start(f32[8,2,128]{2,1,0:T(2,128)S(1)} %maximum_select_fusion.1), channel_id=1, source_target_pairs={{0,32},{1,33},{2,34},{3,35},{4,36},{5,37},{6,38},{7,39},{8,40},{9,... | collective-permute-start | bytes 24584 | tf_op jit(solution)/shard_map/gains/ppermute | solution.py:164
  380.9 2.0 copy-start.1

commit v2 on v1

v2 whole, which is shorter than its diff:
```python
import functools
import math

import jax
import jax.numpy as jnp
from jax import lax
from jax.experimental import pallas as pl
from jax.experimental.pallas import tpu as pltpu
from jax.sharding import PartitionSpec as P

HEAD_DIM = 128
EPS = 1e-06
INV_ROOT = 1.0 / math.sqrt(HEAD_DIM)
LOG2E = math.log2(math.e)
NT = (((1,), (1,)), ((), ()))
TN = (((0,), (0,)), ((), ()))
NN = (((1,), (0,)), ((), ()))
GROUPS = 32
BUCKETS = (8, 6, 4, 2)
TOGETHER = 1


def dot(a, b, dims):
    return lax.dot_general(a, b, dims, preferred_element_type=jnp.float32)


def attend_kernel(info_ref, count_ref, list_ref, k0, k1, k2, k3, v0, v1, v2, v3, qg_hbm, gains_ref,
                  og_hbm, p0, p1, p2, p3, gain_ref,
                  ktab, vtab, acc, qg_ref, og_ref, stage, order_ref, in_sems, out_sems):
    mine = info_ref[0]
    chip = info_ref[1]
    copies = [pltpu.make_async_copy(qg_hbm, qg_ref, in_sems.at[8])]
    for j, (pieces, table) in enumerate((((k0, k1, k2, k3), ktab), ((v0, v1, v2, v3), vtab))):
        for i, piece in enumerate(pieces):
            to = table.at[pl.ds((i % 2) * 64, 64), pl.ds((i // 2) * 64, 64)]
            copies.append(pltpu.make_async_copy(piece, to, in_sems.at[4 * j + i]))
    for copy in copies:
        copy.start()

    stops = []
    stop = 0
    for which, most in enumerate(BUCKETS):
        below = BUCKETS[which + 1] if which + 1 < len(BUCKETS) else 0

        def place(g, at, most=most, below=below):
            count = count_ref[4 * g + mine]
            inside = jnp.logical_and(count <= most, count > below)

            @pl.when(inside)
            def _():
                order_ref[at] = g

            return at + inside.astype(jnp.int32)

        stop = lax.fori_loop(0, GROUPS, place, jnp.int32(stop))
        stops.append(stop)

    @pl.loop(0, 128)
    def _(t):
        acc[t] = jnp.zeros((128, 256), jnp.float32)

    gain_query = gains_ref[0:1, :]
    gain_ref[...] = jnp.zeros_like(gain_ref)
    for copy in copies:
        copy.wait()

    zero = jnp.zeros((128, 128), jnp.bfloat16)

    def forward(i, most, first):
        g = order_ref[i]
        live = count_ref[4 * g + mine]
        listed = [list_ref[(4 * g + mine) * 8 + j] for j in range(most)]
        spots = [((c & 1) ^ chip) * 64 + (c >> 1) for c in listed]
        wide = jnp.concatenate([qg_ref[2 * g, 0], qg_ref[2 * g + 1, 0]], axis=0).astype(jnp.float32)
        grad = jnp.concatenate([qg_ref[2 * g, 1], qg_ref[2 * g + 1, 1]], axis=0)
        scale = lax.rsqrt(jnp.mean(wide * wide, axis=-1, keepdims=True) + EPS)
        hat = wide * scale
        normed = (hat * gain_query).astype(jnp.bfloat16)
        keys = jnp.concatenate([ktab[t] for t in spots], axis=0)
        values = jnp.concatenate([vtab[t] for t in spots], axis=0)
        flat = dot(normed, keys, NT)
        scores = []
        for j in range(most):
            s = flat[:, j * 128:(j + 1) * 128]
            if j == most - 1 or (j and not first):
                s = jnp.where(j < live, s, -jnp.inf)
            scores.append(s)
        top = jnp.max(functools.reduce(jnp.maximum, scores), axis=-1, keepdims=True)
        exps = [jnp.exp2((s - top) * (INV_ROOT * LOG2E)) for s in scores]
        total = jnp.sum(functools.reduce(jnp.add, exps), axis=-1, keepdims=True)
        inverse = 1.0 / total
        weights = [(e * inverse).astype(jnp.bfloat16) for e in exps]
        attended = dot(jnp.concatenate(weights, axis=1), values, NN).astype(jnp.bfloat16)
        og_ref[2 * g, 0] = attended[:64]
        og_ref[2 * g + 1, 0] = attended[64:]
        inner = jnp.sum(grad.astype(jnp.float32) * attended.astype(jnp.float32), axis=-1, keepdims=True)
        return g, spots, wide, grad, scale, hat, normed, keys, values, weights, inner

    def backward(state, most):
        g, spots, wide, grad, scale, hat, normed, keys, values, weights, inner = state
        flat = dot(grad, values, NT)
        score_grads = []
        for j in range(most):
            wg = flat[:, j * 128:(j + 1) * 128]
            score_grads.append((weights[j].astype(jnp.float32) * (wg - inner)).astype(jnp.bfloat16))
        norm_grad = dot(jnp.concatenate(score_grads, axis=1), keys, NN) * INV_ROOT
        pair = jnp.concatenate(
            [jnp.concatenate([normed, zero], axis=1), jnp.concatenate([zero, grad], axis=1)], axis=0
        )
        for j in range(most):
            acc[spots[j]] += dot(jnp.concatenate([score_grads[j], weights[j]], axis=0), pair, TN)
        gain_ref[0:1, :] += jnp.sum(norm_grad * hat, axis=0, keepdims=True)
        weighted = norm_grad * gain_query
        mean = jnp.mean(weighted * wide, axis=-1, keepdims=True)
        query_grad = (scale * weighted - wide * (scale * scale * scale) * mean).astype(jnp.bfloat16)
        og_ref[2 * g, 1] = query_grad[:64]
        og_ref[2 * g + 1, 1] = query_grad[64:]

    start = 0
    for which, most in enumerate(BUCKETS):
        stop = (stops[which] + TOGETHER - 1) // TOGETHER

        @pl.loop(start, stop)
        def _(step, most=most):
            states = [forward(step * TOGETHER + u, most, u == 0) for u in range(TOGETHER)]
            for state in states:
                backward(state, most)

        start = stop

    back = [pltpu.make_async_copy(og_ref, og_hbm, out_sems.at[16])]
    back[0].start()
    outs = (p0, p1, p2, p3)
    for part in range(4):

        @pl.loop(part * 16, part * 16 + 16)
        def _(s):
            for x in range(2):
                both = acc[x * 64 + s]
                k = (both[:, :128] * INV_ROOT).astype(jnp.bfloat16)
                v = both[:, 128:].astype(jnp.bfloat16)
                for c in range(2):
                    stage[2 * c + x, s, 0] = k[c * 64:(c + 1) * 64]
                    stage[2 * c + x, s, 1] = v[c * 64:(c + 1) * 64]

        for i, out in enumerate(outs):
            rows = pl.ds(part * 16, 16)
            back.append(pltpu.make_async_copy(stage.at[i, rows], out.at[rows], out_sems.at[part * 4 + i]))
            back[-1].start()
    for copy in back:
        copy.wait()


def attend(info, counts, lists, keys, values, qg, gains):
    smem = pl.BlockSpec(memory_space=pltpu.SMEM)
    vmem = pl.BlockSpec(memory_space=pltpu.VMEM)
    hbm = pl.BlockSpec(memory_space=pl.ANY)
    piece = jax.ShapeDtypeStruct((64, 2, 64, 128), jnp.bfloat16)
    return pl.pallas_call(
        attend_kernel,
        out_shape=(piece, piece, piece, piece, piece, jax.ShapeDtypeStruct((8, 128), jnp.float32)),
        in_specs=[smem] * 3 + [hbm] * 9 + [vmem],
        out_specs=(hbm,) * 5 + (vmem,),
        scratch_shapes=[
            pltpu.VMEM((128, 128, 128), jnp.bfloat16),
            pltpu.VMEM((128, 128, 128), jnp.bfloat16),
            pltpu.VMEM((128, 128, 256), jnp.float32),
            pltpu.VMEM((64, 2, 64, 128), jnp.bfloat16),
            pltpu.VMEM((64, 2, 64, 128), jnp.bfloat16),
            pltpu.VMEM((4, 64, 2, 64, 128), jnp.bfloat16),
            pltpu.SMEM((GROUPS,), jnp.int32),
            pltpu.SemaphoreType.DMA((9,)),
            pltpu.SemaphoreType.DMA((17,)),
        ],
        compiler_params=pltpu.CompilerParams(vmem_limit_bytes=56 * 1024 * 1024),
        cost_estimate=pl.CostEstimate(flops=6 * 10**9, bytes_accessed=20 * 2**20, transcendentals=4 * 2**20),
        name="attend",
    )(info, counts, lists, *keys, *values, qg, gains)


HEADS = 16


def finish_kernel(own_ref, core_ref, far_ref, kv_ref, gain_ref, out_ref, row_ref):
    @pl.when(pl.program_id(0) == 0)
    def _():
        row_ref[...] = jnp.zeros_like(row_ref)

    gain = gain_ref[0:1, :]

    @pl.loop(0, own_ref.shape[0], unroll=2)
    def _(s):
        total = own_ref[s].astype(jnp.float32) + core_ref[s].astype(jnp.float32) + far_ref[s].astype(jnp.float32)
        out_ref[s, 1] = total[1].astype(jnp.bfloat16)
        total = total[0]
        wide = kv_ref[s, 0].astype(jnp.float32)
        scale = lax.rsqrt(jnp.mean(wide * wide, axis=-1, keepdims=True) + EPS)
        weighted = total * gain
        inner = jnp.mean(weighted * wide, axis=-1, keepdims=True)
        out_ref[s, 0] = (scale * weighted - wide * (scale * scale * scale) * inner).astype(jnp.bfloat16)
        row_ref[0:1, :] += jnp.sum(total * (wide * scale), axis=0, keepdims=True)


def finish(own, core, far, kv, gain):
    block = pl.BlockSpec((8, 2, 64, 128), lambda i: (i, 0, 0, 0))
    first = pl.BlockSpec((8, 1, 64, 128), lambda i: (i, 0, 0, 0))
    whole = pl.BlockSpec((1, 128), lambda i: (0, 0))
    return pl.pallas_call(
        finish_kernel,
        grid=(8,),
        out_shape=(jax.ShapeDtypeStruct((64, 2, 64, 128), jnp.bfloat16), jax.ShapeDtypeStruct((8, 128), jnp.float32)),
        in_specs=[block, block, block, first, whole],
        out_specs=(block, pl.BlockSpec((8, 128), lambda i: (0, 0))),
        name="finish",
    )(own, core, far, kv, gain)


def unpack_kernel(in_ref, a_ref, b_ref):
    for i, out in enumerate((a_ref, b_ref)):
        for h in range(4):
            for r in range(4):
                out[r * 64:(r + 1) * 64, h * 128:(h + 1) * 128] = in_ref[h * 4 + r, i]


def unpack(pieces):
    rows = jax.ShapeDtypeStruct((256, HEADS * HEAD_DIM), jnp.bfloat16)
    return pl.pallas_call(
        unpack_kernel,
        grid=(4,),
        out_shape=(rows, rows),
        in_specs=[pl.BlockSpec((16, 2, 64, 128), lambda i: (i, 0, 0, 0))],
        out_specs=(pl.BlockSpec((256, 512), lambda i: (0, i)),) * 2,
        cost_estimate=pl.CostEstimate(flops=0, bytes_accessed=2**22, transcendentals=0),
        name="unpack",
    )(pieces)


def unpack_front_kernel(core_ref, in_ref, got_ref, a_ref, b_ref):
    core = core_ref[0]
    for i, out in enumerate((a_ref, b_ref)):
        for h in range(4):
            for block in range(2):
                near = pl.multiple_of(block * 128 + core * 64, 64)
                away = pl.multiple_of(block * 128 + (1 - core) * 64, 64)
                out[pl.ds(near, 64), h * 128:(h + 1) * 128] = in_ref[h * 4 + 2 * core + block, i]
                out[pl.ds(away, 64), h * 128:(h + 1) * 128] = got_ref[h, block, i]


def unpack_front(core, pieces, got):
    rows = jax.ShapeDtypeStruct((256, HEADS * HEAD_DIM), jnp.bfloat16)
    return pl.pallas_call(
        unpack_front_kernel,
        grid=(4,),
        out_shape=(rows, rows),
        in_specs=[
            pl.BlockSpec(memory_space=pltpu.SMEM),
            pl.BlockSpec((16, 2, 64, 128), lambda i: (i, 0, 0, 0)),
            pl.BlockSpec((4, 2, 2, 64, 128), lambda i: (i, 0, 0, 0, 0)),
        ],
        out_specs=(pl.BlockSpec((256, 512), lambda i: (0, i)),) * 2,
        cost_estimate=pl.CostEstimate(flops=0, bytes_accessed=2**22, transcendentals=0),
        name="unpack_front",
    )(core.reshape(1), pieces, got)


def to_send(rows):
    return jnp.transpose(rows.reshape(4, 64, HEADS, HEAD_DIM), (2, 0, 1, 3)).reshape(64, 64, HEAD_DIM)


def exchange(array):
    return lax.all_to_all(array, "seq", split_axis=0, concat_axis=0, tiled=True)


def across(array, flip):
    return lax.ppermute(array, "seq", [(i, i ^ flip) for i in range(64)])


def halves_swapped(rows, core):
    shaped = rows.reshape(2, 2, 64, HEADS * HEAD_DIM)
    kept = jnp.where(core == 0, shaped[:, 0], shaped[:, 1])
    given = jnp.where(core == 0, shaped[:, 1], shaped[:, 0])
    got = across(given, 1)
    return jnp.concatenate([jnp.where(core == 0, kept, got), jnp.where(core == 0, got, kept)])


def over_copies(row):
    for flip in (1, 2):
        row = row + lax.ppermute(row, "dp", [(i, i ^ flip) for i in range(4)])
    for flip in (1, 2):
        row = row + across(row, flip)
    return row


def body(query_rows, key_rows, value_rows, output_grad, query_gain, key_gain, block_list, block_count):
    position = lax.axis_index("seq")
    head = position // 4
    chip = position // 2 % 2
    core = position % 2
    lists = lax.dynamic_slice_in_dim(block_list[0], head, 1, 0).reshape(1024)
    counts = lax.dynamic_slice_in_dim(block_count[0], head, 1, 0).reshape(128)
    info = jnp.stack([position % 4, chip]).astype(jnp.int32)
    gain_query = lax.dynamic_slice_in_dim(query_gain, head, 1, 0)
    gain_key = lax.dynamic_slice_in_dim(key_gain, head, 1, 0)

    with jax.named_scope("gather"):
        kv_own = exchange(jnp.stack([to_send(key_rows[0]), to_send(value_rows[0])], axis=1))
        pair_send = jnp.stack(
            [to_send(halves_swapped(query_rows[0], core)), to_send(halves_swapped(output_grad[0], core))], axis=1
        )
        pair_send, kv_own, lists, counts, info = lax.optimization_barrier((pair_send, kv_own, lists, counts, info))
        value_own = kv_own[:, 1]
        value_chip = across(value_own, 2)
        wide = kv_own[:, 0].astype(jnp.float32)
        scale = lax.rsqrt(jnp.mean(wide * wide, axis=-1, keepdims=True) + EPS)
        key_own = (wide * scale * gain_key).astype(jnp.bfloat16)
        key_chip = across(key_own, 2)
        query_pair = exchange(pair_send)
        keys = (key_own, key_chip, across(key_own, 1), across(key_chip, 1))
        values = (value_own, value_chip, across(value_own, 1), across(value_chip, 1))
    with jax.named_scope("attend"):
        outs = attend(info, counts, lists, keys, values, query_pair, gain_query)
    front, part_own, part_chip, part_core, part_far, query_row = outs
    with jax.named_scope("return"):
        far = (part_chip.astype(jnp.float32) + across(part_far, 1).astype(jnp.float32)).astype(jnp.bfloat16)
        near = across(part_core, 1)
        front, far = lax.optimization_barrier((front, far))
        far = across(far, 2)
        front = exchange(front)
        given = front.reshape(HEADS, 2, 2, 2, 64, HEAD_DIM)
        got = across(jnp.where(core == 0, given[:, 1], given[:, 0]), 1)
        attended, query_grad = unpack_front(core, front, got)
        kv_grad, key_row = finish(part_own, near, far, kv_own, gain_key)
        key_grad, value_grad = unpack(exchange(kv_grad))
    with jax.named_scope("gains"):
        rows = jnp.concatenate([over_copies(query_row[0:1]), over_copies(key_row[0:1])])
        other = across(rows, 4)
        low = position // 4 % 2 == 0
        rows = jnp.where(low, jnp.stack([rows, other]), jnp.stack([other, rows]))
        turns = [rows] + [lax.ppermute(rows, "seq", [(i, (i + 8 * d) % 64) for i in range(64)]) for d in range(1, 8)]
        turns = jnp.stack(turns[::-1] + turns[::-1])
        turns = lax.dynamic_slice_in_dim(turns, 7 - position // 8, 8, 0).reshape(HEADS, 2, HEAD_DIM)
    return (attended[None], query_grad[None], key_grad[None], value_grad[None], turns[:, 0], turns[:, 1])


def solution(mesh):
    rows = P("dp", "seq", None)
    return jax.shard_map(
        body,
        mesh=mesh,
        in_specs=(rows, rows, rows, rows, P(), P(), P("dp", None, None, None), P("dp", None, None)),
        out_specs=(rows, rows, rows, rows, P(), P()),
        check_vma=False,
    )
```

time: 383 us -> 383 us (level)
  blocking collectives: 63.2 us -> 0 us
  waiting for transfers between devices: 164 us -> 219 us
  starting transfers between devices: 48.8 us -> 76.7 us
  Pallas kernels: 70.2 us -> 52.7 us
    all_to_all x1 -> x0, blocking collectives: 63.2 us -> none  [exchange(): return lax.all_to_all(array, 'seq', split_axis=0, concat_axis=0, tiled=True)]
    all_to_all x3 -> x4, waiting for transfers between devices: 0.01 us -> 40.2 us  [exchange(): return lax.all_to_all(array, 'seq', split_axis=0, concat_axis=0, tiled=True)]
    ppermute x2 -> x11, waiting for transfers between devices: 7.98 us -> 37.7 us  [the longest x7 35 us: body(): lax.ppermute(rows, 'seq', [(i, (i + 8 * d) % 64) for i in range(64)])]
    ppermute x2 -> x11, starting transfers between devices: 0.74 us -> 27 us  [the longest x7 16 us: body(): lax.ppermute(rows, 'seq', [(i, (i + 8 * d) % 64) for i in range(64)])]
    pallas_call x1 -> x4, Pallas kernels: 70.2 us -> 52.7 us  [the longest x1 36.3 us: attend(): pl.pallas_call(attend_kernel, out_shape=(piece, piece, piece, piece, piec...]
    ppermute x12 -> x17, waiting for transfers between devices: 156 us -> 141 us  [across(): return lax.ppermute(array, 'seq', [(i, i ^ flip) for i in range(64)])]
    all_to_all x3 -> x4, starting transfers between devices: 32.6 us -> 40.1 us  [exchange(): return lax.all_to_all(array, 'seq', split_axis=0, concat_axis=0, tiled=True)]
    ppermute x12 -> x17, starting transfers between devices: 15.5 us -> 9.51 us  [across(): return lax.ppermute(array, 'seq', [(i, i ^ flip) for i in range(64)])]
  transfers between devices with their start and end apart: 17 -> 32, of which waited for: 9 -> 15; matrix products, arithmetic and copies ran while one was open for 6% -> 5% of each run, Pallas kernels for 0% -> 3%
where the time goes in v2:
time: 383 us; the launch traced here: 379 us
  waiting for transfers between devices  219 us (57%)
  starting transfers between devices  76.7 us (20%)
  Pallas kernels  52.7 us (14%)
  local copies, waits for them, and re-layouts  15.2 us (4%)
  other arithmetic  14.6 us (4%)
    ppermute x17, waiting for transfers between devices, across(): return lax.ppermute(array, 'seq', [(i, i ^ flip) for i in range(64)])  141 us
    all_to_all x4, waiting for transfers between devices, exchange(): return lax.all_to_all(array, 'seq', split_axis=0, concat_axis=0, tiled=True)  40.2 us
    all_to_all x4, starting transfers between devices, exchange(): return lax.all_to_all(array, 'seq', split_axis=0, concat_axis=0, tiled=True)  40.1 us
    pallas_call x1, Pallas kernels, attend(): pl.pallas_call(attend_kernel, out_shape=(piece, piece, piece, piece, piec...  36.3 us
    ppermute x7, waiting for transfers between devices, body(): lax.ppermute(rows, 'seq', [(i, (i + 8 * d) % 64) for i in range(64)])  35 us
    ppermute x7, starting transfers between devices, body(): lax.ppermute(rows, 'seq', [(i, (i + 8 * d) % 64) for i in range(64)])  16 us
    ppermute x4, starting transfers between devices, over_copies(): row = row + lax.ppermute(row, 'dp', [(i, i ^ flip) for i in range(4)])  11.1 us
    ppermute x17, starting transfers between devices, across(): return lax.ppermute(array, 'seq', [(i, i ^ flip) for i in range(64)])  9.51 us
  transfers between devices with their start and end apart: 32, of which 15 were waited for; matrix products, arithmetic and copies ran while one was open for 5% of the time, Pallas kernels for 3%

profile of v2, /device:TPU:16, one launch (start us, length us, event | category | flops | bytes accessed | tf_op | source)
XLA Modules:
  0.0 379.2 jit_solution(17451611939856225577)
XLA Ops:
  0.7 1.5 copy.42
  3.0 1.5 pad_maximum_fusion.1
  4.5 12.1 %all-to-all-start = ((bf16[64,2,64,128]{3,2,1,0:T(8,128)(2,1)}), bf16[64,2,64,128]{3,2,1,0:T(8,128)(2,1)S(1)}, u32[]{:S(2)}, u32[]{:S(2)}) async-start(bf16[64,2,64,128]{3,2,1,0:T(8,128)(2,1)} %pad_maximum_fusion.1), calls=%async_computation | async-start | bytes 4194304 | tf_op jit(solution)/shard_map/gather/all_to_all | solution.py:271
  16.7 0.9 select_bitcast_fusion
  18.1 0.8 select_bitcast_fusion.1
  19.1 0.7 reshape.136.list_ref
  19.8 1.2 fusion.5.count_ref
  21.0 0.6 pad_add_fusion.info_ref
  21.6 1.1 bitcast_select_fusion.1
  23.5 0.7 copy-done.6
  24.3 1.1 bitcast_select_fusion.3
  26.2 1.6 pad_maximum_fusion
  27.8 40.2 %all-to-all-done.kv_ref = bf16[64,2,64,128]{3,2,1,0:T(8,128)(2,1)S(1)} async-done(((bf16[64,2,64,128]{3,2,1,0:T(8,128)(2,1)}), bf16[64,2,64,128]{3,2,1,0:T(8,128)(2,1)S(1)}, u32[]{:S(2)}, u32[]{:S(2)}) %all-to-all-start) | async-done | bytes 2097184 | tf_op jit(solution)/shard_map/gather/all_to_all | solution.py:271
  68.0 5.6 %all-to-all-start.1 = ((bf16[64,2,64,128]{3,2,1,0:T(8,128)(2,1)}), bf16[64,2,64,128]{3,2,1,0:T(8,128)(2,1)}, u32[]{:S(2)}, u32[]{:S(2)}) async-start(bf16[64,2,64,128]{3,2,1,0:T(8,128)(2,1)} %pad_maximum_fusion), calls=%async_computation.1 | async-start | bytes 4194304 | tf_op jit(solution)/shard_map/gather/all_to_all | solution.py:271
  73.6 0.7 fusion.8
  74.4 1.6 collective-permute-start.5
  76.0 0.6 fusion
  76.6 0.7 fusion.2.k0
  77.4 0.6 collective-permute-start.2
  78.5 42.2 %collective-permute-done.5.v1 = bf16[64,64,128]{2,1,0:T(8,128)(2,1)S(1)} collective-permute-done((bf16[64,64,128]{2,1,0:T(8,128)(2,1)S(1)}, bf16[64,64,128]{2,1,0:T(8,128)(2,1)S(1)}, u32[]{:S(2)}, u32[]{:S(2)}) %collective-permute-start.5) | collective-permute-done | bytes 1048608 | tf_op jit(solution)/shard_map/gather/ppermute | solution.py:275
  120.7 22.5 %collective-permute-done.2.k1 = bf16[64,64,128]{2,1,0:T(8,128)(2,1)S(1)} collective-permute-done((bf16[64,64,128]{2,1,0:T(8,128)(2,1)S(1)}, bf16[64,64,128]{2,1,0:T(8,128)(2,1)S(1)}, u32[]{:S(2)}, u32[]{:S(2)}) %collective-permute-start.2) | collective-permute-done | bytes 1048608 | tf_op jit(solution)/shard_map/gather/ppermute | solution.py:275
  143.2 1.2 constant_dynamic-slice_fusion.1.gains_ref
  144.5 1.0 copy-done.14
  145.4 1.0 copy-done.15
  146.4 36.3 %attend.1 = (bf16[64,2,64,128]{3,2,1,0:T(8,128)(2,1)}, bf16[64,2,64,128]{3,2,1,0:T(8,128)(2,1)}, bf16[64,2,64,128]{3,2,1,0:T(8,128)(2,1)}, bf16[64,2,64,128]{3,2...) custom-call(s32[2]{0:T(128)} %pad_add_fusion.info_ref, s32[128]{0:T(128)} %fusion.5.count_ref, ...), custom_call_target="tpu_custom_call" | custom-call | flops 6000000000 | bytes 20971520 | tf_op jit(solution)/shard_map/attend/attend/pallas_call | solution.py:159
  182.8 4.4 %collective-permute-done.8 = bf16[64,2,64,128]{3,2,1,0:T(8,128)(2,1)S(1)} collective-permute-done((bf16[64,2,64,128]{3,2,1,0:T(8,128)(2,1)}, bf16[64,2,64,128]{3,2,1,0:T(8,128)(2,1)S(1)}, u32[]{:S(2)}, u32[]{:S(2)}) %collective-permute-start.8) | collective-permute-done | bytes 2097184 | tf_op jit(solution)/shard_map/return/ppermute | solution.py:275
  187.2 3.8 %add_convert_fusion = bf16[64,2,64,128]{3,2,1,0:T(8,128)(2,1)} fusion(bf16[64,2,64,128]{3,2,1,0:T(8,128)(2,1)S(1)} %collective-permute-done.8, bf16[64,2,64,128]{3,2,1,0:T(8,128)(2,1)} %get-tuple-element.31), kind=kLoop, calls=%fused_computation | loop fusion | flops 4194304 | bytes 6291456 | tf_op jit(solution)/shard_map/return/convert_element_type | solution.py:324
  191.1 12.3 %all-to-all-start.2 = ((bf16[64,2,64,128]{3,2,1,0:T(8,128)(2,1)}), bf16[64,2,64,128]{3,2,1,0:T(8,128)(2,1)S(1)}, u32[]{:S(2)}, u32[]{:S(2)}) async-start(bf16[64,2,64,128]{3,2,1,0:T(8,128)(2,1)} %get-tuple-element.33), calls=%async_computation.2 | async-start | bytes 4194304 | tf_op jit(solution)/shard_map/return/all_to_all | solution.py:271
  203.5 1.7 collective-permute-start.11
  205.2 0.7 slice.48
  205.9 3.8 collective-permute-start.12
  209.6 1.2 constant_dynamic-slice_fusion.2.gain_ref
  210.8 62.5 %collective-permute-done.11.far_ref = bf16[64,2,64,128]{3,2,1,0:T(8,128)(2,1)} collective-permute-done((bf16[64,2,64,128]{3,2,1,0:T(8,128)(2,1)}, bf16[64,2,64,128]{3,2,1,0:T(8,128)(2,1)}, u32[]{:S(2)}, u32[]{:S(2)}) %collective-permute-start.11) | collective-permute-done | bytes 2097184 | tf_op jit(solution)/shard_map/return/ppermute | solution.py:275
  273.3 8.5 %finish.1 = (bf16[64,2,64,128]{3,2,1,0:T(8,128)(2,1)}, f32[8,128]{1,0:T(8,128)}) custom-call(bf16[64,2,64,128]{3,2,1,0:T(8,128)(2,1)} %get-tuple-element.36.own_ref, bf16[64,2,64,128]{3,2,1,0:T(8,128)(2,1)} %collective-permute-done.10.core_ref, bf16[64,2,64,128]{3,2,1,0:T(8,128)(2,1)} %collective-permute-done.11.far_ref, bf16[64,2,64,128]{3,2,1,0:T(8,128)(2,1)} %copy-done.2, ...), custom_call_target="tpu_custom_call" | custom-call | tf_op jit(solution)/shard_map/return/finish/pallas_call | solution.py:208
  281.8 0.7 slice.49
  282.5 3.8 collective-permute-start.16
  286.3 0.7 slice_add_fusion.1
  286.9 1.2 collective-permute-start.13
  288.2 0.7 slice_add_fusion
  288.9 2.3 collective-permute-start.17
  291.2 0.8 collective-permute-done.13
  292.0 1.9 collective-permute-done.17
  294.0 0.6 collective-permute-start.15
  294.5 0.5 collective-permute-done.18
  295.1 1.0 collective-permute-start.19
  296.1 1.5 collective-permute-done.15
  297.6 1.0 collective-permute-done.19
  298.6 10.2 %all-to-all-start.3 = ((bf16[64,2,64,128]{3,2,1,0:T(8,128)(2,1)}), bf16[64,2,64,128]{3,2,1,0:T(8,128)(2,1)}, u32[]{:S(2)}, u32[]{:S(2)}) async-start(bf16[64,2,64,128]{3,2,1,0:T(8,128)(2,1)} %get-tuple-element.39), calls=%async_computation.3 | async-start | bytes 4194304 | tf_op jit(solution)/shard_map/return/all_to_all | solution.py:271
  308.8 3.1 collective-permute-start.20
  311.9 4.4 %collective-permute-done.20 = f32[2,128]{1,0:T(2,128)S(1)} collective-permute-done((f32[2,128]{1,0:T(2,128)S(1)}, f32[2,128]{1,0:T(2,128)S(1)}, u32[]{:S(2)}, u32[]{:S(2)}) %collective-permute-start.20) | collective-permute-done | bytes 1056 | tf_op jit(solution)/shard_map/gains/ppermute | solution.py:275
  316.3 4.1 %collective-permute-start.21 = (f32[2,2,128]{2,1,0:T(2,128)S(1)}, f32[2,2,128]{2,1,0:T(2,128)S(1)}, u32[]{:S(2)}, u32[]{:S(2)}) collective-permute-start(f32[2,2,128]{2,1,0:T(2,128)S(1)} %maximum_select_fusion), channel_id=1, source_target_pairs={{0,56},{1,57},{2,58},{3,59},{4,60},{5,61},{6,62},{7,63},{8,0},{9,1... | collective-permute-start | bytes 6152 | tf_op jit(solution)/shard_map/gains/ppermute | solution.py:339
  320.5 1.0 collective-permute-start.26
  321.5 4.6 %collective-permute-start.25 = (f32[2,2,128]{2,1,0:T(2,128)S(1)}, f32[2,2,128]{2,1,0:T(2,128)S(1)}, u32[]{:S(2)}, u32[]{:S(2)}) collective-permute-start(f32[2,2,128]{2,1,0:T(2,128)S(1)} %maximum_select_fusion), channel_id=1, source_target_pairs={{0,24},{1,25},{2,26},{3,27},{4,28},{5,29},{6,30},{7,31},{8,32},{9,... | collective-permute-start | bytes 6152 | tf_op jit(solution)/shard_map/gains/ppermute | solution.py:339
  326.1 0.9 collective-permute-start.24
  327.0 29.0 %collective-permute-done.21 = f32[2,2,128]{2,1,0:T(2,128)S(1)} collective-permute-done((f32[2,2,128]{2,1,0:T(2,128)S(1)}, f32[2,2,128]{2,1,0:T(2,128)S(1)}, u32[]{:S(2)}, u32[]{:S(2)}) %collective-permute-start.21) | collective-permute-done | bytes 2080 | tf_op jit(solution)/shard_map/gains/ppermute | solution.py:339
  355.9 1.7 collective-permute-start.22
  357.7 2.7 collective-permute-done.22
  360.4 3.6 collective-permute-start.23
  364.0 3.3 collective-permute-done.23
  367.8 0.6 slice_bitcast_fusion.7
  368.4 2.0 collective-permute-done.9.got_ref
  370.3 1.0 copy-done.10
  371.3 4.0 %unpack_front.1 = (bf16[256,2048]{1,0:T(8,128)(2,1)}, bf16[256,2048]{1,0:T(8,128)(2,1)}) custom-call(s32[1]{0:T(128)} %bitcast.core_ref, bf16[64,2,64,128]{3,2,1,0:T(8,128)(2,1)} %copy-done.3, bf16[16,2,2,64,128]{4,3,2,1,0:T(8,128)(2,1)} %copy-done.10), custom_call_target="tpu_custom_call" | custom-call | bytes 4194304 | tf_op jit(solution)/shard_map/return/unpack_front/pallas_call | solution.py:251
  375.3 3.9 %unpack.1 = (bf16[256,2048]{1,0:T(8,128)(2,1)}, bf16[256,2048]{1,0:T(8,128)(2,1)}) custom-call(bf16[64,2,64,128]{3,2,1,0:T(8,128)(2,1)} %all-to-all-done.3.in_ref), custom_call_target="tpu_custom_call" | custom-call | bytes 4194304 | tf_op jit(solution)/shard_map/return/unpack/pallas_call | solution.py:227
  (99 shorter events, 4.4 us)
Async XLA Ops:
  0.6 18.3 %copy-start = (s32[1,16,128,8]{2,3,1,0:T(8,128)S(1)}, s32[1,16,128,8]{2,3,1,0:T(8,128)}, u32[]{:S(2)}) copy-start(s32[1,16,128,8]{2,3,1,0:T(8,128)} %param.14) | copy-start | bytes 196612
  0.6 1.8 copy-start.8
  4.5 12.1 %copy-start.4 = (bf16[1,256,2048]{2,1,0:T(8,128)(2,1)S(1)}, bf16[1,256,2048]{2,1,0:T(8,128)(2,1)}, u32[]{:S(2)}) copy-start(bf16[1,256,2048]{2,1,0:T(8,128)(2,1)} %param.11) | copy-start | bytes 3145732
  4.5 63.4 %all-to-all-start = ((bf16[64,2,64,128]{3,2,1,0:T(8,128)(2,1)}), bf16[64,2,64,128]{3,2,1,0:T(8,128)(2,1)S(1)}, u32[]{:S(2)}, u32[]{:S(2)}) async-start(bf16[64,2,64,128]{3,2,1,0:T(8,128)(2,1)} %pad_maximum_fusion.1), calls=%async_computation | async-start | bytes 4194304 | tf_op jit(solution)/shard_map/gather/all_to_all | solution.py:271
  16.6 1.4 copy-start.5
  17.5 4.0 %collective-permute-start.1 = (bf16[2,64,2048]{2,1,0:T(8,128)(2,1)}, bf16[2,64,2048]{2,1,0:T(8,128)(2,1)}, u32[]{:S(2)}, u32[]{:S(2)}) collective-permute-start(bf16[2,64,2048]{2,1,0:T(8,128)(2,1)} %select_bitcast_fusion), channel_id=1, source_target_pairs={{0,1},{1,0},{2,3},{3,2},{4,5},{5,4},{6,7},{7,6},{8,9},{9,8},{10,11... | collective-permute-start | bytes 1572872 | tf_op jit(solution)/shard_map/gather/ppermute | solution.py:275
  18.9 4.6 %collective-permute-start = (bf16[2,64,2048]{2,1,0:T(8,128)(2,1)}, bf16[2,64,2048]{2,1,0:T(8,128)(2,1)}, u32[]{:S(2)}, u32[]{:S(2)}) collective-permute-start(bf16[2,64,2048]{2,1,0:T(8,128)(2,1)} %select_bitcast_fusion.1), channel_id=1, source_target_pairs={{0,1},{1,0},{2,3},{3,2},{4,5},{5,4},{6,7},{7,6},{8,9},{9,8},{10,11... | collective-permute-start | bytes 1572872 | tf_op jit(solution)/shard_map/gather/ppermute | solution.py:275
  23.0 1.2 copy-start.6
  68.0 8.6 %copy-start.2 = (bf16[64,2,64,128]{3,2,1,0:T(8,128)(2,1)}, bf16[64,2,64,128]{3,2,1,0:T(8,128)(2,1)S(1)}, u32[]{:S(2)}) copy-start(bf16[64,2,64,128]{3,2,1,0:T(8,128)(2,1)S(1)} %all-to-all-done.kv_ref) | copy-start | bytes 6291460
  68.0 78.4 %all-to-all-start.1 = ((bf16[64,2,64,128]{3,2,1,0:T(8,128)(2,1)}), bf16[64,2,64,128]{3,2,1,0:T(8,128)(2,1)}, u32[]{:S(2)}, u32[]{:S(2)}) async-start(bf16[64,2,64,128]{3,2,1,0:T(8,128)(2,1)} %pad_maximum_fusion), calls=%async_computation.1 | async-start | bytes 4194304 | tf_op jit(solution)/shard_map/gather/all_to_all | solution.py:271
  74.4 70.0 %copy-start.9 = (bf16[64,64,128]{2,1,0:T(8,128)(2,1)}, bf16[64,64,128]{2,1,0:T(8,128)(2,1)S(1)}, u32[]{:S(2)}) copy-start(bf16[64,64,128]{2,1,0:T(8,128)(2,1)S(1)} %slice_bitcast_fusion.2.v0) | copy-start | bytes 3145732
  74.4 46.3 %collective-permute-start.5 = (bf16[64,64,128]{2,1,0:T(8,128)(2,1)S(1)}, bf16[64,64,128]{2,1,0:T(8,128)(2,1)S(1)}, u32[]{:S(2)}, u32[]{:S(2)}) collective-permute-start(bf16[64,64,128]{2,1,0:T(8,128)(2,1)S(1)} %slice_bitcast_fusion.2.v0), channel_id=1, source_target_pairs={{0,2},{1,3},{2,0},{3,1},{4,6},{5,7},{6,4},{7,5},{8,10},{9,11},{10,... | collective-permute-start | bytes 3145736 | tf_op jit(solution)/shard_map/gather/ppermute | solution.py:275
  77.4 69.1 %copy-start.7 = (bf16[64,64,128]{2,1,0:T(8,128)(2,1)}, bf16[64,64,128]{2,1,0:T(8,128)(2,1)S(1)}, u32[]{:S(2)}) copy-start(bf16[64,64,128]{2,1,0:T(8,128)(2,1)S(1)} %fusion.2.k0) | copy-start | bytes 3145732
  77.4 65.8 %collective-permute-start.2 = (bf16[64,64,128]{2,1,0:T(8,128)(2,1)S(1)}, bf16[64,64,128]{2,1,0:T(8,128)(2,1)S(1)}, u32[]{:S(2)}, u32[]{:S(2)}) collective-permute-start(bf16[64,64,128]{2,1,0:T(8,128)(2,1)S(1)} %fusion.2.k0), channel_id=1, source_target_pairs={{0,2},{1,3},{2,0},{3,1},{4,6},{5,7},{6,4},{7,5},{8,10},{9,11},{10,... | collective-permute-start | bytes 3145736 | tf_op jit(solution)/shard_map/gather/ppermute | solution.py:275
  78.0 66.4 %collective-permute-start.6 = (bf16[64,64,128]{2,1,0:T(8,128)(2,1)S(1)}, bf16[64,64,128]{2,1,0:T(8,128)(2,1)S(1)}, u32[]{:S(2)}, u32[]{:S(2)}) collective-permute-start(bf16[64,64,128]{2,1,0:T(8,128)(2,1)S(1)} %slice_bitcast_fusion.2.v0), channel_id=1, source_target_pairs={{0,1},{1,0},{2,3},{3,2},{4,5},{5,4},{6,7},{7,6},{8,9},{9,8},{10,11... | collective-permute-start | bytes 3145736 | tf_op jit(solution)/shard_map/gather/ppermute | solution.py:275
  78.0 66.4 %collective-permute-start.3 = (bf16[64,64,128]{2,1,0:T(8,128)(2,1)S(1)}, bf16[64,64,128]{2,1,0:T(8,128)(2,1)S(1)}, u32[]{:S(2)}, u32[]{:S(2)}) collective-permute-start(bf16[64,64,128]{2,1,0:T(8,128)(2,1)S(1)} %fusion.2.k0), channel_id=1, source_target_pairs={{0,1},{1,0},{2,3},{3,2},{4,5},{5,4},{6,7},{7,6},{8,9},{9,8},{10,11... | collective-permute-start | bytes 3145736 | tf_op jit(solution)/shard_map/gather/ppermute | solution.py:275
  120.7 23.8 %copy-start.11 = (bf16[64,64,128]{2,1,0:T(8,128)(2,1)}, bf16[64,64,128]{2,1,0:T(8,128)(2,1)S(1)}, u32[]{:S(2)}) copy-start(bf16[64,64,128]{2,1,0:T(8,128)(2,1)S(1)} %collective-permute-done.5.v1) | copy-start | bytes 3145732
  120.7 23.8 %collective-permute-start.7 = (bf16[64,64,128]{2,1,0:T(8,128)(2,1)S(1)}, bf16[64,64,128]{2,1,0:T(8,128)(2,1)S(1)}, u32[]{:S(2)}, u32[]{:S(2)}) collective-permute-start(bf16[64,64,128]{2,1,0:T(8,128)(2,1)S(1)} %collective-permute-done.5.v1), channel_id=1, source_target_pairs={{0,1},{1,0},{2,3},{3,2},{4,5},{5,4},{6,7},{7,6},{8,9},{9,8},{10,11... | collective-permute-start | bytes 3145736 | tf_op jit(solution)/shard_map/gather/ppermute | solution.py:275
  143.2 3.3 copy-start.12
  143.2 3.2 collective-permute-start.4
  144.4 2.0 copy-start.13
  144.4 1.0 copy-start.14
  145.4 1.0 copy-start.15
  182.7 4.5 %collective-permute-start.8 = (bf16[64,2,64,128]{3,2,1,0:T(8,128)(2,1)}, bf16[64,2,64,128]{3,2,1,0:T(8,128)(2,1)S(1)}, u32[]{:S(2)}, u32[]{:S(2)}) collective-permute-start(bf16[64,2,64,128]{3,2,1,0:T(8,128)(2,1)} %get-tuple-element.32), channel_id=1, source_target_pairs={{0,1},{1,0},{2,3},{3,2},{4,5},{5,4},{6,7},{7,6},{8,9},{9,8},{10,11... | collective-permute-start | bytes 6291464 | tf_op jit(solution)/shard_map/return/ppermute | solution.py:275
  191.1 107.6 %all-to-all-start.2 = ((bf16[64,2,64,128]{3,2,1,0:T(8,128)(2,1)}), bf16[64,2,64,128]{3,2,1,0:T(8,128)(2,1)S(1)}, u32[]{:S(2)}, u32[]{:S(2)}) async-start(bf16[64,2,64,128]{3,2,1,0:T(8,128)(2,1)} %get-tuple-element.33), calls=%async_computation.2 | async-start | bytes 4194304 | tf_op jit(solution)/shard_map/return/all_to_all | solution.py:271
  203.4 7.5 %collective-permute-start.10 = (bf16[64,2,64,128]{3,2,1,0:T(8,128)(2,1)}, bf16[64,2,64,128]{3,2,1,0:T(8,128)(2,1)}, u32[]{:S(2)}, u32[]{:S(2)}) collective-permute-start(bf16[64,2,64,128]{3,2,1,0:T(8,128)(2,1)} %get-tuple-element.37), channel_id=1, source_target_pairs={{0,1},{1,0},{2,3},{3,2},{4,5},{5,4},{6,7},{7,6},{8,9},{9,8},{10,11... | collective-permute-start | bytes 6291464 | tf_op jit(solution)/shard_map/return/ppermute | solution.py:275
  203.5 69.8 %collective-permute-start.11 = (bf16[64,2,64,128]{3,2,1,0:T(8,128)(2,1)}, bf16[64,2,64,128]{3,2,1,0:T(8,128)(2,1)}, u32[]{:S(2)}, u32[]{:S(2)}) collective-permute-start(bf16[64,2,64,128]{3,2,1,0:T(8,128)(2,1)} %add_convert_fusion), channel_id=1, source_target_pairs={{0,2},{1,3},{2,0},{3,1},{4,6},{5,7},{6,4},{7,5},{8,10},{9,11},{10,... | collective-permute-start | bytes 6291464 | tf_op jit(solution)/shard_map/return/ppermute | solution.py:275
  205.9 80.4 %collective-permute-start.12 = (f32[1,128]{1,0:T(1,128)S(1)}, f32[1,128]{1,0:T(1,128)S(1)}, u32[]{:S(2)}, u32[]{:S(2)}) collective-permute-start(f32[1,128]{1,0:T(1,128)S(1)} %slice.48), channel_id=1, source_target_pairs={{0,64},{64,0},{128,192},{192,128},{1,65},{65,1},{129,193},{193,129... | collective-permute-start | bytes 1544 | tf_op jit(solution)/shard_map/gains/ppermute | solution.py:288
  282.5 5.7 %collective-permute-start.16 = (f32[1,128]{1,0:T(1,128)S(1)}, f32[1,128]{1,0:T(1,128)S(1)}, u32[]{:S(2)}, u32[]{:S(2)}) collective-permute-start(f32[1,128]{1,0:T(1,128)S(1)} %slice.49), channel_id=1, source_target_pairs={{0,64},{64,0},{128,192},{192,128},{1,65},{65,1},{129,193},{193,129... | collective-permute-start | bytes 1544 | tf_op jit(solution)/shard_map/gains/ppermute | solution.py:288
  286.9 5.0 %collective-permute-start.13 = (f32[1,128]{1,0:T(1,128)S(1)}, f32[1,128]{1,0:T(1,128)S(1)}, u32[]{:S(2)}, u32[]{:S(2)}) collective-permute-start(f32[1,128]{1,0:T(1,128)S(1)} %slice_add_fusion.1), channel_id=1, source_target_pairs={{0,128},{64,192},{128,0},{192,64},{1,129},{65,193},{129,1},{193,65... | collective-permute-start | bytes 1544 | tf_op jit(solution)/shard_map/gains/ppermute | solution.py:288
  288.9 5.0 %collective-permute-start.17 = (f32[1,128]{1,0:T(1,128)S(1)}, f32[1,128]{1,0:T(1,128)S(1)}, u32[]{:S(2)}, u32[]{:S(2)}) collective-permute-start(f32[1,128]{1,0:T(1,128)S(1)} %slice_add_fusion), channel_id=1, source_target_pairs={{0,128},{64,192},{128,0},{192,64},{1,129},{65,193},{129,1},{193,65... | collective-permute-start | bytes 1544 | tf_op jit(solution)/shard_map/gains/ppermute | solution.py:288
  292.0 1.9 collective-permute-start.14
  293.9 1.1 collective-permute-start.18
  294.0 3.6 collective-permute-start.15
  295.1 3.5 collective-permute-start.19
  298.6 68.9 %copy-start.3 = (bf16[64,2,64,128]{3,2,1,0:T(8,128)(2,1)}, bf16[64,2,64,128]{3,2,1,0:T(8,128)(2,1)S(1)}, u32[]{:S(2)}) copy-start(bf16[64,2,64,128]{3,2,1,0:T(8,128)(2,1)S(1)} %all-to-all-done.2.in_ref) | copy-start | bytes 6291460
  298.6 76.7 %all-to-all-start.3 = ((bf16[64,2,64,128]{3,2,1,0:T(8,128)(2,1)}), bf16[64,2,64,128]{3,2,1,0:T(8,128)(2,1)}, u32[]{:S(2)}, u32[]{:S(2)}) async-start(bf16[64,2,64,128]{3,2,1,0:T(8,128)(2,1)} %get-tuple-element.39), calls=%async_computation.3 | async-start | bytes 4194304 | tf_op jit(solution)/shard_map/return/all_to_all | solution.py:271
  308.8 7.5 %collective-permute-start.20 = (f32[2,128]{1,0:T(2,128)S(1)}, f32[2,128]{1,0:T(2,128)S(1)}, u32[]{:S(2)}, u32[]{:S(2)}) collective-permute-start(f32[2,128]{1,0:T(2,128)S(1)} %get-tuple-element.52), channel_id=1, source_target_pairs={{0,4},{1,5},{2,6},{3,7},{4,0},{5,1},{6,2},{7,3},{8,12},{9,13},{10,... | collective-permute-start | bytes 3080 | tf_op jit(solution)/shard_map/gains/ppermute | solution.py:275
  316.3 39.6 %collective-permute-start.21 = (f32[2,2,128]{2,1,0:T(2,128)S(1)}, f32[2,2,128]{2,1,0:T(2,128)S(1)}, u32[]{:S(2)}, u32[]{:S(2)}) collective-permute-start(f32[2,2,128]{2,1,0:T(2,128)S(1)} %maximum_select_fusion), channel_id=1, source_target_pairs={{0,56},{1,57},{2,58},{3,59},{4,60},{5,61},{6,62},{7,63},{8,0},{9,1... | collective-permute-start | bytes 6152 | tf_op jit(solution)/shard_map/gains/ppermute | solution.py:339
  320.5 46.9 %collective-permute-start.27 = (f32[2,2,128]{2,1,0:T(2,128)S(1)}, f32[2,2,128]{2,1,0:T(2,128)S(1)}, u32[]{:S(2)}, u32[]{:S(2)}) collective-permute-start(f32[2,2,128]{2,1,0:T(2,128)S(1)} %maximum_select_fusion), channel_id=1, source_target_pairs={{0,8},{1,9},{2,10},{3,11},{4,12},{5,13},{6,14},{7,15},{8,16},{9,17... | collective-permute-start | bytes 6152 | tf_op jit(solution)/shard_map/gains/ppermute | solution.py:339
  320.5 46.9 %collective-permute-start.26 = (f32[2,2,128]{2,1,0:T(2,128)S(1)}, f32[2,2,128]{2,1,0:T(2,128)S(1)}, u32[]{:S(2)}, u32[]{:S(2)}) collective-permute-start(f32[2,2,128]{2,1,0:T(2,128)S(1)} %maximum_select_fusion), channel_id=1, source_target_pairs={{0,16},{1,17},{2,18},{3,19},{4,20},{5,21},{6,22},{7,23},{8,24},{9,... | collective-permute-start | bytes 6152 | tf_op jit(solution)/shard_map/gains/ppermute | solution.py:339
  321.5 45.9 %collective-permute-start.25 = (f32[2,2,128]{2,1,0:T(2,128)S(1)}, f32[2,2,128]{2,1,0:T(2,128)S(1)}, u32[]{:S(2)}, u32[]{:S(2)}) collective-permute-start(f32[2,2,128]{2,1,0:T(2,128)S(1)} %maximum_select_fusion), channel_id=1, source_target_pairs={{0,24},{1,25},{2,26},{3,27},{4,28},{5,29},{6,30},{7,31},{8,32},{9,... | collective-permute-start | bytes 6152 | tf_op jit(solution)/shard_map/gains/ppermute | solution.py:339
  326.1 41.3 %collective-permute-start.24 = (f32[2,2,128]{2,1,0:T(2,128)S(1)}, f32[2,2,128]{2,1,0:T(2,128)S(1)}, u32[]{:S(2)}, u32[]{:S(2)}) collective-permute-start(f32[2,2,128]{2,1,0:T(2,128)S(1)} %maximum_select_fusion), channel_id=1, source_target_pairs={{0,32},{1,33},{2,34},{3,35},{4,36},{5,37},{6,38},{7,39},{8,40},{9,... | collective-permute-start | bytes 6152 | tf_op jit(solution)/shard_map/gains/ppermute | solution.py:339
  355.9 4.5 %collective-permute-start.22 = (f32[2,2,128]{2,1,0:T(2,128)S(1)}, f32[2,2,128]{2,1,0:T(2,128)S(1)}, u32[]{:S(2)}, u32[]{:S(2)}) collective-permute-start(f32[2,2,128]{2,1,0:T(2,128)S(1)} %maximum_select_fusion), channel_id=1, source_target_pairs={{0,48},{1,49},{2,50},{3,51},{4,52},{5,53},{6,54},{7,55},{8,56},{9,... | collective-permute-start | bytes 6152 | tf_op jit(solution)/shard_map/gains/ppermute | solution.py:339
  360.4 6.9 %collective-permute-start.23 = (f32[2,2,128]{2,1,0:T(2,128)S(1)}, f32[2,2,128]{2,1,0:T(2,128)S(1)}, u32[]{:S(2)}, u32[]{:S(2)}) collective-permute-start(f32[2,2,128]{2,1,0:T(2,128)S(1)} %maximum_select_fusion), channel_id=1, source_target_pairs={{0,40},{1,41},{2,42},{3,43},{4,44},{5,45},{6,46},{7,47},{8,48},{9,... | collective-permute-start | bytes 6152 | tf_op jit(solution)/shard_map/gains/ppermute | solution.py:339
  367.6 2.7 collective-permute-start.9
  370.3 1.0 copy-start.10
  370.3 8.9 %copy-start.1 = (s32[1,16,128,8]{2,3,1,0:T(8,128)S(1)}, s32[1,16,128,8]{2,3,1,0:T(8,128)}, u32[]{:S(2)}) copy-start(s32[1,16,128,8]{2,3,1,0:T(8,128)} %param.14) | copy-start | bytes 196612

commit v3 on v2

v3 whole, which is shorter than its diff:
```python
import functools
import math

import jax
import jax.numpy as jnp
from jax import lax
from jax.experimental import pallas as pl
from jax.experimental.pallas import tpu as pltpu
from jax.sharding import PartitionSpec as P

HEAD_DIM = 128
EPS = 1e-06
INV_ROOT = 1.0 / math.sqrt(HEAD_DIM)
LOG2E = math.log2(math.e)
NT = (((1,), (1,)), ((), ()))
TN = (((0,), (0,)), ((), ()))
NN = (((1,), (0,)), ((), ()))
GROUPS = 32
BUCKETS = (8, 6, 4, 2)
TOGETHER = 1
SEND_ORDER = (5, 3, 1, 7, 4, 2, 0, 6)


def dot(a, b, dims):
    return lax.dot_general(a, b, dims, preferred_element_type=jnp.float32)


def attend_kernel(info_ref, count_ref, list_ref, *refs):
    pieces = refs[:8]
    qg_hbm, gains_ref, og_hbm = refs[8:11]
    parts = refs[11:19]
    gain_query_ref, gain_key_ref, ktab, vtab, acc, qg_ref, og_ref, stage, order_ref, in_sems, out_sems = refs[19:]
    place_x_core = info_ref[0]
    head = info_ref[1]
    copies = [pltpu.make_async_copy(qg_hbm, qg_ref, in_sems.at[16])]
    for i, piece in enumerate(pieces):
        for j, table in enumerate((ktab, vtab)):
            copies.append(pltpu.make_async_copy(piece.at[j], table.at[pl.ds(i * 16, 16)], in_sems.at[2 * i + j]))
    for copy in copies:
        copy.start()

    def block_of(g):
        across = place_x_core ^ (6 * ((g >> 1) & 1))
        return (g >> 2) * 16 + across * 2 + (g & 1)

    stops = []
    stop = 0
    for which, most in enumerate(BUCKETS):
        below = BUCKETS[which + 1] if which + 1 < len(BUCKETS) else 0

        def place(g, at, most=most, below=below):
            count = count_ref[block_of(g)]
            inside = jnp.logical_and(count <= most, count > below)

            @pl.when(inside)
            def _():
                order_ref[at] = g

            return at + inside.astype(jnp.int32)

        stop = lax.fori_loop(0, GROUPS, place, jnp.int32(stop))
        stops.append(stop)

    @pl.loop(0, 128)
    def _(t):
        acc[t] = jnp.zeros((128, 256), jnp.float32)

    gain_query = gains_ref[pl.ds(head, 1), :]
    gain_key = gains_ref[pl.ds(16 + head, 1), :]
    gain_query_ref[...] = jnp.zeros_like(gain_query_ref)
    gain_key_ref[...] = jnp.zeros_like(gain_key_ref)
    for copy in copies:
        copy.wait()

    zero = jnp.zeros((128, 128), jnp.bfloat16)

    def forward(i, most, first):
        g = order_ref[i]
        block = block_of(g)
        live = count_ref[block]
        listed = [list_ref[block * 8 + j] for j in range(most)]
        spots = [(((c >> 1) & 7) ^ place_x_core) * 16 + (c >> 4) * 2 + (c & 1) for c in listed]
        wide = qg_ref[g >> 1, 0, g & 1].astype(jnp.float32)
        grad = qg_ref[g >> 1, 1, g & 1]
        scale = lax.rsqrt(jnp.mean(wide * wide, axis=-1, keepdims=True) + EPS)
        hat = wide * scale
        normed = (hat * gain_query).astype(jnp.bfloat16)
        keys = jnp.concatenate([ktab[t] for t in spots], axis=0)
        values = jnp.concatenate([vtab[t] for t in spots], axis=0)
        flat = dot(normed, keys, NT)
        scores = []
        for j in range(most):
            s = flat[:, j * 128:(j + 1) * 128]
            if j == most - 1 or (j and not first):
                s = jnp.where(j < live, s, -jnp.inf)
            scores.append(s)
        top = jnp.max(functools.reduce(jnp.maximum, scores), axis=-1, keepdims=True)
        exps = [jnp.exp2((s - top) * (INV_ROOT * LOG2E)) for s in scores]
        total = jnp.sum(functools.reduce(jnp.add, exps), axis=-1, keepdims=True)
        inverse = 1.0 / total
        weights = [(e * inverse).astype(jnp.bfloat16) for e in exps]
        attended = dot(jnp.concatenate(weights, axis=1), values, NN).astype(jnp.bfloat16)
        og_ref[g >> 1, 0, g & 1] = attended
        inner = jnp.sum(grad.astype(jnp.float32) * attended.astype(jnp.float32), axis=-1, keepdims=True)
        return g, spots, wide, grad, scale, hat, normed, keys, values, weights, inner

    def backward(state, most):
        g, spots, wide, grad, scale, hat, normed, keys, values, weights, inner = state
        flat = dot(grad, values, NT)
        score_grads = []
        for j in range(most):
            wg = flat[:, j * 128:(j + 1) * 128]
            score_grads.append((weights[j].astype(jnp.float32) * (wg - inner)).astype(jnp.bfloat16))
        norm_grad = dot(jnp.concatenate(score_grads, axis=1), keys, NN) * INV_ROOT
        pair = jnp.concatenate(
            [jnp.concatenate([normed, zero], axis=1), jnp.concatenate([zero, grad], axis=1)], axis=0
        )
        for j in range(most):
            acc[spots[j]] += dot(jnp.concatenate([score_grads[j], weights[j]], axis=0), pair, TN)
        gain_query_ref[0:1, :] += jnp.sum(norm_grad * hat, axis=0, keepdims=True)
        weighted = norm_grad * gain_query
        mean = jnp.mean(weighted * wide, axis=-1, keepdims=True)
        og_ref[g >> 1, 1, g & 1] = (scale * weighted - wide * (scale * scale * scale) * mean).astype(jnp.bfloat16)

    start = 0
    for which, most in enumerate(BUCKETS):
        stop = (stops[which] + TOGETHER - 1) // TOGETHER

        @pl.loop(start, stop)
        def _(step, most=most):
            states = [forward(step * TOGETHER + u, most, u == 0) for u in range(TOGETHER)]
            for state in states:
                backward(state, most)

        start = stop

    back = [pltpu.make_async_copy(og_ref, og_hbm, out_sems.at[8])]
    back[0].start()
    for i in SEND_ORDER:

        @pl.loop(i * 16, i * 16 + 16, unroll=2)
        def _(t, i=i):
            both = acc[t]
            k = (both[:, :128] * INV_ROOT).astype(jnp.bfloat16)
            stage[i, 0, t - i * 16] = k
            stage[i, 1, t - i * 16] = both[:, 128:].astype(jnp.bfloat16)
            sums = jnp.sum(k.astype(jnp.float32) * ktab[t].astype(jnp.float32), axis=0, keepdims=True)
            gain_key_ref[0:1, :] += sums

        back.append(pltpu.make_async_copy(stage.at[i], parts[i], out_sems.at[i]))
        back[-1].start()
    gain_key_ref[0:1, :] = gain_key_ref[0:1, :] / gain_key
    for copy in back:
        copy.wait()


def attend(info, counts, lists, pieces, qg, gains):
    smem = pl.BlockSpec(memory_space=pltpu.SMEM)
    vmem = pl.BlockSpec(memory_space=pltpu.VMEM)
    hbm = pl.BlockSpec(memory_space=pl.ANY)
    part = jax.ShapeDtypeStruct((2, 16, 128, 128), jnp.bfloat16)
    row = jax.ShapeDtypeStruct((8, 128), jnp.float32)
    return pl.pallas_call(
        attend_kernel,
        out_shape=(jax.ShapeDtypeStruct((16, 2, 2, 128, 128), jnp.bfloat16),) + (part,) * 8 + (row, row),
        in_specs=[smem] * 3 + [hbm] * 9 + [vmem],
        out_specs=(hbm,) * 9 + (vmem,) * 2,
        scratch_shapes=[
            pltpu.VMEM((128, 128, 128), jnp.bfloat16),
            pltpu.VMEM((128, 128, 128), jnp.bfloat16),
            pltpu.VMEM((128, 128, 256), jnp.float32),
            pltpu.VMEM((16, 2, 2, 128, 128), jnp.bfloat16),
            pltpu.VMEM((16, 2, 2, 128, 128), jnp.bfloat16),
            pltpu.VMEM((8, 2, 16, 128, 128), jnp.bfloat16),
            pltpu.SMEM((GROUPS,), jnp.int32),
            pltpu.SemaphoreType.DMA((17,)),
            pltpu.SemaphoreType.DMA((9,)),
        ],
        compiler_params=pltpu.CompilerParams(vmem_limit_bytes=56 * 1024 * 1024),
        cost_estimate=pl.CostEstimate(flops=6 * 10**9, bytes_accessed=20 * 2**20, transcendentals=4 * 2**20),
        name="attend",
    )(info, counts, lists, *pieces, qg, gains)


HEADS = 16
ALONG_Z = [[8 * z + rest for z in range(8)] for rest in range(8)]


def finish_kernel(mine_ref, part_ref, core_ref, side_ref, far_ref, kv_ref, gain_ref, out_ref):
    half = mine_ref[0]
    plane = mine_ref[1]
    for own in (True, False):
        hh = half if own else 1 - half
        gain = gain_ref[pl.ds(2 * plane + hh, 1), :]
        if own:
            total = [part_ref[i, 0].astype(jnp.float32) + core_ref[i, 0].astype(jnp.float32) + side_ref[i, 0].astype(jnp.float32)
                     for i in range(2)]
        else:
            total = [far_ref[i, 0].astype(jnp.float32) for i in range(2)]
        wide = kv_ref[0, hh, 0].astype(jnp.float32)
        scale = lax.rsqrt(jnp.mean(wide * wide, axis=-1, keepdims=True) + EPS)
        weighted = total[0] * gain
        inner = jnp.mean(weighted * wide, axis=-1, keepdims=True)
        out_ref[0, hh, 0] = (scale * weighted - wide * (scale * scale * scale) * inner).astype(jnp.bfloat16)
        out_ref[0, hh, 1] = total[1].astype(jnp.bfloat16)


def finish(mine, part, core, side, far, kv, gain):
    piece = pl.BlockSpec((2, 1, 256, 128), lambda i: (0, i, 0, 0))
    return pl.pallas_call(
        finish_kernel,
        grid=(8,),
        out_shape=jax.ShapeDtypeStruct((8, 2, 2, 256, 128), jnp.bfloat16),
        in_specs=[pl.BlockSpec(memory_space=pltpu.SMEM), piece, piece, piece, piece,
                  pl.BlockSpec((1, 2, 1, 256, 128), lambda i: (i, 0, 0, 0, 0)),
                  pl.BlockSpec((HEADS, 128), lambda i: (0, 0))],
        out_specs=pl.BlockSpec((1, 2, 2, 256, 128), lambda i: (i, 0, 0, 0, 0)),
        name="finish",
    )(mine, part, core, side, far, kv, gain)


def unpack_kernel(in_ref, a_ref, b_ref):
    for i, out in enumerate((a_ref, b_ref)):
        for z in range(2):
            for hh in range(2):
                h = 2 * z + hh
                out[:, h * 128:(h + 1) * 128] = in_ref[z, hh, i]


def unpack(pieces):
    rows = jax.ShapeDtypeStruct((256, HEADS * HEAD_DIM), jnp.bfloat16)
    return pl.pallas_call(
        unpack_kernel,
        grid=(4,),
        out_shape=(rows, rows),
        in_specs=[pl.BlockSpec((2, 2, 2, 256, 128), lambda i: (i, 0, 0, 0, 0))],
        out_specs=(pl.BlockSpec((256, 512), lambda i: (0, i)),) * 2,
        cost_estimate=pl.CostEstimate(flops=0, bytes_accessed=2**22, transcendentals=0),
        name="unpack",
    )(pieces)


def unpack_front_kernel(mine_ref, in_ref, got_ref, a_ref, b_ref):
    half = mine_ref[0]
    for i, out in enumerate((a_ref, b_ref)):
        for z in range(2):
            here = pl.multiple_of((2 * z + half) * 128, 128)
            there = pl.multiple_of((2 * z + 1 - half) * 128, 128)
            out[:, pl.ds(here, 128)] = in_ref[z, 0, i]
            out[:, pl.ds(there, 128)] = got_ref[z, i]


def unpack_front(mine, pieces, got):
    rows = jax.ShapeDtypeStruct((256, HEADS * HEAD_DIM), jnp.bfloat16)
    return pl.pallas_call(
        unpack_front_kernel,
        grid=(4,),
        out_shape=(rows, rows),
        in_specs=[
            pl.BlockSpec(memory_space=pltpu.SMEM),
            pl.BlockSpec((2, 1, 2, 256, 128), lambda i: (i, 0, 0, 0, 0)),
            pl.BlockSpec((2, 2, 256, 128), lambda i: (i, 0, 0, 0)),
        ],
        out_specs=(pl.BlockSpec((256, 512), lambda i: (0, i)),) * 2,
        cost_estimate=pl.CostEstimate(flops=0, bytes_accessed=2**22, transcendentals=0),
        name="unpack_front",
    )(mine, pieces, got)


def along_z(array):
    return lax.all_to_all(array, "seq", split_axis=0, concat_axis=0, axis_index_groups=ALONG_Z, tiled=True)


def across(array, flip):
    return lax.ppermute(array, "seq", [(i, i ^ flip) for i in range(64)])


def by_head(rows):
    return jnp.transpose(rows.reshape(256, 8, 2, HEAD_DIM), (1, 2, 0, 3))


def wide_sum(*arrays):
    return functools.reduce(jnp.add, [a.astype(jnp.float32) for a in arrays]).astype(jnp.bfloat16)


def over_copies(row):
    for flip in (1, 2):
        row = row + lax.ppermute(row, "dp", [(i, i ^ flip) for i in range(4)])
    for flip in (1, 2):
        row = row + across(row, flip)
    return row


def body(query_rows, key_rows, value_rows, output_grad, query_gain, key_gain, block_list, block_count):
    position = lax.axis_index("seq")
    head = position // 4
    plane = position // 8
    half = head % 2
    lists = lax.dynamic_slice_in_dim(block_list[0], head, 1, 0).reshape(1024)
    counts = lax.dynamic_slice_in_dim(block_count[0], head, 1, 0).reshape(128)
    info = jnp.stack([position % 8, head]).astype(jnp.int32)
    mine = jnp.stack([half, plane]).astype(jnp.int32)
    gains = jnp.concatenate([query_gain, key_gain])

    def of_half(pair, which):
        return jnp.where(which == 0, pair[:, 0], pair[:, 1])

    with jax.named_scope("gather"):
        query_heads, grad_heads = by_head(query_rows[0]), by_head(output_grad[0])
        given = jnp.stack([of_half(query_heads, 1 - half), of_half(grad_heads, 1 - half)], axis=1)
        got = across(given, 6)
        kept = jnp.stack([of_half(query_heads, half), of_half(grad_heads, half)], axis=1)
        kv = along_z(jnp.stack([by_head(key_rows[0]), by_head(value_rows[0])], axis=2))
        pair_send = jnp.stack([kept, got], axis=1)
        pair_send, kv, lists, counts, info, mine, gains = lax.optimization_barrier(
            (pair_send, kv, lists, counts, info, mine, gains)
        )
        wide = kv[:, :, 0].astype(jnp.float32)
        scale = lax.rsqrt(jnp.mean(wide * wide, axis=-1, keepdims=True) + EPS)
        pair_gain = lax.dynamic_slice_in_dim(key_gain, 2 * plane, 2, 0)
        normed = (wide * scale * pair_gain[None, :, None, :]).astype(jnp.bfloat16)
        values = kv[:, :, 1]
        cross_send = jnp.stack([of_half(normed, 1 - half), of_half(values, 1 - half)])
        own = jnp.stack([of_half(normed, half), of_half(values, half)])
        cross = across(cross_send, 6)
        side = across(own, 2)
        query_pair = along_z(pair_send)
        far = across(cross, 2)
        pieces = []
        for piece in (own, side, far, cross):
            pieces += [piece, across(piece, 1)]
        pieces = [p.reshape(2, 16, 128, 128) for p in pieces]
    with jax.named_scope("attend"):
        outs = attend(info, counts, lists, pieces, query_pair.reshape(16, 2, 2, 128, 128), gains)
    front, parts, query_row, key_row = outs[0], outs[1:9], outs[9], outs[10]
    with jax.named_scope("return"):
        far = wide_sum(parts[4], across(parts[5], 1))
        side = wide_sum(parts[2], across(parts[3], 1))
        front, far, side = lax.optimization_barrier((front, far, side))
        front = along_z(front.reshape(8, 2, 2, 256, HEAD_DIM))
        far = across(far, 2)
        side = across(side, 2)
        cross = across(wide_sum(parts[6], across(parts[7], 1), far), 6)
        core = across(parts[1], 1)
        shape = (2, 8, 256, HEAD_DIM)
        kv_grad = finish(mine, parts[0].reshape(shape), core.reshape(shape), side.reshape(shape), cross.reshape(shape), kv, key_gain)
        got = across(front[:, 1], 6)
        attended, query_grad = unpack_front(mine, front, got)
        key_grad, value_grad = unpack(along_z(kv_grad))
    with jax.named_scope("gains"):
        rows = over_copies(jnp.concatenate([query_row[0:1], key_row[0:1]]))
        other = across(rows, 4)
        rows = jnp.where(half == 0, jnp.stack([rows, other]), jnp.stack([other, rows]))
        turns = [rows] + [lax.ppermute(rows, "seq", [(i, (i + 8 * d) % 64) for i in range(64)]) for d in range(1, 8)]
        turns = jnp.stack(turns[::-1] + turns[::-1])
        turns = lax.dynamic_slice_in_dim(turns, 7 - plane, 8, 0).reshape(HEADS, 2, HEAD_DIM)
    return (attended[None], query_grad[None], key_grad[None], value_grad[None], turns[:, 0], turns[:, 1])


def solution(mesh):
    rows = P("dp", "seq", None)
    return jax.shard_map(
        body,
        mesh=mesh,
        in_specs=(rows, rows, rows, rows, P(), P(), P("dp", None, None, None), P("dp", None, None)),
        out_specs=(rows, rows, rows, rows, P(), P()),
        check_vma=False,
    )
```

time: 383 us -> 316 us (0.83)
  waiting for transfers between devices: 219 us -> 164 us
  starting transfers between devices: 76.7 us -> 52.6 us
  local copies, waits for them, and re-layouts: 15.2 us -> 21.7 us
  other arithmetic: 14.6 us -> 18.7 us
    ppermute x7, waiting for transfers between devices: 35 us -> 1.32 us  [body(): lax.ppermute(rows, 'seq', [(i, (i + 8 * d) % 64) for i in range(64)])]
    ppermute x17 -> x19, waiting for transfers between devices: 141 us -> 124 us  [across(): return lax.ppermute(array, 'seq', [(i, i ^ flip) for i in range(64)])]
    all_to_all x4, starting transfers between devices: 40.1 us -> 23.4 us  [along_z(): lax.all_to_all(array, 'seq', split_axis=0, concat_axis=0, axis_index_grou...]
    ppermute x4 -> x2, starting transfers between devices: 11.1 us -> 0.91 us  [over_copies(): row = row + lax.ppermute(row, 'dp', [(i, i ^ flip) for i in range(4)])]
    all_to_all x4, waiting for transfers between devices: 40.2 us -> 31.5 us  [along_z(): lax.all_to_all(array, 'seq', split_axis=0, concat_axis=0, axis_index_grou...]
    ppermute x4 -> x2, waiting for transfers between devices: 2.75 us -> 7.81 us  [over_copies(): row = row + lax.ppermute(row, 'dp', [(i, i ^ flip) for i in range(4)])]
    squeeze x3 -> x6, local copies, waits for them, and re-layouts: 0.63 us -> 5.4 us  [the longest x4 5.22 us: by_head(): return jnp.transpose(rows.reshape(256, 8, 2, HEAD_DIM), (1, 2, 0, 3))]
    unnamed x50 -> x58, local copies, waits for them, and re-layouts: 6.54 us -> 10.8 us
  transfers between devices with their start and end apart: 32 -> 32, of which waited for: 15 -> 16; matrix products, arithmetic and copies ran while one was open for 5% -> 9% of each run, Pallas kernels for 3% -> 4%
where the time goes in v3:
time: 316 us; the launch traced here: 315 us
  waiting for transfers between devices  164 us (52%)
  Pallas kernels  56.4 us (18%)
  starting transfers between devices  52.6 us (17%)
  local copies, waits for them, and re-layouts  21.7 us (7%)
  other arithmetic  18.7 us (6%)
    ppermute x19, waiting for transfers between devices, across(): return lax.ppermute(array, 'seq', [(i, i ^ flip) for i in range(64)])  124 us
    pallas_call x1, Pallas kernels, attend(): pl.pallas_call(attend_kernel, out_shape=(jax.ShapeDtypeStruct((16, 2, 2,...  41.4 us
    all_to_all x4, waiting for transfers between devices, along_z(): lax.all_to_all(array, 'seq', split_axis=0, concat_axis=0, axis_index_grou...  31.5 us
    all_to_all x4, starting transfers between devices, along_z(): lax.all_to_all(array, 'seq', split_axis=0, concat_axis=0, axis_index_grou...  23.4 us
    ppermute x7, starting transfers between devices, body(): lax.ppermute(rows, 'seq', [(i, (i + 8 * d) % 64) for i in range(64)])  16.2 us
    ppermute x19, starting transfers between devices, across(): return lax.ppermute(array, 'seq', [(i, i ^ flip) for i in range(64)])  12 us
    unnamed x58, local copies, waits for them, and re-layouts  10.8 us
    ppermute x2, waiting for transfers between devices, over_copies(): row = row + lax.ppermute(row, 'dp', [(i, i ^ flip) for i in range(4)])  7.81 us
  transfers between devices with their start and end apart: 32, of which 16 were waited for; matrix products, arithmetic and copies ran while one was open for 9% of the time, Pallas kernels for 4%

profile of v3, /device:TPU:16, one launch (start us, length us, event | category | flops | bytes accessed | tf_op | source)
XLA Modules:
  0.0 314.8 jit_solution(2207997927188035090)
XLA Ops:
  0.7 1.6 copy.42
  2.2 0.7 copy.43
  2.9 0.5 copy.44
  3.5 0.7 copy.45
  4.1 1.5 pad_maximum_fusion.1
  5.7 8.6 %all-to-all-start = ((bf16[8,2,2,256,128]{4,3,2,1,0:T(8,128)(2,1)}), bf16[8,2,2,256,128]{4,3,2,1,0:T(8,128)(2,1)S(1)}, u32[]{:S(2)}, u32[]{:S(2)}) async-start(bf16[8,2,2,256,128]{4,3,2,1,0:T(8,128)(2,1)} %pad_maximum_fusion.1), calls=%async_computation | async-start | bytes 4194304 | tf_op jit(solution)/shard_map/gather/all_to_all | solution.py:271
  14.3 1.3 copy.38
  15.6 1.6 copy.39
  17.2 2.3 copy.40
  19.5 2.3 copy.41
  21.7 2.3 broadcast_select_fusion.3
  24.1 1.1 pad_maximum_fusion.2
  25.1 2.8 collective-permute-start
  28.0 0.7 reshape.251.list_ref
  28.7 1.2 fusion.4.count_ref
  29.9 0.7 pad_add_fusion
  30.5 0.6 pad_maximum_fusion.6.refs_9_
  31.2 20.0 %collective-permute-done = bf16[8,2,256,128]{3,2,0,1:T(8,128)(2,1)} collective-permute-done((bf16[8,2,256,128]{3,2,0,1:T(8,128)(2,1)}, bf16[8,2,256,128]{3,2,0,1:T(8,128)(2,1)}, u32[]{:S(2)}, u32[]{:S(2)}) %collective-permute-start) | collective-permute-done | bytes 1048608 | tf_op jit(solution)/shard_map/gather/ppermute | solution.py:275
  51.3 2.8 pad_maximum_fusion
  54.0 11.4 %all-to-all-done.kv_ref = bf16[8,2,2,256,128]{4,3,2,1,0:T(8,128)(2,1)S(1)} async-done(((bf16[8,2,2,256,128]{4,3,2,1,0:T(8,128)(2,1)}), bf16[8,2,2,256,128]{4,3,2,1,0:T(8,128)(2,1)S(1)}, u32[]{:S(2)}, u32[]{:S(2)}) %all-to-all-start) | async-done | bytes 2097184 | tf_op jit(solution)/shard_map/gather/all_to_all | solution.py:271
  65.5 0.6 fusion
  66.2 1.6 copy-done.4
  67.8 1.5 copy.52
  69.3 4.3 %all-to-all-start.1 = ((bf16[8,2,2,256,128]{4,3,2,1,0:T(8,128)(2,1)}), bf16[8,2,2,256,128]{4,3,2,1,0:T(8,128)(2,1)}, u32[]{:S(2)}, u32[]{:S(2)}) async-start(bf16[8,2,2,256,128]{4,3,2,1,0:T(8,128)(2,1)} %copy.52), calls=%async_computation.1 | async-start | bytes 4194304 | tf_op jit(solution)/shard_map/gather/all_to_all | solution.py:271
  73.7 0.7 fusion.2
  74.7 2.8 collective-permute-start.4
  78.0 20.1 %collective-permute-done.4 = bf16[2,8,256,128]{3,2,1,0:T(8,128)(2,1)S(1)} collective-permute-done((bf16[2,8,256,128]{3,2,1,0:T(8,128)(2,1)S(1)}, bf16[2,8,256,128]{3,2,1,0:T(8,128)(2,1)S(1)}, u32[]{:S(2)}, u32[]{:S(2)}) %collective-permute-start.4) | collective-permute-done | bytes 1048608 | tf_op jit(solution)/shard_map/gather/ppermute | solution.py:275
  98.8 3.5 %collective-permute-done.2 = bf16[2,8,256,128]{3,2,1,0:T(8,128)(2,1)S(1)} collective-permute-done((bf16[2,8,256,128]{3,2,1,0:T(8,128)(2,1)S(1)}, bf16[2,8,256,128]{3,2,1,0:T(8,128)(2,1)S(1)}, u32[]{:S(2)}, u32[]{:S(2)}) %collective-permute-start.2) | collective-permute-done | bytes 1048608 | tf_op jit(solution)/shard_map/gather/ppermute | solution.py:275
  102.3 19.7 %collective-permute-done.5 = bf16[2,8,256,128]{3,2,1,0:T(8,128)(2,1)S(1)} collective-permute-done((bf16[2,8,256,128]{3,2,1,0:T(8,128)(2,1)S(1)}, bf16[2,8,256,128]{3,2,1,0:T(8,128)(2,1)S(1)}, u32[]{:S(2)}, u32[]{:S(2)}) %collective-permute-start.5) | collective-permute-done | bytes 1048608 | tf_op jit(solution)/shard_map/gather/ppermute | solution.py:275
  122.1 1.2 pad_maximum_fusion.3.refs_0_
  123.5 0.9 copy-done.17
  124.7 1.0 copy-done.18
  125.7 41.4 %attend.1 = (bf16[16,2,2,128,128]{4,3,2,1,0:T(8,128)(2,1)}, bf16[2,16,128,128]{3,2,1,0:T(8,128)(2,1)}, bf16[2,16,128,128]{3,2,1,0:T(8,128)(2,1)}, bf16[2,16,128,...) custom-call(s32[2]{0:T(128)} %get-tuple-element.32.info_ref, ...), custom_call_target="tpu_custom_call" | custom-call | flops 6000000000 | bytes 20971520 | tf_op jit(solution)/shard_map/attend/attend/pallas_call | solution.py:163
  167.7 2.4 collective-permute-done.8
  170.1 2.6 add_convert_fusion.2
  172.7 1.3 add_convert_fusion.1
  174.0 6.1 %all-to-all-start.2 = ((bf16[8,2,2,256,128]{4,3,2,1,0:T(8,128)(2,1)}), bf16[8,2,2,256,128]{4,3,2,1,0:T(8,128)(2,1)S(1)}, u32[]{:S(2)}, u32[]{:S(2)}) async-start(bf16[8,2,2,256,128]{4,3,2,1,0:T(8,128)(2,1)} %bitcast.116), calls=%async_computation.2 | async-start | bytes 4194304 | tf_op jit(solution)/shard_map/return/all_to_all | solution.py:271
  180.7 1.8 collective-permute-start.12
  182.4 0.6 collective-permute-done.13
  183.0 23.4 %collective-permute-done.14 = bf16[2,16,128,128]{3,2,1,0:T(8,128)(2,1)S(1)} collective-permute-done((bf16[2,16,128,128]{3,2,1,0:T(8,128)(2,1)}, bf16[2,16,128,128]{3,2,1,0:T(8,128)(2,1)S(1)}, u32[]{:S(2)}, u32[]{:S(2)}) %collective-permute-start.14) | collective-permute-done | bytes 1048608 | tf_op jit(solution)/shard_map/return/ppermute | solution.py:275
  206.4 2.7 add_convert_fusion
  209.6 0.7 slice.64
  210.3 0.7 slice.65
  211.4 3.1 collective-permute-done.16
  215.0 4.7 %collective-permute-done.17 = f32[2,128]{1,0:T(2,128)S(1)} collective-permute-done((f32[2,128]{1,0:T(2,128)S(1)}, f32[2,128]{1,0:T(2,128)S(1)}, u32[]{:S(2)}, u32[]{:S(2)}) %collective-permute-start.17) | collective-permute-done | bytes 1056 | tf_op jit(solution)/shard_map/gains/ppermute | solution.py:288
  219.8 1.1 collective-permute-done.18
  221.3 7.2 %collective-permute-done.19 = f32[2,128]{1,0:T(2,128)S(1)} collective-permute-done((f32[2,128]{1,0:T(2,128)S(1)}, f32[2,128]{1,0:T(2,128)S(1)}, u32[]{:S(2)}, u32[]{:S(2)}) %collective-permute-start.19) | collective-permute-done | bytes 1056 | tf_op jit(solution)/shard_map/gains/ppermute | solution.py:275
  228.5 0.9 collective-permute-start.20
  229.4 4.2 %collective-permute-done.20 = f32[2,128]{1,0:T(2,128)S(1)} collective-permute-done((f32[2,128]{1,0:T(2,128)S(1)}, f32[2,128]{1,0:T(2,128)S(1)}, u32[]{:S(2)}, u32[]{:S(2)}) %collective-permute-start.20) | collective-permute-done | bytes 1056 | tf_op jit(solution)/shard_map/gains/ppermute | solution.py:275
  233.6 3.2 %collective-permute-start.21 = (f32[2,2,128]{2,1,0:T(2,128)S(1)}, f32[2,2,128]{2,1,0:T(2,128)S(1)}, u32[]{:S(2)}, u32[]{:S(2)}) collective-permute-start(f32[2,2,128]{2,1,0:T(2,128)S(1)} %maximum_select_fusion), channel_id=1, source_target_pairs={{0,56},{1,57},{2,58},{3,59},{4,60},{5,61},{6,62},{7,63},{8,0},{9,1... | collective-permute-start | bytes 6152 | tf_op jit(solution)/shard_map/gains/ppermute | solution.py:354
  236.8 1.3 collective-permute-done.21
  238.1 3.2 %collective-permute-start.22 = (f32[2,2,128]{2,1,0:T(2,128)S(1)}, f32[2,2,128]{2,1,0:T(2,128)S(1)}, u32[]{:S(2)}, u32[]{:S(2)}) collective-permute-start(f32[2,2,128]{2,1,0:T(2,128)S(1)} %maximum_select_fusion), channel_id=1, source_target_pairs={{0,48},{1,49},{2,50},{3,51},{4,52},{5,53},{6,54},{7,55},{8,56},{9,... | collective-permute-start | bytes 6152 | tf_op jit(solution)/shard_map/gains/ppermute | solution.py:354
  241.4 5.0 %collective-permute-start.25 = (f32[2,2,128]{2,1,0:T(2,128)S(1)}, f32[2,2,128]{2,1,0:T(2,128)S(1)}, u32[]{:S(2)}, u32[]{:S(2)}) collective-permute-start(f32[2,2,128]{2,1,0:T(2,128)S(1)} %maximum_select_fusion), channel_id=1, source_target_pairs={{0,24},{1,25},{2,26},{3,27},{4,28},{5,29},{6,30},{7,31},{8,32},{9,... | collective-permute-start | bytes 6152 | tf_op jit(solution)/shard_map/gains/ppermute | solution.py:354
  246.4 2.7 collective-permute-start.24
  249.1 7.3 %finish.1 = bf16[8,2,2,256,128]{4,3,2,1,0:T(8,128)(2,1)} custom-call(s32[2]{0:T(128)} %get-tuple-element.31.mine_ref, bf16[2,8,256,128]{3,2,1,0:T(8,128)(2,1)} %bitcast.118, bf16[2,8,256,128]{3,2,1,0:T(8,128)(2,1)} %bitcast.119, bf16[2,8,256,128]{3,2,1,0:T(8,128)(2,1)} %bitcast.43.side_ref, bf16[2,8,256,128]{3,2,1,0:T(8,128)(2,1)} %bitcast.44.far_ref, ...), custom_call_target="tpu_custom_call" | custom-call | tf_op jit(solution)/shard_map/return/finish/pallas_call | solution.py:210
  256.3 2.1 collective-permute-start.23
  258.4 4.4 %all-to-all-start.3 = ((bf16[8,2,2,256,128]{4,3,2,1,0:T(8,128)(2,1)}), bf16[8,2,2,256,128]{4,3,2,1,0:T(8,128)(2,1)}, u32[]{:S(2)}, u32[]{:S(2)}) async-start(bf16[8,2,2,256,128]{4,3,2,1,0:T(8,128)(2,1)} %finish.1), calls=%async_computation.3 | async-start | bytes 4194304 | tf_op jit(solution)/shard_map/return/all_to_all | solution.py:271
  263.1 0.6 collective-permute-start.10
  263.7 0.6 slice_bitcast_fusion.3
  264.4 21.5 %collective-permute-done.10.got_ref = bf16[8,2,256,128]{3,2,1,0:T(8,128)(2,1)S(1)} collective-permute-done((bf16[8,2,256,128]{3,2,1,0:T(8,128)(2,1)S(1)}, bf16[8,2,256,128]{3,2,1,0:T(8,128)(2,1)S(1)}, u32[]{:S(2)}, u32[]{:S(2)}) %collective-permute-start.10) | collective-permute-done | bytes 1048608 | tf_op jit(solution)/shard_map/return/ppermute | solution.py:275
  285.9 1.0 copy-done.11
  286.9 3.9 %unpack_front.1 = (bf16[256,2048]{1,0:T(8,128)(2,1)}, bf16[256,2048]{1,0:T(8,128)(2,1)}) custom-call(s32[2]{0:T(128)} %get-tuple-element.31.mine_ref, bf16[8,2,2,256,128]{4,3,2,1,0:T(8,128)(2,1)} %copy-done.3, bf16[8,2,256,128]{3,2,1,0:T(8,128)(2,1)} %copy-done.11), custom_call_target="tpu_custom_call" | custom-call | bytes 4194304 | tf_op jit(solution)/shard_map/return/unpack_front/pallas_call | solution.py:255
  290.7 20.1 %all-to-all-done.3.in_ref = bf16[8,2,2,256,128]{4,3,2,1,0:T(8,128)(2,1)} async-done(((bf16[8,2,2,256,128]{4,3,2,1,0:T(8,128)(2,1)}), bf16[8,2,2,256,128]{4,3,2,1,0:T(8,128)(2,1)}, u32[]{:S(2)}, u32[]{:S(2)}) %all-to-all-start.3) | async-done | bytes 2097184 | tf_op jit(solution)/shard_map/return/all_to_all | solution.py:271
  310.9 3.9 %unpack.1 = (bf16[256,2048]{1,0:T(8,128)(2,1)}, bf16[256,2048]{1,0:T(8,128)(2,1)}) custom-call(bf16[8,2,2,256,128]{4,3,2,1,0:T(8,128)(2,1)} %all-to-all-done.3.in_ref), custom_call_target="tpu_custom_call" | custom-call | bytes 4194304 | tf_op jit(solution)/shard_map/return/unpack/pallas_call | solution.py:232
  (107 shorter events, 5.6 us)
Async XLA Ops:
  0.6 27.2 %copy-start = (s32[1,16,128,8]{2,3,1,0:T(8,128)S(1)}, s32[1,16,128,8]{2,3,1,0:T(8,128)}, u32[]{:S(2)}) copy-start(s32[1,16,128,8]{2,3,1,0:T(8,128)} %param.14) | copy-start | bytes 196612
  0.6 2.3 copy-start.9
  5.7 8.6 %copy-start.10 = (bf16[1,256,2048]{2,1,0:T(8,128)(2,1)S(1)}, bf16[1,256,2048]{2,1,0:T(8,128)(2,1)}, u32[]{:S(2)}) copy-start(bf16[1,256,2048]{2,1,0:T(8,128)(2,1)} %param.8) | copy-start | bytes 3145732
  5.7 59.8 %all-to-all-start = ((bf16[8,2,2,256,128]{4,3,2,1,0:T(8,128)(2,1)}), bf16[8,2,2,256,128]{4,3,2,1,0:T(8,128)(2,1)S(1)}, u32[]{:S(2)}, u32[]{:S(2)}) async-start(bf16[8,2,2,256,128]{4,3,2,1,0:T(8,128)(2,1)} %pad_maximum_fusion.1), calls=%async_computation | async-start | bytes 4194304 | tf_op jit(solution)/shard_map/gather/all_to_all | solution.py:271
  24.0 5.8 %copy-start.12 = (f32[16,128]{1,0:T(8,128)S(1)}, f32[16,128]{1,0:T(8,128)}, u32[]{:S(2)}) copy-start(f32[16,128]{1,0:T(8,128)} %gain_ref.1) | copy-start | bytes 24580
  24.0 6.5 %copy-start.13 = (f32[16,128]{1,0:T(8,128)S(1)}, f32[16,128]{1,0:T(8,128)}, u32[]{:S(2)}) copy-start(f32[16,128]{1,0:T(8,128)} %param.12) | copy-start | bytes 24580
  24.0 7.1 %copy-start.5 = (bf16[8,1,256,128]{3,2,0,1:T(8,128)(2,1)S(1)}, bf16[8,1,256,128]{3,2,0,1:T(8,128)(2,1)}, u32[]{:S(2)}) copy-start(bf16[8,1,256,128]{3,2,0,1:T(8,128)(2,1)} %get-tuple-element.60) | copy-start | bytes 1572868
  24.0 7.1 %copy-start.6 = (bf16[8,1,256,128]{3,2,0,1:T(8,128)(2,1)S(1)}, bf16[8,1,256,128]{3,2,0,1:T(8,128)(2,1)}, u32[]{:S(2)}) copy-start(bf16[8,1,256,128]{3,2,0,1:T(8,128)(2,1)} %get-tuple-element.67) | copy-start | bytes 1572868
  25.1 26.1 %collective-permute-start = (bf16[8,2,256,128]{3,2,0,1:T(8,128)(2,1)}, bf16[8,2,256,128]{3,2,0,1:T(8,128)(2,1)}, u32[]{:S(2)}, u32[]{:S(2)}) collective-permute-start(bf16[8,2,256,128]{3,2,0,1:T(8,128)(2,1)} %pad_maximum_fusion.2), channel_id=1, source_target_pairs={{0,6},{1,7},{2,4},{3,5},{4,2},{5,3},{6,0},{7,1},{8,14},{9,15},{10,... | collective-permute-start | bytes 3145736 | tf_op jit(solution)/shard_map/gather/ppermute | solution.py:275
  65.5 8.2 %copy-start.2 = (bf16[8,2,2,256,128]{4,3,2,1,0:T(8,128)(2,1)}, bf16[8,2,2,256,128]{4,3,2,1,0:T(8,128)(2,1)S(1)}, u32[]{:S(2)}) copy-start(bf16[8,2,2,256,128]{4,3,2,1,0:T(8,128)(2,1)S(1)} %all-to-all-done.kv_ref) | copy-start | bytes 6291460
  65.5 2.3 copy-start.4
  69.3 56.4 %all-to-all-start.1 = ((bf16[8,2,2,256,128]{4,3,2,1,0:T(8,128)(2,1)}), bf16[8,2,2,256,128]{4,3,2,1,0:T(8,128)(2,1)}, u32[]{:S(2)}, u32[]{:S(2)}) async-start(bf16[8,2,2,256,128]{4,3,2,1,0:T(8,128)(2,1)} %copy.52), calls=%async_computation.1 | async-start | bytes 4194304 | tf_op jit(solution)/shard_map/gather/all_to_all | solution.py:271
  74.7 23.4 %collective-permute-start.4 = (bf16[2,8,256,128]{3,2,1,0:T(8,128)(2,1)S(1)}, bf16[2,8,256,128]{3,2,1,0:T(8,128)(2,1)S(1)}, u32[]{:S(2)}, u32[]{:S(2)}) collective-permute-start(bf16[2,8,256,128]{3,2,1,0:T(8,128)(2,1)S(1)} %pad_maximum_fusion.5), channel_id=1, source_target_pairs={{0,6},{1,7},{2,4},{3,5},{4,2},{5,3},{6,0},{7,1},{8,14},{9,15},{10,... | collective-permute-start | bytes 3145736 | tf_op jit(solution)/shard_map/gather/ppermute | solution.py:275
  77.7 24.7 %collective-permute-start.2 = (bf16[2,8,256,128]{3,2,1,0:T(8,128)(2,1)S(1)}, bf16[2,8,256,128]{3,2,1,0:T(8,128)(2,1)S(1)}, u32[]{:S(2)}, u32[]{:S(2)}) collective-permute-start(bf16[2,8,256,128]{3,2,1,0:T(8,128)(2,1)S(1)} %pad_maximum_fusion.4), channel_id=1, source_target_pairs={{0,2},{1,3},{2,0},{3,1},{4,6},{5,7},{6,4},{7,5},{8,10},{9,11},{10,... | collective-permute-start | bytes 3145736 | tf_op jit(solution)/shard_map/gather/ppermute | solution.py:275
  98.1 27.7 %copy-start.14 = (bf16[2,8,256,128]{3,2,1,0:T(8,128)(2,1)}, bf16[2,8,256,128]{3,2,1,0:T(8,128)(2,1)S(1)}, u32[]{:S(2)}) copy-start(bf16[2,8,256,128]{3,2,1,0:T(8,128)(2,1)S(1)} %collective-permute-done.4) | copy-start | bytes 3145732
  98.1 24.0 %collective-permute-start.5 = (bf16[2,8,256,128]{3,2,1,0:T(8,128)(2,1)S(1)}, bf16[2,8,256,128]{3,2,1,0:T(8,128)(2,1)S(1)}, u32[]{:S(2)}, u32[]{:S(2)}) collective-permute-start(bf16[2,8,256,128]{3,2,1,0:T(8,128)(2,1)S(1)} %collective-permute-done.4), channel_id=1, source_target_pairs={{0,2},{1,3},{2,0},{3,1},{4,6},{5,7},{6,4},{7,5},{8,10},{9,11},{10,... | collective-permute-start | bytes 3145736 | tf_op jit(solution)/shard_map/gather/ppermute | solution.py:275
  98.3 25.0 %collective-permute-start.1 = (bf16[2,8,256,128]{3,2,1,0:T(8,128)(2,1)S(1)}, bf16[2,8,256,128]{3,2,1,0:T(8,128)(2,1)S(1)}, u32[]{:S(2)}, u32[]{:S(2)}) collective-permute-start(bf16[2,8,256,128]{3,2,1,0:T(8,128)(2,1)S(1)} %pad_maximum_fusion.4), channel_id=1, source_target_pairs={{0,1},{1,0},{2,3},{3,2},{4,5},{5,4},{6,7},{7,6},{8,9},{9,8},{10,11... | collective-permute-start | bytes 3145736 | tf_op jit(solution)/shard_map/gather/ppermute | solution.py:275
  98.3 25.0 %collective-permute-start.7 = (bf16[2,8,256,128]{3,2,1,0:T(8,128)(2,1)S(1)}, bf16[2,8,256,128]{3,2,1,0:T(8,128)(2,1)S(1)}, u32[]{:S(2)}, u32[]{:S(2)}) collective-permute-start(bf16[2,8,256,128]{3,2,1,0:T(8,128)(2,1)S(1)} %collective-permute-done.4), channel_id=1, source_target_pairs={{0,1},{1,0},{2,3},{3,2},{4,5},{5,4},{6,7},{7,6},{8,9},{9,8},{10,11... | collective-permute-start | bytes 3145736 | tf_op jit(solution)/shard_map/gather/ppermute | solution.py:275
  102.3 23.4 %copy-start.15 = (bf16[2,8,256,128]{3,2,1,0:T(8,128)(2,1)}, bf16[2,8,256,128]{3,2,1,0:T(8,128)(2,1)S(1)}, u32[]{:S(2)}) copy-start(bf16[2,8,256,128]{3,2,1,0:T(8,128)(2,1)S(1)} %collective-permute-done.2) | copy-start | bytes 3145732
  102.3 21.0 %collective-permute-start.3 = (bf16[2,8,256,128]{3,2,1,0:T(8,128)(2,1)S(1)}, bf16[2,8,256,128]{3,2,1,0:T(8,128)(2,1)S(1)}, u32[]{:S(2)}, u32[]{:S(2)}) collective-permute-start(bf16[2,8,256,128]{3,2,1,0:T(8,128)(2,1)S(1)} %collective-permute-done.2), channel_id=1, source_target_pairs={{0,1},{1,0},{2,3},{3,2},{4,5},{5,4},{6,7},{7,6},{8,9},{9,8},{10,11... | collective-permute-start | bytes 3145736 | tf_op jit(solution)/shard_map/gather/ppermute | solution.py:275
  122.0 1.4 copy-start.16
  122.0 3.7 %collective-permute-start.6 = (bf16[2,8,256,128]{3,2,1,0:T(8,128)(2,1)S(1)}, bf16[2,8,256,128]{3,2,1,0:T(8,128)(2,1)}, u32[]{:S(2)}, u32[]{:S(2)}) collective-permute-start(bf16[2,8,256,128]{3,2,1,0:T(8,128)(2,1)S(1)} %collective-permute-done.5), channel_id=1, source_target_pairs={{0,1},{1,0},{2,3},{3,2},{4,5},{5,4},{6,7},{7,6},{8,9},{9,8},{10,11... | collective-permute-start | bytes 3145736 | tf_op jit(solution)/shard_map/gather/ppermute | solution.py:275
  123.3 1.0 copy-start.17
  123.4 1.3 copy-start.19
  124.7 1.0 copy-start.18
  167.1 5.5 %copy-start.8 = (bf16[2,16,128,128]{3,2,1,0:T(8,128)(2,1)S(1)}, bf16[2,16,128,128]{3,2,1,0:T(8,128)(2,1)}, u32[]{:S(2)}) copy-start(bf16[2,16,128,128]{3,2,1,0:T(8,128)(2,1)} %get-tuple-element.41) | copy-start | bytes 3145732
  167.1 3.0 collective-permute-start.8
  167.2 5.4 %collective-permute-start.9 = (bf16[2,16,128,128]{3,2,1,0:T(8,128)(2,1)}, bf16[2,16,128,128]{3,2,1,0:T(8,128)(2,1)S(1)}, u32[]{:S(2)}, u32[]{:S(2)}) collective-permute-start(bf16[2,16,128,128]{3,2,1,0:T(8,128)(2,1)} %get-tuple-element.42), channel_id=1, source_target_pairs={{0,1},{1,0},{2,3},{3,2},{4,5},{5,4},{6,7},{7,6},{8,9},{9,8},{10,11... | collective-permute-start | bytes 3145736 | tf_op jit(solution)/shard_map/return/ppermute | solution.py:275
  174.0 84.4 %all-to-all-start.2 = ((bf16[8,2,2,256,128]{4,3,2,1,0:T(8,128)(2,1)}), bf16[8,2,2,256,128]{4,3,2,1,0:T(8,128)(2,1)S(1)}, u32[]{:S(2)}, u32[]{:S(2)}) async-start(bf16[8,2,2,256,128]{4,3,2,1,0:T(8,128)(2,1)} %bitcast.116), calls=%async_computation.2 | async-start | bytes 4194304 | tf_op jit(solution)/shard_map/return/all_to_all | solution.py:271
  180.1 2.9 collective-permute-start.13
  180.2 26.3 %collective-permute-start.14 = (bf16[2,16,128,128]{3,2,1,0:T(8,128)(2,1)}, bf16[2,16,128,128]{3,2,1,0:T(8,128)(2,1)S(1)}, u32[]{:S(2)}, u32[]{:S(2)}) collective-permute-start(bf16[2,16,128,128]{3,2,1,0:T(8,128)(2,1)} %add_convert_fusion.2), channel_id=1, source_target_pairs={{0,2},{1,3},{2,0},{3,1},{4,6},{5,7},{6,4},{7,5},{8,10},{9,11},{10,... | collective-permute-start | bytes 3145736 | tf_op jit(solution)/shard_map/return/ppermute | solution.py:275
  180.3 61.1 %collective-permute-start.11 = (bf16[2,16,128,128]{3,2,1,0:T(8,128)(2,1)}, bf16[2,16,128,128]{3,2,1,0:T(8,128)(2,1)S(1)}, u32[]{:S(2)}, u32[]{:S(2)}) collective-permute-start(bf16[2,16,128,128]{3,2,1,0:T(8,128)(2,1)} %get-tuple-element.47), channel_id=1, source_target_pairs={{0,1},{1,0},{2,3},{3,2},{4,5},{5,4},{6,7},{7,6},{8,9},{9,8},{10,11... | collective-permute-start | bytes 3145736 | tf_op jit(solution)/shard_map/return/ppermute | solution.py:275
  180.7 60.7 %collective-permute-start.12 = (bf16[2,16,128,128]{3,2,1,0:T(8,128)(2,1)}, bf16[2,16,128,128]{3,2,1,0:T(8,128)(2,1)}, u32[]{:S(2)}, u32[]{:S(2)}) collective-permute-start(bf16[2,16,128,128]{3,2,1,0:T(8,128)(2,1)} %add_convert_fusion.1), channel_id=1, source_target_pairs={{0,2},{1,3},{2,0},{3,1},{4,6},{5,7},{6,4},{7,5},{8,10},{9,11},{10,... | collective-permute-start | bytes 3145736 | tf_op jit(solution)/shard_map/return/ppermute | solution.py:275
  209.1 37.3 %collective-permute-start.15 = (bf16[2,16,128,128]{3,2,1,0:T(8,128)(2,1)}, bf16[2,16,128,128]{3,2,1,0:T(8,128)(2,1)}, u32[]{:S(2)}, u32[]{:S(2)}) collective-permute-start(bf16[2,16,128,128]{3,2,1,0:T(8,128)(2,1)} %add_convert_fusion), channel_id=1, source_target_pairs={{0,6},{1,7},{2,4},{3,5},{4,2},{5,3},{6,0},{7,1},{8,14},{9,15},{10,... | collective-permute-start | bytes 3145736 | tf_op jit(solution)/shard_map/return/ppermute | solution.py:275
  211.0 3.6 %collective-permute-start.16 = (f32[2,128]{1,0:T(2,128)S(1)}, f32[2,128]{1,0:T(2,128)S(1)}, u32[]{:S(2)}, u32[]{:S(2)}) collective-permute-start(f32[2,128]{1,0:T(2,128)S(1)} %pad_maximum_fusion.7), channel_id=1, source_target_pairs={{0,64},{64,0},{128,192},{192,128},{1,65},{65,1},{129,193},{193,129... | collective-permute-start | bytes 3080 | tf_op jit(solution)/shard_map/gains/ppermute | solution.py:288
  214.5 5.2 %collective-permute-start.17 = (f32[2,128]{1,0:T(2,128)S(1)}, f32[2,128]{1,0:T(2,128)S(1)}, u32[]{:S(2)}, u32[]{:S(2)}) collective-permute-start(f32[2,128]{1,0:T(2,128)S(1)} %fusion.5), channel_id=1, source_target_pairs={{0,128},{64,192},{128,0},{192,64},{1,129},{65,193},{129,1},{193,65... | collective-permute-start | bytes 3080 | tf_op jit(solution)/shard_map/gains/ppermute | solution.py:288
  219.7 1.2 collective-permute-start.18
  220.9 7.6 %collective-permute-start.19 = (f32[2,128]{1,0:T(2,128)S(1)}, f32[2,128]{1,0:T(2,128)S(1)}, u32[]{:S(2)}, u32[]{:S(2)}) collective-permute-start(f32[2,128]{1,0:T(2,128)S(1)} %add.67), channel_id=1, source_target_pairs={{0,2},{1,3},{2,0},{3,1},{4,6},{5,7},{6,4},{7,5},{8,10},{9,11},{10,... | collective-permute-start | bytes 3080 | tf_op jit(solution)/shard_map/gains/ppermute | solution.py:275
  228.5 5.1 %collective-permute-start.20 = (f32[2,128]{1,0:T(2,128)S(1)}, f32[2,128]{1,0:T(2,128)S(1)}, u32[]{:S(2)}, u32[]{:S(2)}) collective-permute-start(f32[2,128]{1,0:T(2,128)S(1)} %add.68), channel_id=1, source_target_pairs={{0,4},{1,5},{2,6},{3,7},{4,0},{5,1},{6,2},{7,3},{8,12},{9,13},{10,... | collective-permute-start | bytes 3080 | tf_op jit(solution)/shard_map/gains/ppermute | solution.py:275
  233.6 4.5 %collective-permute-start.21 = (f32[2,2,128]{2,1,0:T(2,128)S(1)}, f32[2,2,128]{2,1,0:T(2,128)S(1)}, u32[]{:S(2)}, u32[]{:S(2)}) collective-permute-start(f32[2,2,128]{2,1,0:T(2,128)S(1)} %maximum_select_fusion), channel_id=1, source_target_pairs={{0,56},{1,57},{2,58},{3,59},{4,60},{5,61},{6,62},{7,63},{8,0},{9,1... | collective-permute-start | bytes 6152 | tf_op jit(solution)/shard_map/gains/ppermute | solution.py:354
  236.8 26.1 %collective-permute-start.27 = (f32[2,2,128]{2,1,0:T(2,128)S(1)}, f32[2,2,128]{2,1,0:T(2,128)S(1)}, u32[]{:S(2)}, u32[]{:S(2)}) collective-permute-start(f32[2,2,128]{2,1,0:T(2,128)S(1)} %maximum_select_fusion), channel_id=1, source_target_pairs={{0,8},{1,9},{2,10},{3,11},{4,12},{5,13},{6,14},{7,15},{8,16},{9,17... | collective-permute-start | bytes 6152 | tf_op jit(solution)/shard_map/gains/ppermute | solution.py:354
  238.1 18.2 %collective-permute-start.22 = (f32[2,2,128]{2,1,0:T(2,128)S(1)}, f32[2,2,128]{2,1,0:T(2,128)S(1)}, u32[]{:S(2)}, u32[]{:S(2)}) collective-permute-start(f32[2,2,128]{2,1,0:T(2,128)S(1)} %maximum_select_fusion), channel_id=1, source_target_pairs={{0,48},{1,49},{2,50},{3,51},{4,52},{5,53},{6,54},{7,55},{8,56},{9,... | collective-permute-start | bytes 6152 | tf_op jit(solution)/shard_map/gains/ppermute | solution.py:354
  241.3 7.7 %copy-start.7 = (bf16[2,16,128,128]{3,2,1,0:T(8,128)(2,1)}, bf16[2,16,128,128]{3,2,1,0:T(8,128)(2,1)S(1)}, u32[]{:S(2)}) copy-start(bf16[2,16,128,128]{3,2,1,0:T(8,128)(2,1)S(1)} %collective-permute-done.11) | copy-start | bytes 3145732
  241.3 21.6 %collective-permute-start.26 = (f32[2,2,128]{2,1,0:T(2,128)S(1)}, f32[2,2,128]{2,1,0:T(2,128)S(1)}, u32[]{:S(2)}, u32[]{:S(2)}) collective-permute-start(f32[2,2,128]{2,1,0:T(2,128)S(1)} %maximum_select_fusion), channel_id=1, source_target_pairs={{0,16},{1,17},{2,18},{3,19},{4,20},{5,21},{6,22},{7,23},{8,24},{9,... | collective-permute-start | bytes 6152 | tf_op jit(solution)/shard_map/gains/ppermute | solution.py:354
  241.4 21.5 %collective-permute-start.25 = (f32[2,2,128]{2,1,0:T(2,128)S(1)}, f32[2,2,128]{2,1,0:T(2,128)S(1)}, u32[]{:S(2)}, u32[]{:S(2)}) collective-permute-start(f32[2,2,128]{2,1,0:T(2,128)S(1)} %maximum_select_fusion), channel_id=1, source_target_pairs={{0,24},{1,25},{2,26},{3,27},{4,28},{5,29},{6,30},{7,31},{8,32},{9,... | collective-permute-start | bytes 6152 | tf_op jit(solution)/shard_map/gains/ppermute | solution.py:354
  246.4 16.5 %collective-permute-start.24 = (f32[2,2,128]{2,1,0:T(2,128)S(1)}, f32[2,2,128]{2,1,0:T(2,128)S(1)}, u32[]{:S(2)}, u32[]{:S(2)}) collective-permute-start(f32[2,2,128]{2,1,0:T(2,128)S(1)} %maximum_select_fusion), channel_id=1, source_target_pairs={{0,32},{1,33},{2,34},{3,35},{4,36},{5,37},{6,38},{7,39},{8,40},{9,... | collective-permute-start | bytes 6152 | tf_op jit(solution)/shard_map/gains/ppermute | solution.py:354
  256.3 6.5 %collective-permute-start.23 = (f32[2,2,128]{2,1,0:T(2,128)S(1)}, f32[2,2,128]{2,1,0:T(2,128)S(1)}, u32[]{:S(2)}, u32[]{:S(2)}) collective-permute-start(f32[2,2,128]{2,1,0:T(2,128)S(1)} %maximum_select_fusion), channel_id=1, source_target_pairs={{0,40},{1,41},{2,42},{3,43},{4,44},{5,45},{6,46},{7,47},{8,48},{9,... | collective-permute-start | bytes 6152 | tf_op jit(solution)/shard_map/gains/ppermute | solution.py:354
  258.4 4.6 %copy-start.3 = (bf16[8,2,2,256,128]{4,3,2,1,0:T(8,128)(2,1)}, bf16[8,2,2,256,128]{4,3,2,1,0:T(8,128)(2,1)S(1)}, u32[]{:S(2)}) copy-start(bf16[8,2,2,256,128]{4,3,2,1,0:T(8,128)(2,1)S(1)} %all-to-all-done.2.in_ref) | copy-start | bytes 6291460
  258.4 52.4 %all-to-all-start.3 = ((bf16[8,2,2,256,128]{4,3,2,1,0:T(8,128)(2,1)}), bf16[8,2,2,256,128]{4,3,2,1,0:T(8,128)(2,1)}, u32[]{:S(2)}, u32[]{:S(2)}) async-start(bf16[8,2,2,256,128]{4,3,2,1,0:T(8,128)(2,1)} %finish.1), calls=%async_computation.3 | async-start | bytes 4194304 | tf_op jit(solution)/shard_map/return/all_to_all | solution.py:271
  263.1 22.8 %collective-permute-start.10 = (bf16[8,2,256,128]{3,2,1,0:T(8,128)(2,1)S(1)}, bf16[8,2,256,128]{3,2,1,0:T(8,128)(2,1)S(1)}, u32[]{:S(2)}, u32[]{:S(2)}) collective-permute-start(bf16[8,2,256,128]{3,2,1,0:T(8,128)(2,1)S(1)} %slice_bitcast_fusion), channel_id=1, source_target_pairs={{0,6},{1,7},{2,4},{3,5},{4,2},{5,3},{6,0},{7,1},{8,14},{9,15},{10,... | collective-permute-start | bytes 3145736 | tf_op jit(solution)/shard_map/return/ppermute | solution.py:275
  263.7 51.0 %copy-start.1 = (s32[1,16,128,8]{2,3,1,0:T(8,128)S(1)}, s32[1,16,128,8]{2,3,1,0:T(8,128)}, u32[]{:S(2)}) copy-start(s32[1,16,128,8]{2,3,1,0:T(8,128)} %param.14) | copy-start | bytes 196612
  285.9 1.0 copy-start.11

commit v4 on v3

--- a/solution.py
+++ b/solution.py
@@ -27,9 +27,9 @@
 
 def attend_kernel(info_ref, count_ref, list_ref, *refs):
     pieces = refs[:8]
-    qg_hbm, gains_ref, og_hbm = refs[8:11]
-    parts = refs[11:19]
-    gain_query_ref, gain_key_ref, ktab, vtab, acc, qg_ref, og_ref, stage, order_ref, in_sems, out_sems = refs[19:]
+    qg_hbm, query_gain_ref, key_gain_ref, og_hbm = refs[8:12]
+    parts = refs[12:20]
+    gain_query_ref, gain_key_ref, ktab, vtab, acc, qg_ref, og_ref, stage, order_ref, in_sems, out_sems = refs[20:]
     place_x_core = info_ref[0]
     head = info_ref[1]
     copies = [pltpu.make_async_copy(qg_hbm, qg_ref, in_sems.at[16])]
@@ -65,8 +65,8 @@
     def _(t):
         acc[t] = jnp.zeros((128, 256), jnp.float32)
 
-    gain_query = gains_ref[pl.ds(head, 1), :]
-    gain_key = gains_ref[pl.ds(16 + head, 1), :]
+    gain_query = query_gain_ref[pl.ds(head, 1), :]
+    gain_key = key_gain_ref[pl.ds(head, 1), :]
     gain_query_ref[...] = jnp.zeros_like(gain_query_ref)
     gain_key_ref[...] = jnp.zeros_like(gain_key_ref)
     for copy in copies:
@@ -154,7 +154,7 @@
         copy.wait()
 
 
-def attend(info, counts, lists, pieces, qg, gains):
+def attend(info, counts, lists, pieces, qg, query_gain, key_gain):
     smem = pl.BlockSpec(memory_space=pltpu.SMEM)
     vmem = pl.BlockSpec(memory_space=pltpu.VMEM)
     hbm = pl.BlockSpec(memory_space=pl.ANY)
@@ -163,7 +163,7 @@
     return pl.pallas_call(
         attend_kernel,
         out_shape=(jax.ShapeDtypeStruct((16, 2, 2, 128, 128), jnp.bfloat16),) + (part,) * 8 + (row, row),
-        in_specs=[smem] * 3 + [hbm] * 9 + [vmem],
+        in_specs=[smem] * 3 + [hbm] * 9 + [vmem] * 2,
         out_specs=(hbm,) * 9 + (vmem,) * 2,
         scratch_shapes=[
             pltpu.VMEM((128, 128, 128), jnp.bfloat16),
@@ -179,104 +179,197 @@
         compiler_params=pltpu.CompilerParams(vmem_limit_bytes=56 * 1024 * 1024),
         cost_estimate=pl.CostEstimate(flops=6 * 10**9, bytes_accessed=20 * 2**20, transcendentals=4 * 2**20),
         name="attend",
-    )(info, counts, lists, *pieces, qg, gains)
+    )(info, counts, lists, *pieces, qg, query_gain, key_gain)
 
 
 HEADS = 16
 ALONG_Z = [[8 * z + rest for z in range(8)] for rest in range(8)]
-
-
-def finish_kernel(mine_ref, part_ref, core_ref, side_ref, far_ref, kv_ref, gain_ref, out_ref):
+ROWS = jax.ShapeDtypeStruct((256, HEADS * HEAD_DIM), jnp.bfloat16)
+PAIRS = jax.ShapeDtypeStruct((8, 2, 2, 256, HEAD_DIM), jnp.bfloat16)
+HALF_PAIRS = jax.ShapeDtypeStruct((8, 2, 256, HEAD_DIM), jnp.bfloat16)
+
+
+def columns(head):
+    if isinstance(head, int):
+        return pl.ds(head * HEAD_DIM, HEAD_DIM)
+    return pl.ds(pl.multiple_of(head * HEAD_DIM, HEAD_DIM), HEAD_DIM)
+
+
+def staged(groups, in_sems, out_sems):
+    loads, stores = [], []
+    for ins, _ in groups:
+        made = [pltpu.make_async_copy(a, b, in_sems.at[sum(map(len, loads)) + i]) for i, (a, b) in enumerate(ins)]
+        loads.append(made)
+    for made in loads:
+        for copy in made:
+            copy.start()
+    for made, (_, outs) in zip(loads, groups):
+        for copy in made:
+            copy.wait()
+        for a, b in outs:
+            stores.append(pltpu.make_async_copy(a, b, out_sems.at[len(stores)]))
+            stores[-1].start()
+    for copy in stores:
+        copy.wait()
+
+
+def pack_kernel(a_ref, b_ref, out_ref, buf, in_sems, out_sems):
+    staged([([(ref.at[:, columns(2 * z + hh)], buf.at[z, hh, i])
+              for hh in range(2) for i, ref in enumerate((a_ref, b_ref))], [(buf.at[z], out_ref.at[z])])
+            for z in range(8)], in_sems, out_sems)
+
+
+def give_kernel(mine_ref, a_ref, b_ref, out_ref, buf, in_sems, out_sems):
+    staged([([(ref.at[:, columns(2 * z + 1 - mine_ref[0])], buf.at[z, i]) for i, ref in enumerate((a_ref, b_ref))],
+             [(buf.at[z], out_ref.at[z])]) for z in range(8)], in_sems, out_sems)
+
+
+def pack_pair_kernel(mine_ref, a_ref, b_ref, got_ref, out_ref, buf, in_sems, out_sems):
+    staged([([(got_ref.at[z], buf.at[z, 1])]
+             + [(ref.at[:, columns(2 * z + mine_ref[0])], buf.at[z, 0, i]) for i, ref in enumerate((a_ref, b_ref))],
+             [(buf.at[z], out_ref.at[z])]) for z in range(8)], in_sems, out_sems)
+
+
+def plane_columns(z):
+    return pl.ds(z * 2 * HEAD_DIM, 2 * HEAD_DIM)
+
+
+def unpack_kernel(in_ref, a_ref, b_ref, buf, in_sems, out_sems):
+    staged([([(in_ref.at[z, hh, i], buf.at[i, :, columns(2 * z + hh)]) for hh in range(2) for i in range(2)],
+             [(buf.at[i, :, plane_columns(z)], ref.at[:, plane_columns(z)]) for i, ref in enumerate((a_ref, b_ref))])
+            for z in range(8)], in_sems, out_sems)
+
+
+def unpack_front_kernel(mine_ref, in_ref, got_ref, a_ref, b_ref, buf, in_sems, out_sems):
+    half = mine_ref[0]
+    staged([([(in_ref.at[z, 0, i], buf.at[i, :, columns(2 * z + half)]) for i in range(2)]
+             + [(got_ref.at[z, i], buf.at[i, :, columns(2 * z + 1 - half)]) for i in range(2)],
+             [(buf.at[i, :, plane_columns(z)], ref.at[:, plane_columns(z)]) for i, ref in enumerate((a_ref, b_ref))])
+            for z in range(8)], in_sems, out_sems)
+
+
+def mover(kernel, name, out_shape, *args):
+    smem = pl.BlockSpec(memory_space=pltpu.SMEM)
+    hbm = pl.BlockSpec(memory_space=pl.ANY)
+    many = isinstance(out_shape, tuple)
+    return pl.pallas_call(
+        kernel,
+        out_shape=out_shape,
+        in_specs=[smem if a.dtype == jnp.int32 else hbm for a in args],
+        out_specs=(hbm,) * len(out_shape) if many else hbm,
+        scratch_shapes=[
+            pltpu.VMEM((2,) + ROWS.shape if many else out_shape.shape, jnp.bfloat16),
+            pltpu.SemaphoreType.DMA((32,)),
+            pltpu.SemaphoreType.DMA((16,)),
+        ],
+        compiler_params=pltpu.CompilerParams(vmem_limit_bytes=24 * 1024 * 1024),
+        cost_estimate=pl.CostEstimate(flops=0, bytes_accessed=2**22, transcendentals=0),
+        name=name,
+    )(*args)
+
+
+def norm_kernel(mine_ref, kv_hbm, gain_ref, own_hbm, cross_hbm, kv, out, in_sems, out_sems):
     half = mine_ref[0]
     plane = mine_ref[1]
-    for own in (True, False):
-        hh = half if own else 1 - half
-        gain = gain_ref[pl.ds(2 * plane + hh, 1), :]
-        if own:
-            total = [part_ref[i, 0].astype(jnp.float32) + core_ref[i, 0].astype(jnp.float32) + side_ref[i, 0].astype(jnp.float32)
-                     for i in range(2)]
-        else:
-            total = [far_ref[i, 0].astype(jnp.float32) for i in range(2)]
-        wide = kv_ref[0, hh, 0].astype(jnp.float32)
-        scale = lax.rsqrt(jnp.mean(wide * wide, axis=-1, keepdims=True) + EPS)
-        weighted = total[0] * gain
-        inner = jnp.mean(weighted * wide, axis=-1, keepdims=True)
-        out_ref[0, hh, 0] = (scale * weighted - wide * (scale * scale * scale) * inner).astype(jnp.bfloat16)
-        out_ref[0, hh, 1] = total[1].astype(jnp.bfloat16)
+    loads = [pltpu.make_async_copy(kv_hbm.at[z], kv.at[z], in_sems.at[z]) for z in range(8)]
+    for load in loads:
+        load.start()
+    stores = []
+    for z in range(8):
+        loads[z].wait()
+        for which, target in ((0, cross_hbm), (1, own_hbm)):
+            hh = half if which else 1 - half
+            wide = kv[z, hh, 0].astype(jnp.float32)
+            scale = lax.rsqrt(jnp.mean(wide * wide, axis=-1, keepdims=True) + EPS)
+            out[which, z] = (wide * scale * gain_ref[pl.ds(2 * plane + hh, 1), :]).astype(jnp.bfloat16)
+            stores.append(pltpu.make_async_copy(out.at[which, z], target.at[0, z], out_sems.at[4 * z + 2 * which]))
+            stores.append(pltpu.make_async_copy(kv.at[z, hh, 1], target.at[1, z], out_sems.at[4 * z + 2 * which + 1]))
+            stores[-2].start()
+            stores[-1].start()
+    for store in stores:
+        store.wait()
+
+
+def norm(mine, kv, gain):
+    hbm = pl.BlockSpec(memory_space=pl.ANY)
+    piece = jax.ShapeDtypeStruct((2, 8, 256, HEAD_DIM), jnp.bfloat16)
+    return pl.pallas_call(
+        norm_kernel,
+        out_shape=(piece, piece),
+        in_specs=[pl.BlockSpec(memory_space=pltpu.SMEM), hbm, pl.BlockSpec(memory_space=pltpu.VMEM)],
+        out_specs=(hbm, hbm),
+        scratch_shapes=[
+            pltpu.VMEM((8, 2, 2, 256, HEAD_DIM), jnp.bfloat16),
+            pltpu.VMEM((2, 8, 256, HEAD_DIM), jnp.bfloat16),
+            pltpu.SemaphoreType.DMA((8,)),
+            pltpu.SemaphoreType.DMA((32,)),
+        ],
+        compiler_params=pltpu.CompilerParams(vmem_limit_bytes=24 * 1024 * 1024),
+        cost_estimate=pl.CostEstimate(flops=10**7, bytes_accessed=2**22, transcendentals=2**13),
+        name="norm",
+    )(mine, kv, gain)
+
+
+def finish_kernel(mine_ref, part_hbm, core_hbm, side_hbm, far_hbm, kv_hbm, gain_ref, out_hbm,
+                  sums, kv, out, in_sems, out_sems):
+    half = mine_ref[0]
+    plane = mine_ref[1]
+    loads = []
+    for z in range(8):
+        for i, ref in enumerate((part_hbm, core_hbm, side_hbm, far_hbm)):
+            loads.append(pltpu.make_async_copy(ref.at[:, z], sums.at[i, :, z], in_sems.at[5 * z + i]))
+        loads.append(pltpu.make_async_copy(kv_hbm.at[z, :, 0], kv.at[z], in_sems.at[5 * z + 4]))
+    for load in loads:
+        load.start()
+    stores = []
+    for z in range(8):
+        for load in loads[5 * z:5 * z + 5]:
+            load.wait()
+        for own in (True, False):
+            hh = half if own else 1 - half
+            gain = gain_ref[pl.ds(2 * plane + hh, 1), :]
+            if own:
+                total = [functools.reduce(jnp.add, [sums[j, i, z].astype(jnp.float32) for j in range(3)]) for i in range(2)]
+            else:
+                total = [sums[3, i, z].astype(jnp.float32) for i in range(2)]
+            wide = kv[z, hh].astype(jnp.float32)
+            scale = lax.rsqrt(jnp.mean(wide * wide, axis=-1, keepdims=True) + EPS)
+            weighted = total[0] * gain
+            inner = jnp.mean(weighted * wide, axis=-1, keepdims=True)
+            out[z, hh, 0] = (scale * weighted - wide * (scale * scale * scale) * inner).astype(jnp.bfloat16)
+            out[z, hh, 1] = total[1].astype(jnp.bfloat16)
+        stores.append(pltpu.make_async_copy(out.at[z], out_hbm.at[z], out_sems.at[z]))
+        stores[-1].start()
+    for store in stores:
+        store.wait()
 
 
 def finish(mine, part, core, side, far, kv, gain):
-    piece = pl.BlockSpec((2, 1, 256, 128), lambda i: (0, i, 0, 0))
+    hbm = pl.BlockSpec(memory_space=pl.ANY)
     return pl.pallas_call(
         finish_kernel,
-        grid=(8,),
-        out_shape=jax.ShapeDtypeStruct((8, 2, 2, 256, 128), jnp.bfloat16),
-        in_specs=[pl.BlockSpec(memory_space=pltpu.SMEM), piece, piece, piece, piece,
-                  pl.BlockSpec((1, 2, 1, 256, 128), lambda i: (i, 0, 0, 0, 0)),
-                  pl.BlockSpec((HEADS, 128), lambda i: (0, 0))],
-        out_specs=pl.BlockSpec((1, 2, 2, 256, 128), lambda i: (i, 0, 0, 0, 0)),
+        out_shape=PAIRS,
+        in_specs=[pl.BlockSpec(memory_space=pltpu.SMEM)] + [hbm] * 5 + [pl.BlockSpec(memory_space=pltpu.VMEM)],
+        out_specs=hbm,
+        scratch_shapes=[
+            pltpu.VMEM((4, 2, 8, 256, HEAD_DIM), jnp.bfloat16),
+            pltpu.VMEM((8, 2, 256, HEAD_DIM), jnp.bfloat16),
+            pltpu.VMEM((8, 2, 2, 256, HEAD_DIM), jnp.bfloat16),
+            pltpu.SemaphoreType.DMA((40,)),
+            pltpu.SemaphoreType.DMA((8,)),
+        ],
+        compiler_params=pltpu.CompilerParams(vmem_limit_bytes=24 * 1024 * 1024),
+        cost_estimate=pl.CostEstimate(flops=10**7, bytes_accessed=2**23, transcendentals=2**13),
         name="finish",
     )(mine, part, core, side, far, kv, gain)
 
 
-def unpack_kernel(in_ref, a_ref, b_ref):
-    for i, out in enumerate((a_ref, b_ref)):
-        for z in range(2):
-            for hh in range(2):
-                h = 2 * z + hh
-                out[:, h * 128:(h + 1) * 128] = in_ref[z, hh, i]
-
-
-def unpack(pieces):
-    rows = jax.ShapeDtypeStruct((256, HEADS * HEAD_DIM), jnp.bfloat16)
-    return pl.pallas_call(
-        unpack_kernel,
-        grid=(4,),
-        out_shape=(rows, rows),
-        in_specs=[pl.BlockSpec((2, 2, 2, 256, 128), lambda i: (i, 0, 0, 0, 0))],
-        out_specs=(pl.BlockSpec((256, 512), lambda i: (0, i)),) * 2,
-        cost_estimate=pl.CostEstimate(flops=0, bytes_accessed=2**22, transcendentals=0),
-        name="unpack",
-    )(pieces)
-
-
-def unpack_front_kernel(mine_ref, in_ref, got_ref, a_ref, b_ref):
-    half = mine_ref[0]
-    for i, out in enumerate((a_ref, b_ref)):
-        for z in range(2):
-            here = pl.multiple_of((2 * z + half) * 128, 128)
-            there = pl.multiple_of((2 * z + 1 - half) * 128, 128)
-            out[:, pl.ds(here, 128)] = in_ref[z, 0, i]
-            out[:, pl.ds(there, 128)] = got_ref[z, i]
-
-
-def unpack_front(mine, pieces, got):
-    rows = jax.ShapeDtypeStruct((256, HEADS * HEAD_DIM), jnp.bfloat16)
-    return pl.pallas_call(
-        unpack_front_kernel,
-        grid=(4,),
-        out_shape=(rows, rows),
-        in_specs=[
-            pl.BlockSpec(memory_space=pltpu.SMEM),
-            pl.BlockSpec((2, 1, 2, 256, 128), lambda i: (i, 0, 0, 0, 0)),
-            pl.BlockSpec((2, 2, 256, 128), lambda i: (i, 0, 0, 0)),
-        ],
-        out_specs=(pl.BlockSpec((256, 512), lambda i: (0, i)),) * 2,
-        cost_estimate=pl.CostEstimate(flops=0, bytes_accessed=2**22, transcendentals=0),
-        name="unpack_front",
-    )(mine, pieces, got)
-
-
 def along_z(array):
     return lax.all_to_all(array, "seq", split_axis=0, concat_axis=0, axis_index_groups=ALONG_Z, tiled=True)
 
 
 def across(array, flip):
     return lax.ppermute(array, "seq", [(i, i ^ flip) for i in range(64)])
-
-
-def by_head(rows):
-    return jnp.transpose(rows.reshape(256, 8, 2, HEAD_DIM), (1, 2, 0, 3))
 
 
 def wide_sum(*arrays):
@@ -300,28 +393,13 @@
     counts = lax.dynamic_slice_in_dim(block_count[0], head, 1, 0).reshape(128)
     info = jnp.stack([position % 8, head]).astype(jnp.int32)
     mine = jnp.stack([half, plane]).astype(jnp.int32)
-    gains = jnp.concatenate([query_gain, key_gain])
-
-    def of_half(pair, which):
-        return jnp.where(which == 0, pair[:, 0], pair[:, 1])
 
     with jax.named_scope("gather"):
-        query_heads, grad_heads = by_head(query_rows[0]), by_head(output_grad[0])
-        given = jnp.stack([of_half(query_heads, 1 - half), of_half(grad_heads, 1 - half)], axis=1)
-        got = across(given, 6)
-        kept = jnp.stack([of_half(query_heads, half), of_half(grad_heads, half)], axis=1)
-        kv = along_z(jnp.stack([by_head(key_rows[0]), by_head(value_rows[0])], axis=2))
-        pair_send = jnp.stack([kept, got], axis=1)
-        pair_send, kv, lists, counts, info, mine, gains = lax.optimization_barrier(
-            (pair_send, kv, lists, counts, info, mine, gains)
-        )
-        wide = kv[:, :, 0].astype(jnp.float32)
-        scale = lax.rsqrt(jnp.mean(wide * wide, axis=-1, keepdims=True) + EPS)
-        pair_gain = lax.dynamic_slice_in_dim(key_gain, 2 * plane, 2, 0)
-        normed = (wide * scale * pair_gain[None, :, None, :]).astype(jnp.bfloat16)
-        values = kv[:, :, 1]
-        cross_send = jnp.stack([of_half(normed, 1 - half), of_half(values, 1 - half)])
-        own = jnp.stack([of_half(normed, half), of_half(values, half)])
+        kv = along_z(mover(pack_kernel, "pack", PAIRS, key_rows[0], value_rows[0]))
+        got = across(mover(give_kernel, "give", HALF_PAIRS, mine, query_rows[0], output_grad[0]), 6)
+        pair_send = mover(pack_pair_kernel, "pack_pair", PAIRS, mine, query_rows[0], output_grad[0], got)
+        pair_send, kv, lists, counts, info = lax.optimization_barrier((pair_send, kv, lists, counts, info))
+        own, cross_send = norm(mine, kv, key_gain)
         cross = across(cross_send, 6)
         side = across(own, 2)
         query_pair = along_z(pair_send)
@@ -331,30 +409,35 @@
             pieces += [piece, across(piece, 1)]
         pieces = [p.reshape(2, 16, 128, 128) for p in pieces]
     with jax.named_scope("attend"):
-        outs = attend(info, counts, lists, pieces, query_pair.reshape(16, 2, 2, 128, 128), gains)
+        outs = attend(info, counts, lists, pieces, query_pair.reshape(16, 2, 2, 128, 128), query_gain, key_gain)
     front, parts, query_row, key_row = outs[0], outs[1:9], outs[9], outs[10]
     with jax.named_scope("return"):
         far = wide_sum(parts[4], across(parts[5], 1))
         side = wide_sum(parts[2], across(parts[3], 1))
-        front, far, side = lax.optimization_barrier((front, far, side))
+        far = across(far, 2)
+        front, side = lax.optimization_barrier((front, side))
         front = along_z(front.reshape(8, 2, 2, 256, HEAD_DIM))
-        far = across(far, 2)
         side = across(side, 2)
         cross = across(wide_sum(parts[6], across(parts[7], 1), far), 6)
         core = across(parts[1], 1)
         shape = (2, 8, 256, HEAD_DIM)
         kv_grad = finish(mine, parts[0].reshape(shape), core.reshape(shape), side.reshape(shape), cross.reshape(shape), kv, key_gain)
-        got = across(front[:, 1], 6)
-        attended, query_grad = unpack_front(mine, front, got)
-        key_grad, value_grad = unpack(along_z(kv_grad))
     with jax.named_scope("gains"):
         rows = over_copies(jnp.concatenate([query_row[0:1], key_row[0:1]]))
         other = across(rows, 4)
         rows = jnp.where(half == 0, jnp.stack([rows, other]), jnp.stack([other, rows]))
-        turns = [rows] + [lax.ppermute(rows, "seq", [(i, (i + 8 * d) % 64) for i in range(64)]) for d in range(1, 8)]
-        turns = jnp.stack(turns[::-1] + turns[::-1])
-        turns = lax.dynamic_slice_in_dim(turns, 7 - plane, 8, 0).reshape(HEADS, 2, HEAD_DIM)
-    return (attended[None], query_grad[None], key_grad[None], value_grad[None], turns[:, 0], turns[:, 1])
+        rows, kv_grad = lax.optimization_barrier((rows, kv_grad))
+        index = jnp.arange(8, dtype=jnp.int32)[:, None, None, None]
+        table = jnp.where(index == plane, rows[None], 0.0)
+        for d in range(1, 8):
+            came = lax.ppermute(rows, "seq", [(i, (i + 8 * d) % 64) for i in range(64)])
+            table = jnp.where(index == (plane - d) % 8, came[None], table)
+        table = table.reshape(HEADS, 2, HEAD_DIM)
+    with jax.named_scope("return"):
+        got = across(front[:, 1], 6)
+        attended, query_grad = mover(unpack_front_kernel, "unpack_front", (ROWS, ROWS), mine, front, got)
+        key_grad, value_grad = mover(unpack_kernel, "unpack", (ROWS, ROWS), along_z(kv_grad))
+    return (attended[None], query_grad[None], key_grad[None], value_grad[None], table[:, 0], table[:, 1])
 
 
 def solution(mesh):

time: 316 us -> 311 us (0.984)
  other arithmetic: 18.7 us -> 6.59 us
  starting transfers between devices: 52.6 us -> 59.4 us
  Pallas kernels: 56.4 us -> 62.7 us
    ppermute x7, waiting for transfers between devices: 1.32 us -> 35.2 us  [body(): came = lax.ppermute(rows, 'seq', [(i, (i + 8 * d) % 64) for i in range(64)])]
    ppermute x19, waiting for transfers between devices: 124 us -> 102 us  [across(): return lax.ppermute(array, 'seq', [(i, i ^ flip) for i in range(64)])]
    all_to_all x4, waiting for transfers between devices: 31.5 us -> 16.5 us  [along_z(): lax.all_to_all(array, 'seq', split_axis=0, concat_axis=0, axis_index_grou...]
    another operation x8 -> x1, other arithmetic: 6.92 us -> 0.07 us  [body(): mine = jnp.stack([half, plane]).astype(jnp.int32)]
    pallas_call x3 -> x7, Pallas kernels: 15 us -> 21.4 us  [the longest x5 11.2 us: mover(): pl.pallas_call(kernel, out_shape=out_shape, in_specs=[smem if a.dtype ==...]
    squeeze x6 -> x1, local copies, waits for them, and re-layouts: 5.91 us -> 0.61 us  [body(): table[:, 1]]
    ppermute x19, starting transfers between devices: 12 us -> 16.2 us  [across(): return lax.ppermute(array, 'seq', [(i, i ^ flip) for i in range(64)])]
    unnamed x58 -> x42, local copies, waits for them, and re-layouts: 10.8 us -> 11.6 us
  transfers between devices with their start and end apart: 32 -> 32, of which waited for: 16 -> 17; matrix products, arithmetic and copies ran while one was open for 9% -> 5% of each run, Pallas kernels for 4% -> 6%
where the time goes in v4:
time: 311 us; the launch traced here: 310 us
  waiting for transfers between devices  161 us (52%)
  Pallas kernels  62.7 us (20%)
  starting transfers between devices  59.4 us (19%)
  local copies, waits for them, and re-layouts  19.3 us (6%)
  other arithmetic  6.59 us (2%)
    ppermute x19, waiting for transfers between devices, across(): return lax.ppermute(array, 'seq', [(i, i ^ flip) for i in range(64)])  102 us
    pallas_call x1, Pallas kernels, attend(): pl.pallas_call(attend_kernel, out_shape=(jax.ShapeDtypeStruct((16, 2, 2,...  41.3 us
    ppermute x7, waiting for transfers between devices, body(): came = lax.ppermute(rows, 'seq', [(i, (i + 8 * d) % 64) for i in range(64)])  35.2 us
    all_to_all x4, starting transfers between devices, along_z(): lax.all_to_all(array, 'seq', split_axis=0, concat_axis=0, axis_index_grou...  25.6 us
    all_to_all x4, waiting for transfers between devices, along_z(): lax.all_to_all(array, 'seq', split_axis=0, concat_axis=0, axis_index_grou...  16.5 us
    ppermute x19, starting transfers between devices, across(): return lax.ppermute(array, 'seq', [(i, i ^ flip) for i in range(64)])  16.2 us
    ppermute x7, starting transfers between devices, body(): came = lax.ppermute(rows, 'seq', [(i, (i + 8 * d) % 64) for i in range(64)])  15.8 us
    unnamed x42, local copies, waits for them, and re-layouts  11.6 us
  transfers between devices with their start and end apart: 32, of which 17 were waited for; matrix products, arithmetic and copies ran while one was open for 5% of the time, Pallas kernels for 6%

profile of v4, /device:TPU:16, one launch (start us, length us, event | category | flops | bytes accessed | tf_op | source)
XLA Modules:
  0.0 309.8 jit_solution(11605120746841358853)
XLA Ops:
  0.7 1.2 copy-done.8
  1.9 1.2 copy-done.9
  3.1 1.2 pack.1
  4.3 1.4 copy-done.2
  5.7 8.6 %all-to-all-start = ((bf16[8,2,2,256,128]{4,3,2,1,0:T(8,128)(2,1)}), bf16[8,2,2,256,128]{4,3,2,1,0:T(8,128)(2,1)S(1)}, u32[]{:S(2)}, u32[]{:S(2)}) async-start(bf16[8,2,2,256,128]{4,3,2,1,0:T(8,128)(2,1)} %copy-done.2), calls=%async_computation | async-start | bytes 4194304 | tf_op jit(solution)/shard_map/gather/all_to_all | solution.py:368
  14.4 1.2 copy-done.5
  15.6 2.2 give.1
  17.8 2.8 collective-permute-start
  20.8 0.7 reshape.129.list_ref
  21.5 1.3 dynamic-slice_bitcast_fusion.count_ref
  22.7 0.7 pad_add_fusion.1.info_ref
  23.4 20.7 %collective-permute-done.got_ref = bf16[8,2,256,128]{3,2,1,0:T(8,128)(2,1)} collective-permute-done((bf16[8,2,256,128]{3,2,1,0:T(8,128)(2,1)}, bf16[8,2,256,128]{3,2,1,0:T(8,128)(2,1)}, u32[]{:S(2)}, u32[]{:S(2)}) %collective-permute-start) | collective-permute-done | bytes 1048608 | tf_op jit(solution)/shard_map/gather/ppermute | solution.py:372
  44.1 1.2 copy-done.6
  45.3 2.3 pack_pair.1
  47.6 1.3 copy-done.3
  49.0 16.5 %all-to-all-done.kv_hbm = bf16[8,2,2,256,128]{4,3,2,1,0:T(8,128)(2,1)S(1)} async-done(((bf16[8,2,2,256,128]{4,3,2,1,0:T(8,128)(2,1)}), bf16[8,2,2,256,128]{4,3,2,1,0:T(8,128)(2,1)S(1)}, u32[]{:S(2)}, u32[]{:S(2)}) %all-to-all-start) | async-done | bytes 2097184 | tf_op jit(solution)/shard_map/gather/all_to_all | solution.py:368
  65.5 4.4 %all-to-all-start.1 = ((bf16[8,2,2,256,128]{4,3,2,1,0:T(8,128)(2,1)}), bf16[8,2,2,256,128]{4,3,2,1,0:T(8,128)(2,1)}, u32[]{:S(2)}, u32[]{:S(2)}) async-start(bf16[8,2,2,256,128]{4,3,2,1,0:T(8,128)(2,1)} %copy-done.3), calls=%async_computation.1 | async-start | bytes 4194304 | tf_op jit(solution)/shard_map/gather/all_to_all | solution.py:368
  69.9 5.7 %norm.1 = (bf16[2,8,256,128]{3,2,1,0:T(8,128)(2,1)S(1)}, bf16[2,8,256,128]{3,2,1,0:T(8,128)(2,1)S(1)}) custom-call(s32[2]{0:T(128)S(1)} %pad_add_fusion.mine_ref, bf16[8,2,2,256,128]{4,3,2,1,0:T(8,128)(2,1)S(1)} %all-to-all-done.kv_hbm, f32[16,128]{1,0:T(8,128)S(1)} %copy-done.10), custom_call_target="tpu_custom_call" | custom-call | flops 10000000 | bytes 4194304 | tf_op jit(solution)/shard_map/gather/norm/pallas_call | solution.py:296
  75.6 2.8 collective-permute-start.4
  78.6 20.3 %collective-permute-done.4 = bf16[2,8,256,128]{3,2,1,0:T(8,128)(2,1)S(1)} collective-permute-done((bf16[2,8,256,128]{3,2,1,0:T(8,128)(2,1)S(1)}, bf16[2,8,256,128]{3,2,1,0:T(8,128)(2,1)S(1)}, u32[]{:S(2)}, u32[]{:S(2)}) %collective-permute-start.4) | collective-permute-done | bytes 1048608 | tf_op jit(solution)/shard_map/gather/ppermute | solution.py:372
  99.2 0.5 collective-permute-start.7
  99.7 2.9 collective-permute-done.2
  102.6 20.1 %collective-permute-done.5 = bf16[2,8,256,128]{3,2,1,0:T(8,128)(2,1)S(1)} collective-permute-done((bf16[2,8,256,128]{3,2,1,0:T(8,128)(2,1)S(1)}, bf16[2,8,256,128]{3,2,1,0:T(8,128)(2,1)S(1)}, u32[]{:S(2)}, u32[]{:S(2)}) %collective-permute-start.5) | collective-permute-done | bytes 1048608 | tf_op jit(solution)/shard_map/gather/ppermute | solution.py:372
  122.7 0.9 copy-done.17
  124.3 1.0 copy-done.19
  125.5 41.3 %attend.1 = (bf16[16,2,2,128,128]{4,3,2,1,0:T(8,128)(2,1)}, bf16[2,16,128,128]{3,2,1,0:T(8,128)(2,1)}, bf16[2,16,128,128]{3,2,1,0:T(8,128)(2,1)}, bf16[2,16,128,...) custom-call(s32[2]{0:T(128)} %pad_add_fusion.1.info_ref, ...), custom_call_target="tpu_custom_call" | custom-call | flops 6000000000 | bytes 20971520 | tf_op jit(solution)/shard_map/attend/attend/pallas_call | solution.py:163
  167.0 0.5 collective-permute-start.18
  167.5 2.9 collective-permute-done.8
  170.4 2.5 add_convert_fusion.2
  172.9 5.5 %all-to-all-start.2 = ((bf16[8,2,2,256,128]{4,3,2,1,0:T(8,128)(2,1)}), bf16[8,2,2,256,128]{4,3,2,1,0:T(8,128)(2,1)}, u32[]{:S(2)}, u32[]{:S(2)}) async-start(bf16[8,2,2,256,128]{4,3,2,1,0:T(8,128)(2,1)} %bitcast.56), calls=%async_computation.2 | async-start | bytes 4194304 | tf_op jit(solution)/shard_map/return/all_to_all | solution.py:368
  178.6 1.7 add_convert_fusion.1
  180.3 2.4 collective-permute-start.19
  182.9 0.4 collective-permute-start.16
  183.3 23.5 %collective-permute-done.19 = bf16[2,16,128,128]{3,2,1,0:T(8,128)(2,1)S(1)} collective-permute-done((bf16[2,16,128,128]{3,2,1,0:T(8,128)(2,1)S(1)}, bf16[2,16,128,128]{3,2,1,0:T(8,128)(2,1)S(1)}, u32[]{:S(2)}, u32[]{:S(2)}) %collective-permute-start.19) | collective-permute-done | bytes 1048608 | tf_op jit(solution)/shard_map/return/ppermute | solution.py:372
  206.8 1.5 add_convert_fusion
  208.3 1.4 collective-permute-start.20
  209.7 0.7 slice.16
  210.3 0.7 slice.17
  211.0 1.4 collective-permute-start.10
  212.4 2.2 collective-permute-done.10
  214.6 0.4 collective-permute-start.11
  215.0 4.8 %collective-permute-done.11 = f32[2,128]{1,0:T(2,128)S(1)} collective-permute-done((f32[2,128]{1,0:T(2,128)S(1)}, f32[2,128]{1,0:T(2,128)S(1)}, u32[]{:S(2)}, u32[]{:S(2)}) %collective-permute-start.11) | collective-permute-done | bytes 1056 | tf_op jit(solution)/shard_map/gains/ppermute | solution.py:381
  219.9 1.1 collective-permute-done.12
  221.0 0.9 collective-permute-start.13
  221.9 7.2 %collective-permute-done.13 = f32[2,128]{1,0:T(2,128)S(1)} collective-permute-done((f32[2,128]{1,0:T(2,128)S(1)}, f32[2,128]{1,0:T(2,128)S(1)}, u32[]{:S(2)}, u32[]{:S(2)}) %collective-permute-start.13) | collective-permute-done | bytes 1056 | tf_op jit(solution)/shard_map/gains/ppermute | solution.py:372
  229.1 2.2 collective-permute-start.14
  231.3 2.9 collective-permute-done.14
  234.2 0.4 collective-permute-done.20
  234.6 4.5 %finish.1 = bf16[8,2,2,256,128]{4,3,2,1,0:T(8,128)(2,1)S(1)} custom-call(s32[2]{0:T(128)S(1)} %pad_add_fusion.mine_ref, bf16[2,8,256,128]{3,2,1,0:T(8,128)(2,1)S(1)} %bitcast.52, bf16[2,8,256,128]{3,2,1,0:T(8,128)(2,1)} %bitcast.25.core_hbm, bf16[2,8,256,128]{3,2,1,0:T(8,128)(2,1)} %bitcast.26.side_hbm, bf16[2,8,256,128]{3,2,1,0:T(8,128)(2,1)} %bitcast.27.far_hbm, ...), custom_call_target="tpu_custom_call" | custom-call | flops 10000000 | bytes 8388608 | tf_op jit(solution)/shard_map/return/finish/pallas_call | solution.py:349
  239.1 1.3 copy-done.1
  240.4 7.1 %all-to-all-start.3 = ((bf16[8,2,2,256,128]{4,3,2,1,0:T(8,128)(2,1)}), bf16[8,2,2,256,128]{4,3,2,1,0:T(8,128)(2,1)S(1)}, u32[]{:S(2)}, u32[]{:S(2)}) async-start(bf16[8,2,2,256,128]{4,3,2,1,0:T(8,128)(2,1)} %copy-done.1), calls=%async_computation.3 | async-start | bytes 4194304 | tf_op jit(solution)/shard_map/return/all_to_all | solution.py:368
  247.5 2.3 slice_bitcast_fusion
  249.8 1.0 collective-permute-start.9
  250.9 3.3 %collective-permute-start.21 = (f32[2,2,128]{2,1,0:T(2,128)S(1)}, f32[2,2,128]{2,1,0:T(2,128)S(1)}, u32[]{:S(2)}, u32[]{:S(2)}) collective-permute-start(f32[2,2,128]{2,1,0:T(2,128)S(1)} %maximum_select_fusion), channel_id=1, source_target_pairs={{0,56},{1,57},{2,58},{3,59},{4,60},{5,61},{6,62},{7,63},{8,0},{9,1... | collective-permute-start | bytes 6152 | tf_op jit(solution)/shard_map/gains/ppermute | solution.py:433
  254.2 2.4 collective-permute-start.22
  256.6 1.5 collective-permute-start.23
  258.0 3.6 %collective-permute-start.24 = (f32[2,2,128]{2,1,0:T(2,128)S(1)}, f32[2,2,128]{2,1,0:T(2,128)S(1)}, u32[]{:S(2)}, u32[]{:S(2)}) collective-permute-start(f32[2,2,128]{2,1,0:T(2,128)S(1)} %maximum_select_fusion), channel_id=1, source_target_pairs={{0,32},{1,33},{2,34},{3,35},{4,36},{5,37},{6,38},{7,39},{8,40},{9,... | collective-permute-start | bytes 6152 | tf_op jit(solution)/shard_map/gains/ppermute | solution.py:433
  261.6 32.4 %collective-permute-done.21 = f32[2,2,128]{2,1,0:T(2,128)S(1)} collective-permute-done((f32[2,2,128]{2,1,0:T(2,128)S(1)}, f32[2,2,128]{2,1,0:T(2,128)S(1)}, u32[]{:S(2)}, u32[]{:S(2)}) %collective-permute-start.21) | collective-permute-done | bytes 2080 | tf_op jit(solution)/shard_map/gains/ppermute | solution.py:433
  294.4 3.8 %collective-permute-start.26 = (f32[2,2,128]{2,1,0:T(2,128)S(1)}, f32[2,2,128]{2,1,0:T(2,128)S(1)}, u32[]{:S(2)}, u32[]{:S(2)}) collective-permute-start(f32[2,2,128]{2,1,0:T(2,128)S(1)} %maximum_select_fusion), channel_id=1, source_target_pairs={{0,16},{1,17},{2,18},{3,19},{4,20},{5,21},{6,22},{7,23},{8,24},{9,... | collective-permute-start | bytes 6152 | tf_op jit(solution)/shard_map/gains/ppermute | solution.py:433
  298.1 1.0 collective-permute-start.27
  300.6 2.7 collective-permute-done.27
  303.5 0.6 slice_bitcast_fusion.1
  304.1 3.1 %unpack_front.1 = (bf16[256,2048]{1,0:T(8,128)(2,1)}, bf16[256,2048]{1,0:T(8,128)(2,1)}) custom-call(s32[2]{0:T(128)S(1)} %pad_add_fusion.mine_ref, bf16[8,2,2,256,128]{4,3,2,1,0:T(8,128)(2,1)} %all-to-all-done.2.in_ref, bf16[8,2,256,128]{3,2,1,0:T(8,128)(2,1)S(1)} %collective-permute-done.9.got_ref), custom_call_target="tpu_custom_call" | custom-call | bytes 4194304 | tf_op jit(solution)/shard_map/return/unpack_front/pallas_call | solution.py:255
  307.3 2.3 unpack.1
  (110 shorter events, 4.3 us)
Async XLA Ops:
  0.6 20.0 %copy-start = (s32[1,16,128,8]{2,3,1,0:T(8,128)S(1)}, s32[1,16,128,8]{2,3,1,0:T(8,128)}, u32[]{:S(2)}) copy-start(s32[1,16,128,8]{2,3,1,0:T(8,128)} %param.14) | copy-start | bytes 196612
  0.6 1.3 copy-start.8
  1.9 1.2 copy-start.9
  4.3 1.4 copy-start.2
  5.7 8.7 %copy-start.4 = (bf16[1,256,2048]{2,1,0:T(8,128)(2,1)S(1)}, bf16[1,256,2048]{2,1,0:T(8,128)(2,1)}, u32[]{:S(2)}) copy-start(bf16[1,256,2048]{2,1,0:T(8,128)(2,1)} %param.8) | copy-start | bytes 3145732
  5.7 59.8 %all-to-all-start = ((bf16[8,2,2,256,128]{4,3,2,1,0:T(8,128)(2,1)}), bf16[8,2,2,256,128]{4,3,2,1,0:T(8,128)(2,1)S(1)}, u32[]{:S(2)}, u32[]{:S(2)}) async-start(bf16[8,2,2,256,128]{4,3,2,1,0:T(8,128)(2,1)} %copy-done.2), calls=%async_computation | async-start | bytes 4194304 | tf_op jit(solution)/shard_map/gather/all_to_all | solution.py:368
  14.4 1.2 copy-start.5
  17.8 26.2 %collective-permute-start = (bf16[8,2,256,128]{3,2,1,0:T(8,128)(2,1)}, bf16[8,2,256,128]{3,2,1,0:T(8,128)(2,1)}, u32[]{:S(2)}, u32[]{:S(2)}) collective-permute-start(bf16[8,2,256,128]{3,2,1,0:T(8,128)(2,1)} %give.1), channel_id=1, source_target_pairs={{0,6},{1,7},{2,4},{3,5},{4,2},{5,3},{6,0},{7,1},{8,14},{9,15},{10,... | collective-permute-start | bytes 3145736 | tf_op jit(solution)/shard_map/gather/ppermute | solution.py:372
  44.1 1.2 copy-start.6
  47.6 1.4 copy-start.3
  49.0 20.9 %copy-start.10 = (f32[16,128]{1,0:T(8,128)S(1)}, f32[16,128]{1,0:T(8,128)}, u32[]{:S(2)}) copy-start(f32[16,128]{1,0:T(8,128)} %gain_ref.3) | copy-start | bytes 24580
  65.5 60.0 %all-to-all-start.1 = ((bf16[8,2,2,256,128]{4,3,2,1,0:T(8,128)(2,1)}), bf16[8,2,2,256,128]{4,3,2,1,0:T(8,128)(2,1)}, u32[]{:S(2)}, u32[]{:S(2)}) async-start(bf16[8,2,2,256,128]{4,3,2,1,0:T(8,128)(2,1)} %copy-done.3), calls=%async_computation.1 | async-start | bytes 4194304 | tf_op jit(solution)/shard_map/gather/all_to_all | solution.py:368
  75.5 49.9 %copy-start.12 = (bf16[2,8,256,128]{3,2,1,0:T(8,128)(2,1)}, bf16[2,8,256,128]{3,2,1,0:T(8,128)(2,1)S(1)}, u32[]{:S(2)}) copy-start(bf16[2,8,256,128]{3,2,1,0:T(8,128)(2,1)S(1)} %get-tuple-element.36) | copy-start | bytes 3145732
  75.6 23.4 %collective-permute-start.4 = (bf16[2,8,256,128]{3,2,1,0:T(8,128)(2,1)S(1)}, bf16[2,8,256,128]{3,2,1,0:T(8,128)(2,1)S(1)}, u32[]{:S(2)}, u32[]{:S(2)}) collective-permute-start(bf16[2,8,256,128]{3,2,1,0:T(8,128)(2,1)S(1)} %get-tuple-element.37), channel_id=1, source_target_pairs={{0,6},{1,7},{2,4},{3,5},{4,2},{5,3},{6,0},{7,1},{8,14},{9,15},{10,... | collective-permute-start | bytes 3145736 | tf_op jit(solution)/shard_map/gather/ppermute | solution.py:372
  78.4 24.2 %collective-permute-start.2 = (bf16[2,8,256,128]{3,2,1,0:T(8,128)(2,1)S(1)}, bf16[2,8,256,128]{3,2,1,0:T(8,128)(2,1)S(1)}, u32[]{:S(2)}, u32[]{:S(2)}) collective-permute-start(bf16[2,8,256,128]{3,2,1,0:T(8,128)(2,1)S(1)} %get-tuple-element.36), channel_id=1, source_target_pairs={{0,2},{1,3},{2,0},{3,1},{4,6},{5,7},{6,4},{7,5},{8,10},{9,11},{10,... | collective-permute-start | bytes 3145736 | tf_op jit(solution)/shard_map/gather/ppermute | solution.py:372
  98.9 23.8 %copy-start.15 = (bf16[2,8,256,128]{3,2,1,0:T(8,128)(2,1)}, bf16[2,8,256,128]{3,2,1,0:T(8,128)(2,1)S(1)}, u32[]{:S(2)}) copy-start(bf16[2,8,256,128]{3,2,1,0:T(8,128)(2,1)S(1)} %collective-permute-done.4) | copy-start | bytes 3145732
  98.9 23.7 %collective-permute-start.5 = (bf16[2,8,256,128]{3,2,1,0:T(8,128)(2,1)S(1)}, bf16[2,8,256,128]{3,2,1,0:T(8,128)(2,1)S(1)}, u32[]{:S(2)}, u32[]{:S(2)}) collective-permute-start(bf16[2,8,256,128]{3,2,1,0:T(8,128)(2,1)S(1)} %collective-permute-done.4), channel_id=1, source_target_pairs={{0,2},{1,3},{2,0},{3,1},{4,6},{5,7},{6,4},{7,5},{8,10},{9,11},{10,... | collective-permute-start | bytes 3145736 | tf_op jit(solution)/shard_map/gather/ppermute | solution.py:372
  99.2 23.5 %collective-permute-start.1 = (bf16[2,8,256,128]{3,2,1,0:T(8,128)(2,1)S(1)}, bf16[2,8,256,128]{3,2,1,0:T(8,128)(2,1)S(1)}, u32[]{:S(2)}, u32[]{:S(2)}) collective-permute-start(bf16[2,8,256,128]{3,2,1,0:T(8,128)(2,1)S(1)} %get-tuple-element.36), channel_id=1, source_target_pairs={{0,1},{1,0},{2,3},{3,2},{4,5},{5,4},{6,7},{7,6},{8,9},{9,8},{10,11... | collective-permute-start | bytes 3145736 | tf_op jit(solution)/shard_map/gather/ppermute | solution.py:372
  99.2 23.5 %collective-permute-start.7 = (bf16[2,8,256,128]{3,2,1,0:T(8,128)(2,1)S(1)}, bf16[2,8,256,128]{3,2,1,0:T(8,128)(2,1)S(1)}, u32[]{:S(2)}, u32[]{:S(2)}) collective-permute-start(bf16[2,8,256,128]{3,2,1,0:T(8,128)(2,1)S(1)} %collective-permute-done.4), channel_id=1, source_target_pairs={{0,1},{1,0},{2,3},{3,2},{4,5},{5,4},{6,7},{7,6},{8,9},{9,8},{10,11... | collective-permute-start | bytes 3145736 | tf_op jit(solution)/shard_map/gather/ppermute | solution.py:372
  102.6 20.1 %copy-start.16 = (bf16[2,8,256,128]{3,2,1,0:T(8,128)(2,1)}, bf16[2,8,256,128]{3,2,1,0:T(8,128)(2,1)S(1)}, u32[]{:S(2)}) copy-start(bf16[2,8,256,128]{3,2,1,0:T(8,128)(2,1)S(1)} %collective-permute-done.2) | copy-start | bytes 3145732
  102.6 20.1 %collective-permute-start.3 = (bf16[2,8,256,128]{3,2,1,0:T(8,128)(2,1)S(1)}, bf16[2,8,256,128]{3,2,1,0:T(8,128)(2,1)S(1)}, u32[]{:S(2)}, u32[]{:S(2)}) collective-permute-start(bf16[2,8,256,128]{3,2,1,0:T(8,128)(2,1)S(1)} %collective-permute-done.2), channel_id=1, source_target_pairs={{0,1},{1,0},{2,3},{3,2},{4,5},{5,4},{6,7},{7,6},{8,9},{9,8},{10,11... | collective-permute-start | bytes 3145736 | tf_op jit(solution)/shard_map/gather/ppermute | solution.py:372
  122.7 1.0 copy-start.17
  122.7 2.8 collective-permute-start.6
  122.7 1.3 copy-start.18
  122.7 1.6 copy-start.20
  124.3 1.0 copy-start.19
  166.8 3.6 %collective-permute-start.8 = (bf16[2,16,128,128]{3,2,1,0:T(8,128)(2,1)}, bf16[2,16,128,128]{3,2,1,0:T(8,128)(2,1)S(1)}, u32[]{:S(2)}, u32[]{:S(2)}) collective-permute-start(bf16[2,16,128,128]{3,2,1,0:T(8,128)(2,1)} %get-tuple-element.41), channel_id=1, source_target_pairs={{0,1},{1,0},{2,3},{3,2},{4,5},{5,4},{6,7},{7,6},{8,9},{9,8},{10,11... | collective-permute-start | bytes 3145736 | tf_op jit(solution)/shard_map/return/ppermute | solution.py:372
  167.0 11.6 %collective-permute-start.18 = (bf16[2,16,128,128]{3,2,1,0:T(8,128)(2,1)}, bf16[2,16,128,128]{3,2,1,0:T(8,128)(2,1)}, u32[]{:S(2)}, u32[]{:S(2)}) collective-permute-start(bf16[2,16,128,128]{3,2,1,0:T(8,128)(2,1)} %get-tuple-element.53), channel_id=1, source_target_pairs={{0,1},{1,0},{2,3},{3,2},{4,5},{5,4},{6,7},{7,6},{8,9},{9,8},{10,11... | collective-permute-start | bytes 3145736 | tf_op jit(solution)/shard_map/return/ppermute | solution.py:372
  172.9 5.7 %copy-start.13 = (bf16[2,16,128,128]{3,2,1,0:T(8,128)(2,1)S(1)}, bf16[2,16,128,128]{3,2,1,0:T(8,128)(2,1)}, u32[]{:S(2)}) copy-start(bf16[2,16,128,128]{3,2,1,0:T(8,128)(2,1)} %get-tuple-element.52) | copy-start | bytes 3145732
  172.9 67.5 %all-to-all-start.2 = ((bf16[8,2,2,256,128]{4,3,2,1,0:T(8,128)(2,1)}), bf16[8,2,2,256,128]{4,3,2,1,0:T(8,128)(2,1)}, u32[]{:S(2)}, u32[]{:S(2)}) async-start(bf16[8,2,2,256,128]{4,3,2,1,0:T(8,128)(2,1)} %bitcast.56), calls=%async_computation.2 | async-start | bytes 4194304 | tf_op jit(solution)/shard_map/return/all_to_all | solution.py:368
  178.5 28.3 %copy-start.14 = (bf16[2,16,128,128]{3,2,1,0:T(8,128)(2,1)S(1)}, bf16[2,16,128,128]{3,2,1,0:T(8,128)(2,1)}, u32[]{:S(2)}) copy-start(bf16[2,16,128,128]{3,2,1,0:T(8,128)(2,1)} %get-tuple-element.50) | copy-start | bytes 3145732
  178.5 4.8 %collective-permute-start.17 = (bf16[2,16,128,128]{3,2,1,0:T(8,128)(2,1)}, bf16[2,16,128,128]{3,2,1,0:T(8,128)(2,1)S(1)}, u32[]{:S(2)}, u32[]{:S(2)}) collective-permute-start(bf16[2,16,128,128]{3,2,1,0:T(8,128)(2,1)} %get-tuple-element.51), channel_id=1, source_target_pairs={{0,1},{1,0},{2,3},{3,2},{4,5},{5,4},{6,7},{7,6},{8,9},{9,8},{10,11... | collective-permute-start | bytes 3145736 | tf_op jit(solution)/shard_map/return/ppermute | solution.py:372
  180.3 26.4 %collective-permute-start.19 = (bf16[2,16,128,128]{3,2,1,0:T(8,128)(2,1)S(1)}, bf16[2,16,128,128]{3,2,1,0:T(8,128)(2,1)S(1)}, u32[]{:S(2)}, u32[]{:S(2)}) collective-permute-start(bf16[2,16,128,128]{3,2,1,0:T(8,128)(2,1)S(1)} %add_convert_fusion.1), channel_id=1, source_target_pairs={{0,2},{1,3},{2,0},{3,1},{4,6},{5,7},{6,4},{7,5},{8,10},{9,11},{10,... | collective-permute-start | bytes 3145736 | tf_op jit(solution)/shard_map/return/ppermute | solution.py:372
  182.8 51.4 %collective-permute-start.15 = (bf16[2,16,128,128]{3,2,1,0:T(8,128)(2,1)}, bf16[2,16,128,128]{3,2,1,0:T(8,128)(2,1)}, u32[]{:S(2)}, u32[]{:S(2)}) collective-permute-start(bf16[2,16,128,128]{3,2,1,0:T(8,128)(2,1)} %get-tuple-element.48), channel_id=1, source_target_pairs={{0,1},{1,0},{2,3},{3,2},{4,5},{5,4},{6,7},{7,6},{8,9},{9,8},{10,11... | collective-permute-start | bytes 3145736 | tf_op jit(solution)/shard_map/return/ppermute | solution.py:372
  182.9 51.3 %collective-permute-start.16 = (bf16[2,16,128,128]{3,2,1,0:T(8,128)(2,1)}, bf16[2,16,128,128]{3,2,1,0:T(8,128)(2,1)}, u32[]{:S(2)}, u32[]{:S(2)}) collective-permute-start(bf16[2,16,128,128]{3,2,1,0:T(8,128)(2,1)} %add_convert_fusion.2), channel_id=1, source_target_pairs={{0,2},{1,3},{2,0},{3,1},{4,6},{5,7},{6,4},{7,5},{8,10},{9,11},{10,... | collective-permute-start | bytes 3145736 | tf_op jit(solution)/shard_map/return/ppermute | solution.py:372
  206.8 27.8 %copy-start.7 = (bf16[2,16,128,128]{3,2,1,0:T(8,128)(2,1)S(1)}, bf16[2,16,128,128]{3,2,1,0:T(8,128)(2,1)}, u32[]{:S(2)}) copy-start(bf16[2,16,128,128]{3,2,1,0:T(8,128)(2,1)} %get-tuple-element.47) | copy-start | bytes 3145732
  206.8 27.8 %copy-start.11 = (f32[16,128]{1,0:T(8,128)S(1)}, f32[16,128]{1,0:T(8,128)}, u32[]{:S(2)}) copy-start(f32[16,128]{1,0:T(8,128)} %gain_ref.3) | copy-start | bytes 24580
  208.3 26.3 %collective-permute-start.20 = (bf16[2,16,128,128]{3,2,1,0:T(8,128)(2,1)}, bf16[2,16,128,128]{3,2,1,0:T(8,128)(2,1)}, u32[]{:S(2)}, u32[]{:S(2)}) collective-permute-start(bf16[2,16,128,128]{3,2,1,0:T(8,128)(2,1)} %add_convert_fusion), channel_id=1, source_target_pairs={{0,6},{1,7},{2,4},{3,5},{4,2},{5,3},{6,0},{7,1},{8,14},{9,15},{10,... | collective-permute-start | bytes 3145736 | tf_op jit(solution)/shard_map/return/ppermute | solution.py:372
  211.0 3.6 %collective-permute-start.10 = (f32[2,128]{1,0:T(2,128)S(1)}, f32[2,128]{1,0:T(2,128)S(1)}, u32[]{:S(2)}, u32[]{:S(2)}) collective-permute-start(f32[2,128]{1,0:T(2,128)S(1)} %pad_maximum_fusion), channel_id=1, source_target_pairs={{0,64},{64,0},{128,192},{192,128},{1,65},{65,1},{129,193},{193,129... | collective-permute-start | bytes 3080 | tf_op jit(solution)/shard_map/gains/ppermute | solution.py:381
  214.6 5.2 %collective-permute-start.11 = (f32[2,128]{1,0:T(2,128)S(1)}, f32[2,128]{1,0:T(2,128)S(1)}, u32[]{:S(2)}, u32[]{:S(2)}) collective-permute-start(f32[2,128]{1,0:T(2,128)S(1)} %fusion), channel_id=1, source_target_pairs={{0,128},{64,192},{128,0},{192,64},{1,129},{65,193},{129,1},{193,65... | collective-permute-start | bytes 3080 | tf_op jit(solution)/shard_map/gains/ppermute | solution.py:381
  219.8 1.2 collective-permute-start.12
  221.0 8.1 %collective-permute-start.13 = (f32[2,128]{1,0:T(2,128)S(1)}, f32[2,128]{1,0:T(2,128)S(1)}, u32[]{:S(2)}, u32[]{:S(2)}) collective-permute-start(f32[2,128]{1,0:T(2,128)S(1)} %add.71), channel_id=1, source_target_pairs={{0,2},{1,3},{2,0},{3,1},{4,6},{5,7},{6,4},{7,5},{8,10},{9,11},{10,... | collective-permute-start | bytes 3080 | tf_op jit(solution)/shard_map/gains/ppermute | solution.py:372
  229.1 5.1 %collective-permute-start.14 = (f32[2,128]{1,0:T(2,128)S(1)}, f32[2,128]{1,0:T(2,128)S(1)}, u32[]{:S(2)}, u32[]{:S(2)}) collective-permute-start(f32[2,128]{1,0:T(2,128)S(1)} %add.72), channel_id=1, source_target_pairs={{0,4},{1,5},{2,6},{3,7},{4,0},{5,1},{6,2},{7,3},{8,12},{9,13},{10,... | collective-permute-start | bytes 3080 | tf_op jit(solution)/shard_map/gains/ppermute | solution.py:372
  239.1 1.4 copy-start.1
  240.4 66.9 %all-to-all-start.3 = ((bf16[8,2,2,256,128]{4,3,2,1,0:T(8,128)(2,1)}), bf16[8,2,2,256,128]{4,3,2,1,0:T(8,128)(2,1)S(1)}, u32[]{:S(2)}, u32[]{:S(2)}) async-start(bf16[8,2,2,256,128]{4,3,2,1,0:T(8,128)(2,1)} %copy-done.1), calls=%async_computation.3 | async-start | bytes 4194304 | tf_op jit(solution)/shard_map/return/all_to_all | solution.py:368
  249.8 54.3 %collective-permute-start.9 = (bf16[8,2,256,128]{3,2,1,0:T(8,128)(2,1)}, bf16[8,2,256,128]{3,2,1,0:T(8,128)(2,1)S(1)}, u32[]{:S(2)}, u32[]{:S(2)}) collective-permute-start(bf16[8,2,256,128]{3,2,1,0:T(8,128)(2,1)} %slice_bitcast_fusion), channel_id=1, source_target_pairs={{0,6},{1,7},{2,4},{3,5},{4,2},{5,3},{6,0},{7,1},{8,14},{9,15},{10,... | collective-permute-start | bytes 3145736 | tf_op jit(solution)/shard_map/return/ppermute | solution.py:372
  250.9 43.1 %collective-permute-start.21 = (f32[2,2,128]{2,1,0:T(2,128)S(1)}, f32[2,2,128]{2,1,0:T(2,128)S(1)}, u32[]{:S(2)}, u32[]{:S(2)}) collective-permute-start(f32[2,2,128]{2,1,0:T(2,128)S(1)} %maximum_select_fusion), channel_id=1, source_target_pairs={{0,56},{1,57},{2,58},{3,59},{4,60},{5,61},{6,62},{7,63},{8,0},{9,1... | collective-permute-start | bytes 6152 | tf_op jit(solution)/shard_map/gains/ppermute | solution.py:433
  254.2 40.2 %collective-permute-start.22 = (f32[2,2,128]{2,1,0:T(2,128)S(1)}, f32[2,2,128]{2,1,0:T(2,128)S(1)}, u32[]{:S(2)}, u32[]{:S(2)}) collective-permute-start(f32[2,2,128]{2,1,0:T(2,128)S(1)} %maximum_select_fusion), channel_id=1, source_target_pairs={{0,48},{1,49},{2,50},{3,51},{4,52},{5,53},{6,54},{7,55},{8,56},{9,... | collective-permute-start | bytes 6152 | tf_op jit(solution)/shard_map/gains/ppermute | solution.py:433
  256.6 41.6 %collective-permute-start.23 = (f32[2,2,128]{2,1,0:T(2,128)S(1)}, f32[2,2,128]{2,1,0:T(2,128)S(1)}, u32[]{:S(2)}, u32[]{:S(2)}) collective-permute-start(f32[2,2,128]{2,1,0:T(2,128)S(1)} %maximum_select_fusion), channel_id=1, source_target_pairs={{0,40},{1,41},{2,42},{3,43},{4,44},{5,45},{6,46},{7,47},{8,48},{9,... | collective-permute-start | bytes 6152 | tf_op jit(solution)/shard_map/gains/ppermute | solution.py:433
  258.0 42.5 %collective-permute-start.24 = (f32[2,2,128]{2,1,0:T(2,128)S(1)}, f32[2,2,128]{2,1,0:T(2,128)S(1)}, u32[]{:S(2)}, u32[]{:S(2)}) collective-permute-start(f32[2,2,128]{2,1,0:T(2,128)S(1)} %maximum_select_fusion), channel_id=1, source_target_pairs={{0,32},{1,33},{2,34},{3,35},{4,36},{5,37},{6,38},{7,39},{8,40},{9,... | collective-permute-start | bytes 6152 | tf_op jit(solution)/shard_map/gains/ppermute | solution.py:433
  294.0 6.6 %collective-permute-start.25 = (f32[2,2,128]{2,1,0:T(2,128)S(1)}, f32[2,2,128]{2,1,0:T(2,128)S(1)}, u32[]{:S(2)}, u32[]{:S(2)}) collective-permute-start(f32[2,2,128]{2,1,0:T(2,128)S(1)} %maximum_select_fusion), channel_id=1, source_target_pairs={{0,24},{1,25},{2,26},{3,27},{4,28},{5,29},{6,30},{7,31},{8,32},{9,... | collective-permute-start | bytes 6152 | tf_op jit(solution)/shard_map/gains/ppermute | solution.py:433
  294.4 6.2 %collective-permute-start.26 = (f32[2,2,128]{2,1,0:T(2,128)S(1)}, f32[2,2,128]{2,1,0:T(2,128)S(1)}, u32[]{:S(2)}, u32[]{:S(2)}) collective-permute-start(f32[2,2,128]{2,1,0:T(2,128)S(1)} %maximum_select_fusion), channel_id=1, source_target_pairs={{0,16},{1,17},{2,18},{3,19},{4,20},{5,21},{6,22},{7,23},{8,24},{9,... | collective-permute-start | bytes 6152 | tf_op jit(solution)/shard_map/gains/ppermute | solution.py:433
  298.1 5.2 %collective-permute-start.27 = (f32[2,2,128]{2,1,0:T(2,128)S(1)}, f32[2,2,128]{2,1,0:T(2,128)S(1)}, u32[]{:S(2)}, u32[]{:S(2)}) collective-permute-start(f32[2,2,128]{2,1,0:T(2,128)S(1)} %maximum_select_fusion), channel_id=1, source_target_pairs={{0,8},{1,9},{2,10},{3,11},{4,12},{5,13},{6,14},{7,15},{8,16},{9,17... | collective-permute-start | bytes 6152 | tf_op jit(solution)/shard_map/gains/ppermute | solution.py:433

commit v5 on v4

--- a/solution.py
+++ b/solution.py
@@ -100,7 +100,8 @@
         inverse = 1.0 / total
         weights = [(e * inverse).astype(jnp.bfloat16) for e in exps]
         attended = dot(jnp.concatenate(weights, axis=1), values, NN).astype(jnp.bfloat16)
-        og_ref[g >> 1, 0, g & 1] = attended
+        row = pl.multiple_of(((g >> 1) & 1) * 512 + (g & 1) * 128, 128)
+        og_ref[g >> 2, pl.ds(row, 128)] = attended
         inner = jnp.sum(grad.astype(jnp.float32) * attended.astype(jnp.float32), axis=-1, keepdims=True)
         return g, spots, wide, grad, scale, hat, normed, keys, values, weights, inner
 
@@ -120,7 +121,8 @@
         gain_query_ref[0:1, :] += jnp.sum(norm_grad * hat, axis=0, keepdims=True)
         weighted = norm_grad * gain_query
         mean = jnp.mean(weighted * wide, axis=-1, keepdims=True)
-        og_ref[g >> 1, 1, g & 1] = (scale * weighted - wide * (scale * scale * scale) * mean).astype(jnp.bfloat16)
+        row = pl.multiple_of(((g >> 1) & 1) * 512 + (g & 1) * 128 + 256, 128)
+        og_ref[g >> 2, pl.ds(row, 128)] = (scale * weighted - wide * (scale * scale * scale) * mean).astype(jnp.bfloat16)
 
     start = 0
     for which, most in enumerate(BUCKETS):
@@ -134,7 +136,8 @@
 
         start = stop
 
-    back = [pltpu.make_async_copy(og_ref, og_hbm, out_sems.at[8])]
+    rows = pl.ds(0, 1024)
+    back = [pltpu.make_async_copy(og_ref.at[:, rows], og_hbm.at[:, rows], out_sems.at[8])]
     back[0].start()
     for i in SEND_ORDER:
 
@@ -149,7 +152,17 @@
 
         back.append(pltpu.make_async_copy(stage.at[i], parts[i], out_sems.at[i]))
         back[-1].start()
-    gain_key_ref[0:1, :] = gain_key_ref[0:1, :] / gain_key
+    split = []
+    for wide in (gain_query_ref[0:1, :], gain_key_ref[0:1, :] / gain_key):
+        for _ in range(3):
+            split.append(wide.astype(jnp.bfloat16).astype(jnp.float32))
+            wide = wide - split[-1]
+    split = jnp.concatenate(split + [jnp.zeros((10, 128), jnp.float32)], axis=0).astype(jnp.bfloat16)
+    for z in range(8):
+        og_ref[z, 1024:1040] = split
+    rows = pl.ds(1024, 16)
+    back.append(pltpu.make_async_copy(og_ref.at[:, rows], og_hbm.at[:, rows], out_sems.at[9]))
+    back[-1].start()
     for copy in back:
         copy.wait()
 
@@ -159,22 +172,23 @@
     vmem = pl.BlockSpec(memory_space=pltpu.VMEM)
     hbm = pl.BlockSpec(memory_space=pl.ANY)
     part = jax.ShapeDtypeStruct((2, 16, 128, 128), jnp.bfloat16)
-    row = jax.ShapeDtypeStruct((8, 128), jnp.float32)
     return pl.pallas_call(
         attend_kernel,
-        out_shape=(jax.ShapeDtypeStruct((16, 2, 2, 128, 128), jnp.bfloat16),) + (part,) * 8 + (row, row),
+        out_shape=(jax.ShapeDtypeStruct((8, 1040, 128), jnp.bfloat16),) + (part,) * 8,
         in_specs=[smem] * 3 + [hbm] * 9 + [vmem] * 2,
-        out_specs=(hbm,) * 9 + (vmem,) * 2,
+        out_specs=(hbm,) * 9,
         scratch_shapes=[
+            pltpu.VMEM((8, 128), jnp.float32),
+            pltpu.VMEM((8, 128), jnp.float32),
             pltpu.VMEM((128, 128, 128), jnp.bfloat16),
             pltpu.VMEM((128, 128, 128), jnp.bfloat16),
             pltpu.VMEM((128, 128, 256), jnp.float32),
             pltpu.VMEM((16, 2, 2, 128, 128), jnp.bfloat16),
-            pltpu.VMEM((16, 2, 2, 128, 128), jnp.bfloat16),
+            pltpu.VMEM((8, 1040, 128), jnp.bfloat16),
             pltpu.VMEM((8, 2, 16, 128, 128), jnp.bfloat16),
             pltpu.SMEM((GROUPS,), jnp.int32),
             pltpu.SemaphoreType.DMA((17,)),
-            pltpu.SemaphoreType.DMA((9,)),
+            pltpu.SemaphoreType.DMA((10,)),
         ],
         compiler_params=pltpu.CompilerParams(vmem_limit_bytes=56 * 1024 * 1024),
         cost_estimate=pl.CostEstimate(flops=6 * 10**9, bytes_accessed=20 * 2**20, transcendentals=4 * 2**20),
@@ -242,8 +256,8 @@
 
 def unpack_front_kernel(mine_ref, in_ref, got_ref, a_ref, b_ref, buf, in_sems, out_sems):
     half = mine_ref[0]
-    staged([([(in_ref.at[z, 0, i], buf.at[i, :, columns(2 * z + half)]) for i in range(2)]
-             + [(got_ref.at[z, i], buf.at[i, :, columns(2 * z + 1 - half)]) for i in range(2)],
+    staged([([(in_ref.at[z, pl.ds(i * 256, 256)], buf.at[i, :, columns(2 * z + half)]) for i in range(2)]
+             + [(got_ref.at[z, pl.ds(i * 256, 256)], buf.at[i, :, columns(2 * z + 1 - half)]) for i in range(2)],
              [(buf.at[i, :, plane_columns(z)], ref.at[:, plane_columns(z)]) for i, ref in enumerate((a_ref, b_ref))])
             for z in range(8)], in_sems, out_sems)
 
@@ -262,7 +276,7 @@
             pltpu.SemaphoreType.DMA((32,)),
             pltpu.SemaphoreType.DMA((16,)),
         ],
-        compiler_params=pltpu.CompilerParams(vmem_limit_bytes=24 * 1024 * 1024),
+        compiler_params=pltpu.CompilerParams(vmem_limit_bytes=56 * 1024 * 1024),
         cost_estimate=pl.CostEstimate(flops=0, bytes_accessed=2**22, transcendentals=0),
         name=name,
     )(*args)
@@ -304,7 +318,7 @@
             pltpu.SemaphoreType.DMA((8,)),
             pltpu.SemaphoreType.DMA((32,)),
         ],
-        compiler_params=pltpu.CompilerParams(vmem_limit_bytes=24 * 1024 * 1024),
+        compiler_params=pltpu.CompilerParams(vmem_limit_bytes=56 * 1024 * 1024),
         cost_estimate=pl.CostEstimate(flops=10**7, bytes_accessed=2**22, transcendentals=2**13),
         name="norm",
     )(mine, kv, gain)
@@ -358,7 +372,7 @@
             pltpu.SemaphoreType.DMA((40,)),
             pltpu.SemaphoreType.DMA((8,)),
         ],
-        compiler_params=pltpu.CompilerParams(vmem_limit_bytes=24 * 1024 * 1024),
+        compiler_params=pltpu.CompilerParams(vmem_limit_bytes=56 * 1024 * 1024),
         cost_estimate=pl.CostEstimate(flops=10**7, bytes_accessed=2**23, transcendentals=2**13),
         name="finish",
     )(mine, part, core, side, far, kv, gain)
@@ -376,12 +390,10 @@
     return functools.reduce(jnp.add, [a.astype(jnp.float32) for a in arrays]).astype(jnp.bfloat16)
 
 
-def over_copies(row):
-    for flip in (1, 2):
-        row = row + lax.ppermute(row, "dp", [(i, i ^ flip) for i in range(4)])
-    for flip in (1, 2):
-        row = row + across(row, flip)
-    return row
+def over_four(array, axis, step):
+    size = lax.axis_size(axis)
+    one, two, three = [lax.ppermute(array, axis, [(i, i ^ (step * f)) for i in range(size)]) for f in (1, 2, 3)]
+    return (array + one) + (two + three)
 
 
 def body(query_rows, key_rows, value_rows, output_grad, query_gain, key_gain, block_list, block_count):
@@ -410,34 +422,31 @@
         pieces = [p.reshape(2, 16, 128, 128) for p in pieces]
     with jax.named_scope("attend"):
         outs = attend(info, counts, lists, pieces, query_pair.reshape(16, 2, 2, 128, 128), query_gain, key_gain)
-    front, parts, query_row, key_row = outs[0], outs[1:9], outs[9], outs[10]
+    front, parts = outs[0], outs[1:9]
     with jax.named_scope("return"):
         far = wide_sum(parts[4], across(parts[5], 1))
         side = wide_sum(parts[2], across(parts[3], 1))
         far = across(far, 2)
         front, side = lax.optimization_barrier((front, side))
-        front = along_z(front.reshape(8, 2, 2, 256, HEAD_DIM))
+        front = along_z(front)
+        far, side = lax.optimization_barrier((far, side))
         side = across(side, 2)
         cross = across(wide_sum(parts[6], across(parts[7], 1), far), 6)
         core = across(parts[1], 1)
         shape = (2, 8, 256, HEAD_DIM)
         kv_grad = finish(mine, parts[0].reshape(shape), core.reshape(shape), side.reshape(shape), cross.reshape(shape), kv, key_gain)
     with jax.named_scope("gains"):
-        rows = over_copies(jnp.concatenate([query_row[0:1], key_row[0:1]]))
+        front, kv_grad = lax.optimization_barrier((front, kv_grad))
+        rows = jnp.sum(front[:, 1024:1030].astype(jnp.float32).reshape(8, 2, 3, HEAD_DIM), axis=2)
+        rows = over_four(rows, "seq", 1)
         other = across(rows, 4)
-        rows = jnp.where(half == 0, jnp.stack([rows, other]), jnp.stack([other, rows]))
-        rows, kv_grad = lax.optimization_barrier((rows, kv_grad))
-        index = jnp.arange(8, dtype=jnp.int32)[:, None, None, None]
-        table = jnp.where(index == plane, rows[None], 0.0)
-        for d in range(1, 8):
-            came = lax.ppermute(rows, "seq", [(i, (i + 8 * d) % 64) for i in range(64)])
-            table = jnp.where(index == (plane - d) % 8, came[None], table)
-        table = table.reshape(HEADS, 2, HEAD_DIM)
+        rows = jnp.stack([jnp.where(half == 0, rows, other), jnp.where(half == 0, other, rows)], axis=1)
+        rows = over_four(rows, "dp", 1).reshape(HEADS, 2, HEAD_DIM)
     with jax.named_scope("return"):
-        got = across(front[:, 1], 6)
+        got = across(front[:, 512:1024], 6)
         attended, query_grad = mover(unpack_front_kernel, "unpack_front", (ROWS, ROWS), mine, front, got)
         key_grad, value_grad = mover(unpack_kernel, "unpack", (ROWS, ROWS), along_z(kv_grad))
-    return (attended[None], query_grad[None], key_grad[None], value_grad[None], table[:, 0], table[:, 1])
+    return (attended[None], query_grad[None], key_grad[None], value_grad[None], rows[:, 0], rows[:, 1])
 
 
 def solution(mesh):

time: 311 us -> 294 us (0.945)
  local copies, waits for them, and re-layouts: 19.3 us -> 8.91 us
  starting transfers between devices: 59.4 us -> 49.1 us
  waiting for transfers between devices: 161 us -> 168 us
    ppermute x9 -> x6, waiting for transfers between devices: 42.1 us -> 3.58 us  [over_four(): lax.ppermute(array, axis, [(i, i ^ step * f) for i in range(size)])]
    ppermute x19 -> x17, waiting for transfers between devices: 102 us -> 128 us  [across(): return lax.ppermute(array, 'seq', [(i, i ^ flip) for i in range(64)])]
    all_to_all x4, waiting for transfers between devices: 16.5 us -> 36.7 us  [along_z(): lax.all_to_all(array, 'seq', split_axis=0, concat_axis=0, axis_index_grou...]
    ppermute x9 -> x6, starting transfers between devices: 17.6 us -> 6.74 us  [over_four(): lax.ppermute(array, axis, [(i, i ^ step * f) for i in range(size)])]
    unnamed x42 -> x34, local copies, waits for them, and re-layouts: 11.6 us -> 5.23 us
    pallas_call x1, Pallas kernels: 41.3 us -> 35.8 us  [attend(): pl.pallas_call(attend_kernel, out_shape=(jax.ShapeDtypeStruct((8, 1040, 1...]
    all_to_all x4, starting transfers between devices: 25.6 us -> 31.1 us  [along_z(): lax.all_to_all(array, 'seq', split_axis=0, concat_axis=0, axis_index_grou...]
    ppermute x19 -> x17, starting transfers between devices: 16.2 us -> 11.3 us  [across(): return lax.ppermute(array, 'seq', [(i, i ^ flip) for i in range(64)])]
  transfers between devices with their start and end apart: 32 -> 27, of which waited for: 17 -> 17; matrix products, arithmetic and copies ran while one was open for 5% -> 3% of each run, Pallas kernels for 6% -> 6%
where the time goes in v5:
time: 294 us; the launch traced here: 293 us
  waiting for transfers between devices  168 us (57%)
  Pallas kernels  59.8 us (20%)
  starting transfers between devices  49.1 us (17%)
  local copies, waits for them, and re-layouts  8.91 us (3%)
  other arithmetic  5.56 us (2%)
    ppermute x17, waiting for transfers between devices, across(): return lax.ppermute(array, 'seq', [(i, i ^ flip) for i in range(64)])  128 us
    all_to_all x4, waiting for transfers between devices, along_z(): lax.all_to_all(array, 'seq', split_axis=0, concat_axis=0, axis_index_grou...  36.7 us
    pallas_call x1, Pallas kernels, attend(): pl.pallas_call(attend_kernel, out_shape=(jax.ShapeDtypeStruct((8, 1040, 1...  35.8 us
    all_to_all x4, starting transfers between devices, along_z(): lax.all_to_all(array, 'seq', split_axis=0, concat_axis=0, axis_index_grou...  31.1 us
    pallas_call x5, Pallas kernels, mover(): pl.pallas_call(kernel, out_shape=out_shape, in_specs=[smem if a.dtype ==...  15.3 us
    ppermute x17, starting transfers between devices, across(): return lax.ppermute(array, 'seq', [(i, i ^ flip) for i in range(64)])  11.3 us
    ppermute x6, starting transfers between devices, over_four(): lax.ppermute(array, axis, [(i, i ^ step * f) for i in range(size)])  6.74 us
  transfers between devices with their start and end apart: 27, of which 17 were waited for; matrix products, arithmetic and copies ran while one was open for 3% of the time, Pallas kernels for 6%

profile of v5, /device:TPU:16, one launch (start us, length us, event | category | flops | bytes accessed | tf_op | source)
XLA Modules:
  0.0 292.8 jit_solution(11133600674229552982)
XLA Ops:
  0.6 2.8 pack.1
  3.4 8.5 %all-to-all-start = ((bf16[8,2,2,256,128]{4,3,2,1,0:T(8,128)(2,1)}), bf16[8,2,2,256,128]{4,3,2,1,0:T(8,128)(2,1)S(1)}, u32[]{:S(2)}, u32[]{:S(2)}) async-start(bf16[8,2,2,256,128]{4,3,2,1,0:T(8,128)(2,1)} %pack.1), calls=%async_computation | async-start | bytes 4194304 | tf_op jit(solution)/shard_map/gather/all_to_all | solution.py:382
  11.9 0.7 pad_add_fusion.mine_ref
  12.6 3.0 %give.1 = bf16[8,2,256,128]{3,2,1,0:T(8,128)(2,1)} custom-call(s32[2]{0:T(128)} %pad_add_fusion.mine_ref, bf16[256,2048]{1,0:T(8,128)(2,1)} %bitcast.39, bf16[256,2048]{1,0:T(8,128)(2,1)} %bitcast.41), custom_call_target="tpu_custom_call" | custom-call | bytes 4194304 | tf_op jit(solution)/shard_map/gather/give/pallas_call | solution.py:269
  15.6 2.8 collective-permute-start
  18.5 0.1 copy.18
  18.6 0.7 reshape.70.list_ref
  19.2 1.2 dynamic-slice_bitcast_fusion.count_ref
  20.5 0.6 pad_add_fusion.1.info_ref
  21.1 20.7 %collective-permute-done.got_ref = bf16[8,2,256,128]{3,2,1,0:T(8,128)(2,1)S(1)} collective-permute-done((bf16[8,2,256,128]{3,2,1,0:T(8,128)(2,1)}, bf16[8,2,256,128]{3,2,1,0:T(8,128)(2,1)S(1)}, u32[]{:S(2)}, u32[]{:S(2)}) %collective-permute-start) | collective-permute-done | bytes 1048608 | tf_op jit(solution)/shard_map/gather/ppermute | solution.py:386
  41.7 1.0 copy-done.8
  42.7 3.4 %pack_pair.1 = bf16[8,2,2,256,128]{4,3,2,1,0:T(8,128)(2,1)} custom-call(s32[2]{0:T(128)} %pad_add_fusion.mine_ref, bf16[256,2048]{1,0:T(8,128)(2,1)} %bitcast.40, bf16[256,2048]{1,0:T(8,128)(2,1)} %bitcast.42, bf16[8,2,256,128]{3,2,1,0:T(8,128)(2,1)} %copy-done.8), custom_call_target="tpu_custom_call" | custom-call | bytes 4194304 | tf_op jit(solution)/shard_map/gather/pack_pair/pallas_call | solution.py:269
  46.1 17.0 %all-to-all-done.kv_hbm = bf16[8,2,2,256,128]{4,3,2,1,0:T(8,128)(2,1)S(1)} async-done(((bf16[8,2,2,256,128]{4,3,2,1,0:T(8,128)(2,1)}), bf16[8,2,2,256,128]{4,3,2,1,0:T(8,128)(2,1)S(1)}, u32[]{:S(2)}, u32[]{:S(2)}) %all-to-all-start) | async-done | bytes 2097184 | tf_op jit(solution)/shard_map/gather/all_to_all | solution.py:382
  63.1 4.4 %all-to-all-start.1 = ((bf16[8,2,2,256,128]{4,3,2,1,0:T(8,128)(2,1)}), bf16[8,2,2,256,128]{4,3,2,1,0:T(8,128)(2,1)}, u32[]{:S(2)}, u32[]{:S(2)}) async-start(bf16[8,2,2,256,128]{4,3,2,1,0:T(8,128)(2,1)} %pack_pair.1), calls=%async_computation.1 | async-start | bytes 4194304 | tf_op jit(solution)/shard_map/gather/all_to_all | solution.py:382
  67.5 3.9 %norm.1 = (bf16[2,8,256,128]{3,2,1,0:T(8,128)(2,1)}, bf16[2,8,256,128]{3,2,1,0:T(8,128)(2,1)}) custom-call(s32[2]{0:T(128)} %pad_add_fusion.mine_ref, bf16[8,2,2,256,128]{4,3,2,1,0:T(8,128)(2,1)} %copy-done.1, f32[16,128]{1,0:T(8,128)} %gain_ref.3), custom_call_target="tpu_custom_call" | custom-call | flops 10000000 | bytes 4194304 | tf_op jit(solution)/shard_map/gather/norm/pallas_call | solution.py:310
  71.4 2.8 collective-permute-start.4
  74.3 0.2 collective-permute-start.2
  74.5 20.5 %collective-permute-done.4 = bf16[2,8,256,128]{3,2,1,0:T(8,128)(2,1)S(1)} collective-permute-done((bf16[2,8,256,128]{3,2,1,0:T(8,128)(2,1)}, bf16[2,8,256,128]{3,2,1,0:T(8,128)(2,1)S(1)}, u32[]{:S(2)}, u32[]{:S(2)}) %collective-permute-start.4) | collective-permute-done | bytes 1048608 | tf_op jit(solution)/shard_map/gather/ppermute | solution.py:386
  95.0 0.3 collective-permute-start.5
  95.3 0.5 collective-permute-start.7
  95.8 3.0 %collective-permute-done.2 = bf16[2,8,256,128]{3,2,1,0:T(8,128)(2,1)S(1)} collective-permute-done((bf16[2,8,256,128]{3,2,1,0:T(8,128)(2,1)}, bf16[2,8,256,128]{3,2,1,0:T(8,128)(2,1)S(1)}, u32[]{:S(2)}, u32[]{:S(2)}) %collective-permute-start.2) | collective-permute-done | bytes 1048608 | tf_op jit(solution)/shard_map/gather/ppermute | solution.py:386
  98.8 19.9 %collective-permute-done.5 = bf16[2,8,256,128]{3,2,1,0:T(8,128)(2,1)S(1)} collective-permute-done((bf16[2,8,256,128]{3,2,1,0:T(8,128)(2,1)S(1)}, bf16[2,8,256,128]{3,2,1,0:T(8,128)(2,1)S(1)}, u32[]{:S(2)}, u32[]{:S(2)}) %collective-permute-start.5) | collective-permute-done | bytes 1048608 | tf_op jit(solution)/shard_map/gather/ppermute | solution.py:386
  118.8 1.0 copy-done.14
  119.8 0.3 copy-done.15
  120.1 1.0 copy-done.16
  121.1 0.5 collective-permute-done.6
  121.6 35.8 %attend.1 = (bf16[8,1040,128]{2,1,0:T(8,128)(2,1)}, bf16[2,16,128,128]{3,2,1,0:T(8,128)(2,1)}, bf16[2,16,128,128]{3,2,1,0:T(8,128)(2,1)}, bf16[2,16,128,128]{3,2...) custom-call(s32[2]{0:T(128)} %pad_add_fusion.1.info_ref, ...), custom_call_target="tpu_custom_call" | custom-call | flops 6000000000 | bytes 20971520 | tf_op jit(solution)/shard_map/attend/attend/pallas_call | solution.py:175
  157.5 0.5 collective-permute-start.10
  158.0 2.9 collective-permute-done.8
  160.9 1.6 add_convert_fusion.2
  162.5 11.6 %all-to-all-start.2 = ((bf16[8,1040,128]{2,1,0:T(8,128)(2,1)}), bf16[8,1040,128]{2,1,0:T(8,128)(2,1)S(1)}, u32[]{:S(2)}, u32[]{:S(2)}) async-start(bf16[8,1040,128]{2,1,0:T(8,128)(2,1)} %get-tuple-element.42), calls=%async_computation.2 | async-start | bytes 4259840 | tf_op jit(solution)/shard_map/return/all_to_all | solution.py:382
  174.1 2.1 add_convert_fusion.1
  176.3 0.3 collective-permute-start.11
  176.6 0.1 collective-permute-start.13
  176.8 0.4 collective-permute-start.9
  177.2 24.5 %collective-permute-done.11 = bf16[2,16,128,128]{3,2,1,0:T(8,128)(2,1)S(1)} collective-permute-done((bf16[2,16,128,128]{3,2,1,0:T(8,128)(2,1)S(1)}, bf16[2,16,128,128]{3,2,1,0:T(8,128)(2,1)S(1)}, u32[]{:S(2)}, u32[]{:S(2)}) %collective-permute-start.11) | collective-permute-done | bytes 1048608 | tf_op jit(solution)/shard_map/return/ppermute | solution.py:386
  201.7 0.3 collective-permute-start.12
  202.0 0.5 add_convert_fusion
  202.5 0.1 collective-permute-start.14
  202.6 23.4 %collective-permute-done.12 = bf16[2,16,128,128]{3,2,1,0:T(8,128)(2,1)S(1)} collective-permute-done((bf16[2,16,128,128]{3,2,1,0:T(8,128)(2,1)S(1)}, bf16[2,16,128,128]{3,2,1,0:T(8,128)(2,1)S(1)}, u32[]{:S(2)}, u32[]{:S(2)}) %collective-permute-start.12) | collective-permute-done | bytes 1048608 | tf_op jit(solution)/shard_map/return/ppermute | solution.py:386
  226.0 2.1 collective-permute-done.14
  228.1 1.0 copy-done.5
  229.0 4.8 %finish.1 = bf16[8,2,2,256,128]{4,3,2,1,0:T(8,128)(2,1)} custom-call(s32[2]{0:T(128)} %pad_add_fusion.mine_ref, bf16[2,8,256,128]{3,2,1,0:T(8,128)(2,1)} %bitcast.43, bf16[2,8,256,128]{3,2,1,0:T(8,128)(2,1)} %bitcast.44, bf16[2,8,256,128]{3,2,1,0:T(8,128)(2,1)} %bitcast.45, bf16[2,8,256,128]{3,2,1,0:T(8,128)(2,1)} %bitcast.46, ...), custom_call_target="tpu_custom_call" | custom-call | flops 10000000 | bytes 8388608 | tf_op jit(solution)/shard_map/return/finish/pallas_call | solution.py:363
  233.9 6.6 %all-to-all-start.3 = ((bf16[8,2,2,256,128]{4,3,2,1,0:T(8,128)(2,1)}), bf16[8,2,2,256,128]{4,3,2,1,0:T(8,128)(2,1)}, u32[]{:S(2)}, u32[]{:S(2)}) async-start(bf16[8,2,2,256,128]{4,3,2,1,0:T(8,128)(2,1)} %finish.1), calls=%async_computation.3 | async-start | bytes 4194304 | tf_op jit(solution)/shard_map/return/all_to_all | solution.py:382
  240.5 1.0 slice.12
  241.5 0.3 collective-permute-start.15
  241.8 0.1 collective-permute-start.18
  241.9 0.4 collective-permute-start.17
  242.3 1.5 collective-permute-start.16
  243.8 1.2 collective-permute-done.18
  245.0 0.6 collective-permute-done.17
  245.7 2.5 collective-permute-start.19
  248.1 2.8 collective-permute-done.19
  250.9 0.1 collective-permute-start.21
  251.0 2.6 collective-permute-start.22
  253.7 2.1 collective-permute-start.20
  255.7 0.5 collective-permute-done.21
  256.3 1.2 collective-permute-done.20
  257.5 0.6 slice_bitcast_fusion
  258.1 7.8 %collective-permute-done.15.got_ref = bf16[8,512,128]{2,1,0:T(8,128)(2,1)S(1)} collective-permute-done((bf16[8,512,128]{2,1,0:T(8,128)(2,1)}, bf16[8,512,128]{2,1,0:T(8,128)(2,1)S(1)}, u32[]{:S(2)}, u32[]{:S(2)}) %collective-permute-start.15) | collective-permute-done | bytes 1048608 | tf_op jit(solution)/shard_map/return/ppermute | solution.py:386
  265.9 1.0 copy-done.6
  266.8 3.4 %unpack_front.1 = (bf16[256,2048]{1,0:T(8,128)(2,1)}, bf16[256,2048]{1,0:T(8,128)(2,1)}) custom-call(s32[2]{0:T(128)} %pad_add_fusion.mine_ref, bf16[8,1040,128]{2,1,0:T(8,128)(2,1)} %copy-done.2, bf16[8,512,128]{2,1,0:T(8,128)(2,1)} %copy-done.6), custom_call_target="tpu_custom_call" | custom-call | bytes 4194304 | tf_op jit(solution)/shard_map/return/unpack_front/pallas_call | solution.py:269
  270.2 19.7 %all-to-all-done.3.in_ref = bf16[8,2,2,256,128]{4,3,2,1,0:T(8,128)(2,1)} async-done(((bf16[8,2,2,256,128]{4,3,2,1,0:T(8,128)(2,1)}), bf16[8,2,2,256,128]{4,3,2,1,0:T(8,128)(2,1)}, u32[]{:S(2)}, u32[]{:S(2)}) %all-to-all-start.3) | async-done | bytes 2097184 | tf_op jit(solution)/shard_map/return/all_to_all | solution.py:382
  289.9 2.7 unpack.1
  (50 shorter events, 0.3 us)
Async XLA Ops:
  0.6 17.8 %copy-start = (s32[1,16,128,8]{2,3,1,0:T(8,128)S(1)}, s32[1,16,128,8]{2,3,1,0:T(8,128)}, u32[]{:S(2)}) copy-start(s32[1,16,128,8]{2,3,1,0:T(8,128)} %param.14) | copy-start | bytes 196612
  3.4 59.7 %all-to-all-start = ((bf16[8,2,2,256,128]{4,3,2,1,0:T(8,128)(2,1)}), bf16[8,2,2,256,128]{4,3,2,1,0:T(8,128)(2,1)S(1)}, u32[]{:S(2)}, u32[]{:S(2)}) async-start(bf16[8,2,2,256,128]{4,3,2,1,0:T(8,128)(2,1)} %pack.1), calls=%async_computation | async-start | bytes 4194304 | tf_op jit(solution)/shard_map/gather/all_to_all | solution.py:382
  15.6 26.1 %collective-permute-start = (bf16[8,2,256,128]{3,2,1,0:T(8,128)(2,1)}, bf16[8,2,256,128]{3,2,1,0:T(8,128)(2,1)S(1)}, u32[]{:S(2)}, u32[]{:S(2)}) collective-permute-start(bf16[8,2,256,128]{3,2,1,0:T(8,128)(2,1)} %give.1), channel_id=1, source_target_pairs={{0,6},{1,7},{2,4},{3,5},{4,2},{5,3},{6,0},{7,1},{8,14},{9,15},{10,... | collective-permute-start | bytes 3145736 | tf_op jit(solution)/shard_map/gather/ppermute | solution.py:386
  41.7 1.0 copy-start.8
  63.1 4.4 %copy-start.1 = (bf16[8,2,2,256,128]{4,3,2,1,0:T(8,128)(2,1)}, bf16[8,2,2,256,128]{4,3,2,1,0:T(8,128)(2,1)S(1)}, u32[]{:S(2)}) copy-start(bf16[8,2,2,256,128]{4,3,2,1,0:T(8,128)(2,1)S(1)} %all-to-all-done.kv_hbm) | copy-start | bytes 6291460
  63.1 58.4 %all-to-all-start.1 = ((bf16[8,2,2,256,128]{4,3,2,1,0:T(8,128)(2,1)}), bf16[8,2,2,256,128]{4,3,2,1,0:T(8,128)(2,1)}, u32[]{:S(2)}, u32[]{:S(2)}) async-start(bf16[8,2,2,256,128]{4,3,2,1,0:T(8,128)(2,1)} %pack_pair.1), calls=%async_computation.1 | async-start | bytes 4194304 | tf_op jit(solution)/shard_map/gather/all_to_all | solution.py:382
  71.4 23.6 %collective-permute-start.4 = (bf16[2,8,256,128]{3,2,1,0:T(8,128)(2,1)}, bf16[2,8,256,128]{3,2,1,0:T(8,128)(2,1)S(1)}, u32[]{:S(2)}, u32[]{:S(2)}) collective-permute-start(bf16[2,8,256,128]{3,2,1,0:T(8,128)(2,1)} %get-tuple-element.37), channel_id=1, source_target_pairs={{0,6},{1,7},{2,4},{3,5},{4,2},{5,3},{6,0},{7,1},{8,14},{9,15},{10,... | collective-permute-start | bytes 3145736 | tf_op jit(solution)/shard_map/gather/ppermute | solution.py:386
  74.3 24.5 %collective-permute-start.2 = (bf16[2,8,256,128]{3,2,1,0:T(8,128)(2,1)}, bf16[2,8,256,128]{3,2,1,0:T(8,128)(2,1)S(1)}, u32[]{:S(2)}, u32[]{:S(2)}) collective-permute-start(bf16[2,8,256,128]{3,2,1,0:T(8,128)(2,1)} %get-tuple-element.36), channel_id=1, source_target_pairs={{0,2},{1,3},{2,0},{3,1},{4,6},{5,7},{6,4},{7,5},{8,10},{9,11},{10,... | collective-permute-start | bytes 3145736 | tf_op jit(solution)/shard_map/gather/ppermute | solution.py:386
  95.0 26.5 %copy-start.10 = (bf16[2,8,256,128]{3,2,1,0:T(8,128)(2,1)}, bf16[2,8,256,128]{3,2,1,0:T(8,128)(2,1)S(1)}, u32[]{:S(2)}) copy-start(bf16[2,8,256,128]{3,2,1,0:T(8,128)(2,1)S(1)} %collective-permute-done.4) | copy-start | bytes 3145732
  95.0 23.7 %collective-permute-start.5 = (bf16[2,8,256,128]{3,2,1,0:T(8,128)(2,1)S(1)}, bf16[2,8,256,128]{3,2,1,0:T(8,128)(2,1)S(1)}, u32[]{:S(2)}, u32[]{:S(2)}) collective-permute-start(bf16[2,8,256,128]{3,2,1,0:T(8,128)(2,1)S(1)} %collective-permute-done.4), channel_id=1, source_target_pairs={{0,2},{1,3},{2,0},{3,1},{4,6},{5,7},{6,4},{7,5},{8,10},{9,11},{10,... | collective-permute-start | bytes 3145736 | tf_op jit(solution)/shard_map/gather/ppermute | solution.py:386
  95.3 23.5 %collective-permute-start.1 = (bf16[2,8,256,128]{3,2,1,0:T(8,128)(2,1)}, bf16[2,8,256,128]{3,2,1,0:T(8,128)(2,1)S(1)}, u32[]{:S(2)}, u32[]{:S(2)}) collective-permute-start(bf16[2,8,256,128]{3,2,1,0:T(8,128)(2,1)} %get-tuple-element.36), channel_id=1, source_target_pairs={{0,1},{1,0},{2,3},{3,2},{4,5},{5,4},{6,7},{7,6},{8,9},{9,8},{10,11... | collective-permute-start | bytes 3145736 | tf_op jit(solution)/shard_map/gather/ppermute | solution.py:386
  95.3 23.5 %collective-permute-start.7 = (bf16[2,8,256,128]{3,2,1,0:T(8,128)(2,1)S(1)}, bf16[2,8,256,128]{3,2,1,0:T(8,128)(2,1)S(1)}, u32[]{:S(2)}, u32[]{:S(2)}) collective-permute-start(bf16[2,8,256,128]{3,2,1,0:T(8,128)(2,1)S(1)} %collective-permute-done.4), channel_id=1, source_target_pairs={{0,1},{1,0},{2,3},{3,2},{4,5},{5,4},{6,7},{7,6},{8,9},{9,8},{10,11... | collective-permute-start | bytes 3145736 | tf_op jit(solution)/shard_map/gather/ppermute | solution.py:386
  98.8 22.8 %copy-start.12 = (bf16[2,8,256,128]{3,2,1,0:T(8,128)(2,1)}, bf16[2,8,256,128]{3,2,1,0:T(8,128)(2,1)S(1)}, u32[]{:S(2)}) copy-start(bf16[2,8,256,128]{3,2,1,0:T(8,128)(2,1)S(1)} %collective-permute-done.2) | copy-start | bytes 3145732
  98.8 20.0 %collective-permute-start.3 = (bf16[2,8,256,128]{3,2,1,0:T(8,128)(2,1)S(1)}, bf16[2,8,256,128]{3,2,1,0:T(8,128)(2,1)S(1)}, u32[]{:S(2)}, u32[]{:S(2)}) collective-permute-start(bf16[2,8,256,128]{3,2,1,0:T(8,128)(2,1)S(1)} %collective-permute-done.2), channel_id=1, source_target_pairs={{0,1},{1,0},{2,3},{3,2},{4,5},{5,4},{6,7},{7,6},{8,9},{9,8},{10,11... | collective-permute-start | bytes 3145736 | tf_op jit(solution)/shard_map/gather/ppermute | solution.py:386
  118.8 2.8 copy-start.13
  118.8 2.8 collective-permute-start.6
  118.8 1.0 copy-start.14
  118.8 1.3 copy-start.15
  120.1 1.0 copy-start.16
  157.4 3.5 %collective-permute-start.8 = (bf16[2,16,128,128]{3,2,1,0:T(8,128)(2,1)}, bf16[2,16,128,128]{3,2,1,0:T(8,128)(2,1)S(1)}, u32[]{:S(2)}, u32[]{:S(2)}) collective-permute-start(bf16[2,16,128,128]{3,2,1,0:T(8,128)(2,1)} %get-tuple-element.41), channel_id=1, source_target_pairs={{0,1},{1,0},{2,3},{3,2},{4,5},{5,4},{6,7},{7,6},{8,9},{9,8},{10,11... | collective-permute-start | bytes 3145736 | tf_op jit(solution)/shard_map/return/ppermute | solution.py:386
  157.5 16.6 %collective-permute-start.10 = (bf16[2,16,128,128]{3,2,1,0:T(8,128)(2,1)}, bf16[2,16,128,128]{3,2,1,0:T(8,128)(2,1)}, u32[]{:S(2)}, u32[]{:S(2)}) collective-permute-start(bf16[2,16,128,128]{3,2,1,0:T(8,128)(2,1)} %get-tuple-element.46), channel_id=1, source_target_pairs={{0,1},{1,0},{2,3},{3,2},{4,5},{5,4},{6,7},{7,6},{8,9},{9,8},{10,11... | collective-permute-start | bytes 3145736 | tf_op jit(solution)/shard_map/return/ppermute | solution.py:386
  162.5 71.4 %all-to-all-start.2 = ((bf16[8,1040,128]{2,1,0:T(8,128)(2,1)}), bf16[8,1040,128]{2,1,0:T(8,128)(2,1)S(1)}, u32[]{:S(2)}, u32[]{:S(2)}) async-start(bf16[8,1040,128]{2,1,0:T(8,128)(2,1)} %get-tuple-element.42), calls=%async_computation.2 | async-start | bytes 4259840 | tf_op jit(solution)/shard_map/return/all_to_all | solution.py:382
  174.1 2.5 copy-start.11
  174.1 2.6 copy-start.9
  174.1 27.9 %copy-start.7 = (bf16[2,16,128,128]{3,2,1,0:T(8,128)(2,1)S(1)}, bf16[2,16,128,128]{3,2,1,0:T(8,128)(2,1)}, u32[]{:S(2)}) copy-start(bf16[2,16,128,128]{3,2,1,0:T(8,128)(2,1)} %get-tuple-element.49) | copy-start | bytes 3145732
  176.3 25.4 %collective-permute-start.11 = (bf16[2,16,128,128]{3,2,1,0:T(8,128)(2,1)S(1)}, bf16[2,16,128,128]{3,2,1,0:T(8,128)(2,1)S(1)}, u32[]{:S(2)}, u32[]{:S(2)}) collective-permute-start(bf16[2,16,128,128]{3,2,1,0:T(8,128)(2,1)S(1)} %add_convert_fusion.1), channel_id=1, source_target_pairs={{0,2},{1,3},{2,0},{3,1},{4,6},{5,7},{6,4},{7,5},{8,10},{9,11},{10,... | collective-permute-start | bytes 3145736 | tf_op jit(solution)/shard_map/return/ppermute | solution.py:386
  176.6 25.4 %collective-permute-start.13 = (bf16[2,16,128,128]{3,2,1,0:T(8,128)(2,1)S(1)}, bf16[2,16,128,128]{3,2,1,0:T(8,128)(2,1)S(1)}, u32[]{:S(2)}, u32[]{:S(2)}) collective-permute-start(bf16[2,16,128,128]{3,2,1,0:T(8,128)(2,1)S(1)} %copy-done.11), channel_id=1, source_target_pairs={{0,1},{1,0},{2,3},{3,2},{4,5},{5,4},{6,7},{7,6},{8,9},{9,8},{10,11... | collective-permute-start | bytes 3145736 | tf_op jit(solution)/shard_map/return/ppermute | solution.py:386
  176.8 25.8 %collective-permute-start.9 = (bf16[2,16,128,128]{3,2,1,0:T(8,128)(2,1)S(1)}, bf16[2,16,128,128]{3,2,1,0:T(8,128)(2,1)S(1)}, u32[]{:S(2)}, u32[]{:S(2)}) collective-permute-start(bf16[2,16,128,128]{3,2,1,0:T(8,128)(2,1)S(1)} %copy-done.9), channel_id=1, source_target_pairs={{0,1},{1,0},{2,3},{3,2},{4,5},{5,4},{6,7},{7,6},{8,9},{9,8},{10,11... | collective-permute-start | bytes 3145736 | tf_op jit(solution)/shard_map/return/ppermute | solution.py:386
  201.7 24.3 %collective-permute-start.12 = (bf16[2,16,128,128]{3,2,1,0:T(8,128)(2,1)S(1)}, bf16[2,16,128,128]{3,2,1,0:T(8,128)(2,1)S(1)}, u32[]{:S(2)}, u32[]{:S(2)}) collective-permute-start(bf16[2,16,128,128]{3,2,1,0:T(8,128)(2,1)S(1)} %add_convert_fusion.2), channel_id=1, source_target_pairs={{0,2},{1,3},{2,0},{3,1},{4,6},{5,7},{6,4},{7,5},{8,10},{9,11},{10,... | collective-permute-start | bytes 3145736 | tf_op jit(solution)/shard_map/return/ppermute | solution.py:386
  202.5 25.6 %collective-permute-start.14 = (bf16[2,16,128,128]{3,2,1,0:T(8,128)(2,1)S(1)}, bf16[2,16,128,128]{3,2,1,0:T(8,128)(2,1)S(1)}, u32[]{:S(2)}, u32[]{:S(2)}) collective-permute-start(bf16[2,16,128,128]{3,2,1,0:T(8,128)(2,1)S(1)} %add_convert_fusion), channel_id=1, source_target_pairs={{0,6},{1,7},{2,4},{3,5},{4,2},{5,3},{6,0},{7,1},{8,14},{9,15},{10,... | collective-permute-start | bytes 3145736 | tf_op jit(solution)/shard_map/return/ppermute | solution.py:386
  202.6 25.5 %copy-start.3 = (bf16[2,16,128,128]{3,2,1,0:T(8,128)(2,1)}, bf16[2,16,128,128]{3,2,1,0:T(8,128)(2,1)S(1)}, u32[]{:S(2)}) copy-start(bf16[2,16,128,128]{3,2,1,0:T(8,128)(2,1)S(1)} %collective-permute-done.9) | copy-start | bytes 3145732
  226.0 2.1 copy-start.4
  228.1 1.0 copy-start.5
  233.8 7.9 %copy-start.2 = (bf16[8,1040,128]{2,1,0:T(8,128)(2,1)}, bf16[8,1040,128]{2,1,0:T(8,128)(2,1)S(1)}, u32[]{:S(2)}) copy-start(bf16[8,1040,128]{2,1,0:T(8,128)(2,1)S(1)} %all-to-all-done.2.in_ref) | copy-start | bytes 6389764
  233.9 56.0 %all-to-all-start.3 = ((bf16[8,2,2,256,128]{4,3,2,1,0:T(8,128)(2,1)}), bf16[8,2,2,256,128]{4,3,2,1,0:T(8,128)(2,1)}, u32[]{:S(2)}, u32[]{:S(2)}) async-start(bf16[8,2,2,256,128]{4,3,2,1,0:T(8,128)(2,1)} %finish.1), calls=%async_computation.3 | async-start | bytes 4194304 | tf_op jit(solution)/shard_map/return/all_to_all | solution.py:382
  241.5 24.4 %collective-permute-start.15 = (bf16[8,512,128]{2,1,0:T(8,128)(2,1)}, bf16[8,512,128]{2,1,0:T(8,128)(2,1)S(1)}, u32[]{:S(2)}, u32[]{:S(2)}) collective-permute-start(bf16[8,512,128]{2,1,0:T(8,128)(2,1)} %slice.12), channel_id=1, source_target_pairs={{0,6},{1,7},{2,4},{3,5},{4,2},{5,3},{6,0},{7,1},{8,14},{9,15},{10,... | collective-permute-start | bytes 3145736 | tf_op jit(solution)/shard_map/return/ppermute | solution.py:386
  241.8 3.2 %collective-permute-start.18 = (f32[8,2,128]{2,0,1:T(8,128)S(1)}, f32[8,2,128]{2,0,1:T(8,128)S(1)}, u32[]{:S(2)}, u32[]{:S(2)}) collective-permute-start(f32[8,2,128]{2,0,1:T(8,128)S(1)} %reduce_sum.9), channel_id=1, source_target_pairs={{0,3},{1,2},{2,1},{3,0},{4,7},{5,6},{6,5},{7,4},{8,11},{9,10},{10,... | collective-permute-start | bytes 24584 | tf_op jit(solution)/shard_map/gains/ppermute | solution.py:395
  241.9 3.7 %collective-permute-start.17 = (f32[8,2,128]{2,0,1:T(8,128)S(1)}, f32[8,2,128]{2,0,1:T(8,128)S(1)}, u32[]{:S(2)}, u32[]{:S(2)}) collective-permute-start(f32[8,2,128]{2,0,1:T(8,128)S(1)} %reduce_sum.9), channel_id=1, source_target_pairs={{0,2},{1,3},{2,0},{3,1},{4,6},{5,7},{6,4},{7,5},{8,10},{9,11},{10,... | collective-permute-start | bytes 24584 | tf_op jit(solution)/shard_map/gains/ppermute | solution.py:395
  242.3 3.4 %collective-permute-start.16 = (f32[8,2,128]{2,0,1:T(8,128)S(1)}, f32[8,2,128]{2,0,1:T(8,128)S(1)}, u32[]{:S(2)}, u32[]{:S(2)}) collective-permute-start(f32[8,2,128]{2,0,1:T(8,128)S(1)} %reduce_sum.9), channel_id=1, source_target_pairs={{0,1},{1,0},{2,3},{3,2},{4,5},{5,4},{6,7},{7,6},{8,9},{9,8},{10,11... | collective-permute-start | bytes 24584 | tf_op jit(solution)/shard_map/gains/ppermute | solution.py:395
  245.7 5.3 %collective-permute-start.19 = (f32[8,2,128]{2,0,1:T(8,128)S(1)}, f32[8,2,128]{2,0,1:T(8,128)S(1)}, u32[]{:S(2)}, u32[]{:S(2)}) collective-permute-start(f32[8,2,128]{2,0,1:T(8,128)S(1)} %add_add_fusion.1), channel_id=1, source_target_pairs={{0,4},{1,5},{2,6},{3,7},{4,0},{5,1},{6,2},{7,3},{8,12},{9,13},{10,... | collective-permute-start | bytes 24584 | tf_op jit(solution)/shard_map/gains/ppermute | solution.py:386
  250.9 5.3 %collective-permute-start.21 = (f32[8,2,2,128]{3,1,0,2:T(2,128)S(1)}, f32[8,2,2,128]{3,1,0,2:T(2,128)S(1)}, u32[]{:S(2)}, u32[]{:S(2)}) collective-permute-start(f32[8,2,2,128]{3,1,0,2:T(2,128)S(1)} %pad_maximum_fusion), channel_id=1, source_target_pairs={{0,128},{64,192},{128,0},{192,64},{1,129},{65,193},{129,1},{193,65... | collective-permute-start | bytes 49160 | tf_op jit(solution)/shard_map/gains/ppermute | solution.py:395
  251.0 5.2 %collective-permute-start.22 = (f32[8,2,2,128]{3,1,0,2:T(2,128)S(1)}, f32[8,2,2,128]{3,1,0,2:T(2,128)S(1)}, u32[]{:S(2)}, u32[]{:S(2)}) collective-permute-start(f32[8,2,2,128]{3,1,0,2:T(2,128)S(1)} %pad_maximum_fusion), channel_id=1, source_target_pairs={{0,192},{64,128},{128,64},{192,0},{1,193},{65,129},{129,65},{193,1... | collective-permute-start | bytes 49160 | tf_op jit(solution)/shard_map/gains/ppermute | solution.py:395
  253.7 3.8 %collective-permute-start.20 = (f32[8,2,2,128]{3,1,0,2:T(2,128)S(1)}, f32[8,2,2,128]{3,1,0,2:T(2,128)S(1)}, u32[]{:S(2)}, u32[]{:S(2)}) collective-permute-start(f32[8,2,2,128]{3,1,0,2:T(2,128)S(1)} %pad_maximum_fusion), channel_id=1, source_target_pairs={{0,64},{64,0},{128,192},{192,128},{1,65},{65,1},{129,193},{193,129... | collective-permute-start | bytes 49160 | tf_op jit(solution)/shard_map/gains/ppermute | solution.py:395
  265.8 1.0 copy-start.6

commit v6 on v5

--- a/solution.py
+++ b/solution.py
@@ -17,7 +17,7 @@
 NN = (((1,), (0,)), ((), ()))
 GROUPS = 32
 BUCKETS = (8, 6, 4, 2)
-TOGETHER = 1
+TOGETHER = 4
 SEND_ORDER = (5, 3, 1, 7, 4, 2, 0, 6)
 
 
@@ -74,12 +74,13 @@
 
     zero = jnp.zeros((128, 128), jnp.bfloat16)
 
-    def forward(i, most, first):
+    def group(i, most, first):
         g = order_ref[i]
         block = block_of(g)
         live = count_ref[block]
         listed = [list_ref[block * 8 + j] for j in range(most)]
         spots = [(((c >> 1) & 7) ^ place_x_core) * 16 + (c >> 4) * 2 + (c & 1) for c in listed]
+        row = pl.multiple_of(((g >> 1) & 1) * 512 + (g & 1) * 128, 128)
         wide = qg_ref[g >> 1, 0, g & 1].astype(jnp.float32)
         grad = qg_ref[g >> 1, 1, g & 1]
         scale = lax.rsqrt(jnp.mean(wide * wide, axis=-1, keepdims=True) + EPS)
@@ -87,6 +88,7 @@
         normed = (hat * gain_query).astype(jnp.bfloat16)
         keys = jnp.concatenate([ktab[t] for t in spots], axis=0)
         values = jnp.concatenate([vtab[t] for t in spots], axis=0)
+        yield
         flat = dot(normed, keys, NT)
         scores = []
         for j in range(most):
@@ -94,35 +96,38 @@
             if j == most - 1 or (j and not first):
                 s = jnp.where(j < live, s, -jnp.inf)
             scores.append(s)
+        yield
         top = jnp.max(functools.reduce(jnp.maximum, scores), axis=-1, keepdims=True)
+        yield
         exps = [jnp.exp2((s - top) * (INV_ROOT * LOG2E)) for s in scores]
         total = jnp.sum(functools.reduce(jnp.add, exps), axis=-1, keepdims=True)
+        yield
         inverse = 1.0 / total
         weights = [(e * inverse).astype(jnp.bfloat16) for e in exps]
         attended = dot(jnp.concatenate(weights, axis=1), values, NN).astype(jnp.bfloat16)
-        row = pl.multiple_of(((g >> 1) & 1) * 512 + (g & 1) * 128, 128)
-        og_ref[g >> 2, pl.ds(row, 128)] = attended
+        yield
+        flat = dot(grad, values, NT)
         inner = jnp.sum(grad.astype(jnp.float32) * attended.astype(jnp.float32), axis=-1, keepdims=True)
-        return g, spots, wide, grad, scale, hat, normed, keys, values, weights, inner
-
-    def backward(state, most):
-        g, spots, wide, grad, scale, hat, normed, keys, values, weights, inner = state
-        flat = dot(grad, values, NT)
+        yield
         score_grads = []
         for j in range(most):
             wg = flat[:, j * 128:(j + 1) * 128]
             score_grads.append((weights[j].astype(jnp.float32) * (wg - inner)).astype(jnp.bfloat16))
         norm_grad = dot(jnp.concatenate(score_grads, axis=1), keys, NN) * INV_ROOT
+        yield
         pair = jnp.concatenate(
             [jnp.concatenate([normed, zero], axis=1), jnp.concatenate([zero, grad], axis=1)], axis=0
         )
-        for j in range(most):
-            acc[spots[j]] += dot(jnp.concatenate([score_grads[j], weights[j]], axis=0), pair, TN)
-        gain_query_ref[0:1, :] += jnp.sum(norm_grad * hat, axis=0, keepdims=True)
+        terms = [dot(jnp.concatenate([score_grads[j], weights[j]], axis=0), pair, TN) for j in range(most)]
         weighted = norm_grad * gain_query
         mean = jnp.mean(weighted * wide, axis=-1, keepdims=True)
-        row = pl.multiple_of(((g >> 1) & 1) * 512 + (g & 1) * 128 + 256, 128)
-        og_ref[g >> 2, pl.ds(row, 128)] = (scale * weighted - wide * (scale * scale * scale) * mean).astype(jnp.bfloat16)
+        query_grad = (scale * weighted - wide * (scale * scale * scale) * mean).astype(jnp.bfloat16)
+        yield
+        og_ref[g >> 2, pl.ds(row, 128)] = attended
+        og_ref[g >> 2, pl.ds(row + 256, 128)] = query_grad
+        for j in range(most):
+            acc[spots[j]] += terms[j]
+        gain_query_ref[0:1, :] += jnp.sum(norm_grad * hat, axis=0, keepdims=True)
 
     start = 0
     for which, most in enumerate(BUCKETS):
@@ -130,9 +135,9 @@
 
         @pl.loop(start, stop)
         def _(step, most=most):
-            states = [forward(step * TOGETHER + u, most, u == 0) for u in range(TOGETHER)]
-            for state in states:
-                backward(state, most)
+            running = [group(step * TOGETHER + u, most, u == 0) for u in range(TOGETHER)]
+            while running:
+                running = [one for one in running if next(one, running) is None]
 
         start = stop
 

time: 294 us -> 278 us (0.946)
  Pallas kernels: 59.8 us -> 41.4 us
    pallas_call x1, Pallas kernels: 35.8 us -> 17.4 us  [attend(): pl.pallas_call(attend_kernel, out_shape=(jax.ShapeDtypeStruct((8, 1040, 1...]
  transfers between devices with their start and end apart: 27 -> 27, of which waited for: 17 -> 17; matrix products, arithmetic and copies ran while one was open for 3% -> 3% of each run, Pallas kernels for 6% -> 7%
where the time goes in v6:
time: 278 us; the launch traced here: 276 us
  waiting for transfers between devices  168 us (60%)
  starting transfers between devices  50.9 us (18%)
  Pallas kernels  41.4 us (15%)
  local copies, waits for them, and re-layouts  8.88 us (3%)
  other arithmetic  5.56 us (2%)
    ppermute x17, waiting for transfers between devices, across(): return lax.ppermute(array, 'seq', [(i, i ^ flip) for i in range(64)])  128 us
    all_to_all x4, waiting for transfers between devices, along_z(): lax.all_to_all(array, 'seq', split_axis=0, concat_axis=0, axis_index_grou...  36.7 us
    all_to_all x4, starting transfers between devices, along_z(): lax.all_to_all(array, 'seq', split_axis=0, concat_axis=0, axis_index_grou...  31.5 us
    pallas_call x1, Pallas kernels, attend(): pl.pallas_call(attend_kernel, out_shape=(jax.ShapeDtypeStruct((8, 1040, 1...  17.4 us
    pallas_call x5, Pallas kernels, mover(): pl.pallas_call(kernel, out_shape=out_shape, in_specs=[smem if a.dtype ==...  15.3 us
    ppermute x17, starting transfers between devices, across(): return lax.ppermute(array, 'seq', [(i, i ^ flip) for i in range(64)])  12.6 us
    ppermute x6, starting transfers between devices, over_four(): lax.ppermute(array, axis, [(i, i ^ step * f) for i in range(size)])  6.73 us
  transfers between devices with their start and end apart: 27, of which 17 were waited for; matrix products, arithmetic and copies ran while one was open for 3% of the time, Pallas kernels for 7%

profile of v6, /device:TPU:16, one launch (start us, length us, event | category | flops | bytes accessed | tf_op | source)
XLA Modules:
  0.0 276.2 jit_solution(1913692635685089319)
XLA Ops:
  0.6 2.8 %pack.1 = bf16[8,2,2,256,128]{4,3,2,1,0:T(8,128)(2,1)} custom-call(bf16[256,2048]{1,0:T(8,128)(2,1)} %bitcast.47, bf16[256,2048]{1,0:T(8,128)(2,1)} %bitcast.48), custom_call_target="tpu_custom_call" | custom-call | bytes 4194304 | tf_op jit(solution)/shard_map/gather/pack/pallas_call | solution.py:274
  3.4 8.5 %all-to-all-start = ((bf16[8,2,2,256,128]{4,3,2,1,0:T(8,128)(2,1)}), bf16[8,2,2,256,128]{4,3,2,1,0:T(8,128)(2,1)S(1)}, u32[]{:S(2)}, u32[]{:S(2)}) async-start(bf16[8,2,2,256,128]{4,3,2,1,0:T(8,128)(2,1)} %pack.1), calls=%async_computation | async-start | bytes 4194304 | tf_op jit(solution)/shard_map/gather/all_to_all | solution.py:387
  11.9 0.7 pad_add_fusion.mine_ref
  12.6 3.0 %give.1 = bf16[8,2,256,128]{3,2,1,0:T(8,128)(2,1)} custom-call(s32[2]{0:T(128)} %pad_add_fusion.mine_ref, bf16[256,2048]{1,0:T(8,128)(2,1)} %bitcast.39, bf16[256,2048]{1,0:T(8,128)(2,1)} %bitcast.41), custom_call_target="tpu_custom_call" | custom-call | bytes 4194304 | tf_op jit(solution)/shard_map/gather/give/pallas_call | solution.py:274
  15.6 2.8 %collective-permute-start = (bf16[8,2,256,128]{3,2,1,0:T(8,128)(2,1)}, bf16[8,2,256,128]{3,2,1,0:T(8,128)(2,1)S(1)}, u32[]{:S(2)}, u32[]{:S(2)}) collective-permute-start(bf16[8,2,256,128]{3,2,1,0:T(8,128)(2,1)} %give.1), channel_id=1, source_target_pairs={{0,6},{1,7},{2,4},{3,5},{4,2},{5,3},{6,0},{7,1},{8,14},{9,15},{10,... | collective-permute-start | bytes 3145736 | tf_op jit(solution)/shard_map/gather/ppermute | solution.py:391
  18.5 0.1 copy.18
  18.6 0.7 reshape.70.list_ref
  19.2 1.2 dynamic-slice_bitcast_fusion.count_ref
  20.5 0.6 pad_add_fusion.1.info_ref
  21.1 20.7 %collective-permute-done.got_ref = bf16[8,2,256,128]{3,2,1,0:T(8,128)(2,1)S(1)} collective-permute-done((bf16[8,2,256,128]{3,2,1,0:T(8,128)(2,1)}, bf16[8,2,256,128]{3,2,1,0:T(8,128)(2,1)S(1)}, u32[]{:S(2)}, u32[]{:S(2)}) %collective-permute-start) | collective-permute-done | bytes 1048608 | tf_op jit(solution)/shard_map/gather/ppermute | solution.py:391
  41.7 1.0 copy-done.8
  42.7 3.4 %pack_pair.1 = bf16[8,2,2,256,128]{4,3,2,1,0:T(8,128)(2,1)} custom-call(s32[2]{0:T(128)} %pad_add_fusion.mine_ref, bf16[256,2048]{1,0:T(8,128)(2,1)} %bitcast.40, bf16[256,2048]{1,0:T(8,128)(2,1)} %bitcast.42, bf16[8,2,256,128]{3,2,1,0:T(8,128)(2,1)} %copy-done.8), custom_call_target="tpu_custom_call" | custom-call | bytes 4194304 | tf_op jit(solution)/shard_map/gather/pack_pair/pallas_call | solution.py:274
  46.1 17.0 %all-to-all-done.kv_hbm = bf16[8,2,2,256,128]{4,3,2,1,0:T(8,128)(2,1)S(1)} async-done(((bf16[8,2,2,256,128]{4,3,2,1,0:T(8,128)(2,1)}), bf16[8,2,2,256,128]{4,3,2,1,0:T(8,128)(2,1)S(1)}, u32[]{:S(2)}, u32[]{:S(2)}) %all-to-all-start) | async-done | bytes 2097184 | tf_op jit(solution)/shard_map/gather/all_to_all | solution.py:387
  63.1 4.4 %all-to-all-start.1 = ((bf16[8,2,2,256,128]{4,3,2,1,0:T(8,128)(2,1)}), bf16[8,2,2,256,128]{4,3,2,1,0:T(8,128)(2,1)}, u32[]{:S(2)}, u32[]{:S(2)}) async-start(bf16[8,2,2,256,128]{4,3,2,1,0:T(8,128)(2,1)} %pack_pair.1), calls=%async_computation.1 | async-start | bytes 4194304 | tf_op jit(solution)/shard_map/gather/all_to_all | solution.py:387
  67.5 3.9 %norm.1 = (bf16[2,8,256,128]{3,2,1,0:T(8,128)(2,1)}, bf16[2,8,256,128]{3,2,1,0:T(8,128)(2,1)}) custom-call(s32[2]{0:T(128)} %pad_add_fusion.mine_ref, bf16[8,2,2,256,128]{4,3,2,1,0:T(8,128)(2,1)} %copy-done.1, f32[16,128]{1,0:T(8,128)} %gain_ref.3), custom_call_target="tpu_custom_call" | custom-call | flops 10000000 | bytes 4194304 | tf_op jit(solution)/shard_map/gather/norm/pallas_call | solution.py:315
  71.4 2.8 %collective-permute-start.4 = (bf16[2,8,256,128]{3,2,1,0:T(8,128)(2,1)}, bf16[2,8,256,128]{3,2,1,0:T(8,128)(2,1)S(1)}, u32[]{:S(2)}, u32[]{:S(2)}) collective-permute-start(bf16[2,8,256,128]{3,2,1,0:T(8,128)(2,1)} %get-tuple-element.37), channel_id=1, source_target_pairs={{0,6},{1,7},{2,4},{3,5},{4,2},{5,3},{6,0},{7,1},{8,14},{9,15},{10,... | collective-permute-start | bytes 3145736 | tf_op jit(solution)/shard_map/gather/ppermute | solution.py:391
  74.3 0.2 collective-permute-start.2
  74.5 20.5 %collective-permute-done.4 = bf16[2,8,256,128]{3,2,1,0:T(8,128)(2,1)S(1)} collective-permute-done((bf16[2,8,256,128]{3,2,1,0:T(8,128)(2,1)}, bf16[2,8,256,128]{3,2,1,0:T(8,128)(2,1)S(1)}, u32[]{:S(2)}, u32[]{:S(2)}) %collective-permute-start.4) | collective-permute-done | bytes 1048608 | tf_op jit(solution)/shard_map/gather/ppermute | solution.py:391
  95.0 0.3 collective-permute-start.5
  95.3 0.5 collective-permute-start.7
  95.8 3.0 %collective-permute-done.2 = bf16[2,8,256,128]{3,2,1,0:T(8,128)(2,1)S(1)} collective-permute-done((bf16[2,8,256,128]{3,2,1,0:T(8,128)(2,1)}, bf16[2,8,256,128]{3,2,1,0:T(8,128)(2,1)S(1)}, u32[]{:S(2)}, u32[]{:S(2)}) %collective-permute-start.2) | collective-permute-done | bytes 1048608 | tf_op jit(solution)/shard_map/gather/ppermute | solution.py:391
  98.8 19.9 %collective-permute-done.5 = bf16[2,8,256,128]{3,2,1,0:T(8,128)(2,1)S(1)} collective-permute-done((bf16[2,8,256,128]{3,2,1,0:T(8,128)(2,1)S(1)}, bf16[2,8,256,128]{3,2,1,0:T(8,128)(2,1)S(1)}, u32[]{:S(2)}, u32[]{:S(2)}) %collective-permute-start.5) | collective-permute-done | bytes 1048608 | tf_op jit(solution)/shard_map/gather/ppermute | solution.py:391
  118.8 1.0 copy-done.14
  119.8 0.3 copy-done.15
  120.1 1.0 copy-done.16
  121.1 0.5 collective-permute-done.6
  121.6 17.4 %attend.1 = (bf16[8,1040,128]{2,1,0:T(8,128)(2,1)}, bf16[2,16,128,128]{3,2,1,0:T(8,128)(2,1)}, bf16[2,16,128,128]{3,2,1,0:T(8,128)(2,1)}, bf16[2,16,128,128]{3,2...) custom-call(s32[2]{0:T(128)} %pad_add_fusion.1.info_ref, ...), custom_call_target="tpu_custom_call" | custom-call | flops 6000000000 | bytes 20971520 | tf_op jit(solution)/shard_map/attend/attend/pallas_call | solution.py:180
  139.0 2.0 collective-permute-start.8
  140.9 0.1 collective-permute-start.10
  141.0 2.9 %collective-permute-done.8 = bf16[2,16,128,128]{3,2,1,0:T(8,128)(2,1)S(1)} collective-permute-done((bf16[2,16,128,128]{3,2,1,0:T(8,128)(2,1)}, bf16[2,16,128,128]{3,2,1,0:T(8,128)(2,1)S(1)}, u32[]{:S(2)}, u32[]{:S(2)}) %collective-permute-start.8) | collective-permute-done | bytes 1048608 | tf_op jit(solution)/shard_map/return/ppermute | solution.py:391
  143.9 1.6 add_convert_fusion.2
  145.6 12.1 %all-to-all-start.2 = ((bf16[8,1040,128]{2,1,0:T(8,128)(2,1)}), bf16[8,1040,128]{2,1,0:T(8,128)(2,1)S(1)}, u32[]{:S(2)}, u32[]{:S(2)}) async-start(bf16[8,1040,128]{2,1,0:T(8,128)(2,1)} %get-tuple-element.42), calls=%async_computation.2 | async-start | bytes 4259840 | tf_op jit(solution)/shard_map/return/all_to_all | solution.py:387
  157.7 2.1 add_convert_fusion.1
  159.9 0.2 collective-permute-start.13
  160.1 0.4 collective-permute-start.9
  160.5 24.5 %collective-permute-done.11 = bf16[2,16,128,128]{3,2,1,0:T(8,128)(2,1)S(1)} collective-permute-done((bf16[2,16,128,128]{3,2,1,0:T(8,128)(2,1)S(1)}, bf16[2,16,128,128]{3,2,1,0:T(8,128)(2,1)S(1)}, u32[]{:S(2)}, u32[]{:S(2)}) %collective-permute-start.11) | collective-permute-done | bytes 1048608 | tf_op jit(solution)/shard_map/return/ppermute | solution.py:391
  185.0 0.3 collective-permute-start.12
  185.3 0.5 add_convert_fusion
  185.8 0.1 collective-permute-start.14
  186.0 23.4 %collective-permute-done.12 = bf16[2,16,128,128]{3,2,1,0:T(8,128)(2,1)S(1)} collective-permute-done((bf16[2,16,128,128]{3,2,1,0:T(8,128)(2,1)S(1)}, bf16[2,16,128,128]{3,2,1,0:T(8,128)(2,1)S(1)}, u32[]{:S(2)}, u32[]{:S(2)}) %collective-permute-start.12) | collective-permute-done | bytes 1048608 | tf_op jit(solution)/shard_map/return/ppermute | solution.py:391
  209.3 2.1 collective-permute-done.14
  211.5 1.0 copy-done.5
  212.4 4.8 %finish.1 = bf16[8,2,2,256,128]{4,3,2,1,0:T(8,128)(2,1)} custom-call(s32[2]{0:T(128)} %pad_add_fusion.mine_ref, bf16[2,8,256,128]{3,2,1,0:T(8,128)(2,1)} %bitcast.43, bf16[2,8,256,128]{3,2,1,0:T(8,128)(2,1)} %bitcast.44, bf16[2,8,256,128]{3,2,1,0:T(8,128)(2,1)} %bitcast.45, bf16[2,8,256,128]{3,2,1,0:T(8,128)(2,1)} %bitcast.46, ...), custom_call_target="tpu_custom_call" | custom-call | flops 10000000 | bytes 8388608 | tf_op jit(solution)/shard_map/return/finish/pallas_call | solution.py:368
  217.2 6.6 %all-to-all-start.3 = ((bf16[8,2,2,256,128]{4,3,2,1,0:T(8,128)(2,1)}), bf16[8,2,2,256,128]{4,3,2,1,0:T(8,128)(2,1)}, u32[]{:S(2)}, u32[]{:S(2)}) async-start(bf16[8,2,2,256,128]{4,3,2,1,0:T(8,128)(2,1)} %finish.1), calls=%async_computation.3 | async-start | bytes 4194304 | tf_op jit(solution)/shard_map/return/all_to_all | solution.py:387
  223.9 1.0 slice.12
  224.9 0.3 collective-permute-start.15
  225.2 0.1 collective-permute-start.18
  225.3 0.3 collective-permute-start.17
  225.6 1.6 collective-permute-start.16
  227.2 1.2 collective-permute-done.18
  228.4 0.7 collective-permute-done.17
  229.1 2.5 collective-permute-start.19
  231.5 2.8 %collective-permute-done.19 = f32[8,2,128]{2,0,1:T(8,128)S(1)} collective-permute-done((f32[8,2,128]{2,0,1:T(8,128)S(1)}, f32[8,2,128]{2,0,1:T(8,128)S(1)}, u32[]{:S(2)}, u32[]{:S(2)}) %collective-permute-start.19) | collective-permute-done | bytes 8224 | tf_op jit(solution)/shard_map/gains/ppermute | solution.py:391
  234.3 1.2 collective-permute-start.21
  235.5 1.3 collective-permute-start.22
  236.8 2.4 collective-permute-start.20
  239.1 0.5 collective-permute-done.21
  239.7 1.2 collective-permute-done.20
  240.9 0.6 slice_bitcast_fusion
  241.5 7.8 %collective-permute-done.15.got_ref = bf16[8,512,128]{2,1,0:T(8,128)(2,1)S(1)} collective-permute-done((bf16[8,512,128]{2,1,0:T(8,128)(2,1)}, bf16[8,512,128]{2,1,0:T(8,128)(2,1)S(1)}, u32[]{:S(2)}, u32[]{:S(2)}) %collective-permute-start.15) | collective-permute-done | bytes 1048608 | tf_op jit(solution)/shard_map/return/ppermute | solution.py:391
  249.3 1.0 copy-done.6
  250.3 3.4 %unpack_front.1 = (bf16[256,2048]{1,0:T(8,128)(2,1)}, bf16[256,2048]{1,0:T(8,128)(2,1)}) custom-call(s32[2]{0:T(128)} %pad_add_fusion.mine_ref, bf16[8,1040,128]{2,1,0:T(8,128)(2,1)} %copy-done.2, bf16[8,512,128]{2,1,0:T(8,128)(2,1)} %copy-done.6), custom_call_target="tpu_custom_call" | custom-call | bytes 4194304 | tf_op jit(solution)/shard_map/return/unpack_front/pallas_call | solution.py:274
  253.7 19.7 %all-to-all-done.3.in_ref = bf16[8,2,2,256,128]{4,3,2,1,0:T(8,128)(2,1)} async-done(((bf16[8,2,2,256,128]{4,3,2,1,0:T(8,128)(2,1)}), bf16[8,2,2,256,128]{4,3,2,1,0:T(8,128)(2,1)}, u32[]{:S(2)}, u32[]{:S(2)}) %all-to-all-start.3) | async-done | bytes 2097184 | tf_op jit(solution)/shard_map/return/all_to_all | solution.py:387
  273.4 2.7 unpack.1
  (50 shorter events, 0.3 us)
Async XLA Ops:
  0.6 17.8 %copy-start = (s32[1,16,128,8]{2,3,1,0:T(8,128)S(1)}, s32[1,16,128,8]{2,3,1,0:T(8,128)}, u32[]{:S(2)}) copy-start(s32[1,16,128,8]{2,3,1,0:T(8,128)} %param.14) | copy-start | bytes 196612
  3.4 59.7 %all-to-all-start = ((bf16[8,2,2,256,128]{4,3,2,1,0:T(8,128)(2,1)}), bf16[8,2,2,256,128]{4,3,2,1,0:T(8,128)(2,1)S(1)}, u32[]{:S(2)}, u32[]{:S(2)}) async-start(bf16[8,2,2,256,128]{4,3,2,1,0:T(8,128)(2,1)} %pack.1), calls=%async_computation | async-start | bytes 4194304 | tf_op jit(solution)/shard_map/gather/all_to_all | solution.py:387
  15.6 26.1 %collective-permute-start = (bf16[8,2,256,128]{3,2,1,0:T(8,128)(2,1)}, bf16[8,2,256,128]{3,2,1,0:T(8,128)(2,1)S(1)}, u32[]{:S(2)}, u32[]{:S(2)}) collective-permute-start(bf16[8,2,256,128]{3,2,1,0:T(8,128)(2,1)} %give.1), channel_id=1, source_target_pairs={{0,6},{1,7},{2,4},{3,5},{4,2},{5,3},{6,0},{7,1},{8,14},{9,15},{10,... | collective-permute-start | bytes 3145736 | tf_op jit(solution)/shard_map/gather/ppermute | solution.py:391
  41.7 1.0 copy-start.8
  63.1 4.4 %copy-start.1 = (bf16[8,2,2,256,128]{4,3,2,1,0:T(8,128)(2,1)}, bf16[8,2,2,256,128]{4,3,2,1,0:T(8,128)(2,1)S(1)}, u32[]{:S(2)}) copy-start(bf16[8,2,2,256,128]{4,3,2,1,0:T(8,128)(2,1)S(1)} %all-to-all-done.kv_hbm) | copy-start | bytes 6291460
  63.1 58.4 %all-to-all-start.1 = ((bf16[8,2,2,256,128]{4,3,2,1,0:T(8,128)(2,1)}), bf16[8,2,2,256,128]{4,3,2,1,0:T(8,128)(2,1)}, u32[]{:S(2)}, u32[]{:S(2)}) async-start(bf16[8,2,2,256,128]{4,3,2,1,0:T(8,128)(2,1)} %pack_pair.1), calls=%async_computation.1 | async-start | bytes 4194304 | tf_op jit(solution)/shard_map/gather/all_to_all | solution.py:387
  71.4 23.6 %collective-permute-start.4 = (bf16[2,8,256,128]{3,2,1,0:T(8,128)(2,1)}, bf16[2,8,256,128]{3,2,1,0:T(8,128)(2,1)S(1)}, u32[]{:S(2)}, u32[]{:S(2)}) collective-permute-start(bf16[2,8,256,128]{3,2,1,0:T(8,128)(2,1)} %get-tuple-element.37), channel_id=1, source_target_pairs={{0,6},{1,7},{2,4},{3,5},{4,2},{5,3},{6,0},{7,1},{8,14},{9,15},{10,... | collective-permute-start | bytes 3145736 | tf_op jit(solution)/shard_map/gather/ppermute | solution.py:391
  74.3 24.5 %collective-permute-start.2 = (bf16[2,8,256,128]{3,2,1,0:T(8,128)(2,1)}, bf16[2,8,256,128]{3,2,1,0:T(8,128)(2,1)S(1)}, u32[]{:S(2)}, u32[]{:S(2)}) collective-permute-start(bf16[2,8,256,128]{3,2,1,0:T(8,128)(2,1)} %get-tuple-element.36), channel_id=1, source_target_pairs={{0,2},{1,3},{2,0},{3,1},{4,6},{5,7},{6,4},{7,5},{8,10},{9,11},{10,... | collective-permute-start | bytes 3145736 | tf_op jit(solution)/shard_map/gather/ppermute | solution.py:391
  95.0 26.5 %copy-start.10 = (bf16[2,8,256,128]{3,2,1,0:T(8,128)(2,1)}, bf16[2,8,256,128]{3,2,1,0:T(8,128)(2,1)S(1)}, u32[]{:S(2)}) copy-start(bf16[2,8,256,128]{3,2,1,0:T(8,128)(2,1)S(1)} %collective-permute-done.4) | copy-start | bytes 3145732
  95.0 23.7 %collective-permute-start.5 = (bf16[2,8,256,128]{3,2,1,0:T(8,128)(2,1)S(1)}, bf16[2,8,256,128]{3,2,1,0:T(8,128)(2,1)S(1)}, u32[]{:S(2)}, u32[]{:S(2)}) collective-permute-start(bf16[2,8,256,128]{3,2,1,0:T(8,128)(2,1)S(1)} %collective-permute-done.4), channel_id=1, source_target_pairs={{0,2},{1,3},{2,0},{3,1},{4,6},{5,7},{6,4},{7,5},{8,10},{9,11},{10,... | collective-permute-start | bytes 3145736 | tf_op jit(solution)/shard_map/gather/ppermute | solution.py:391
  95.3 23.5 %collective-permute-start.1 = (bf16[2,8,256,128]{3,2,1,0:T(8,128)(2,1)}, bf16[2,8,256,128]{3,2,1,0:T(8,128)(2,1)S(1)}, u32[]{:S(2)}, u32[]{:S(2)}) collective-permute-start(bf16[2,8,256,128]{3,2,1,0:T(8,128)(2,1)} %get-tuple-element.36), channel_id=1, source_target_pairs={{0,1},{1,0},{2,3},{3,2},{4,5},{5,4},{6,7},{7,6},{8,9},{9,8},{10,11... | collective-permute-start | bytes 3145736 | tf_op jit(solution)/shard_map/gather/ppermute | solution.py:391
  95.3 23.5 %collective-permute-start.7 = (bf16[2,8,256,128]{3,2,1,0:T(8,128)(2,1)S(1)}, bf16[2,8,256,128]{3,2,1,0:T(8,128)(2,1)S(1)}, u32[]{:S(2)}, u32[]{:S(2)}) collective-permute-start(bf16[2,8,256,128]{3,2,1,0:T(8,128)(2,1)S(1)} %collective-permute-done.4), channel_id=1, source_target_pairs={{0,1},{1,0},{2,3},{3,2},{4,5},{5,4},{6,7},{7,6},{8,9},{9,8},{10,11... | collective-permute-start | bytes 3145736 | tf_op jit(solution)/shard_map/gather/ppermute | solution.py:391
  98.8 22.8 %copy-start.12 = (bf16[2,8,256,128]{3,2,1,0:T(8,128)(2,1)}, bf16[2,8,256,128]{3,2,1,0:T(8,128)(2,1)S(1)}, u32[]{:S(2)}) copy-start(bf16[2,8,256,128]{3,2,1,0:T(8,128)(2,1)S(1)} %collective-permute-done.2) | copy-start | bytes 3145732
  98.8 20.0 %collective-permute-start.3 = (bf16[2,8,256,128]{3,2,1,0:T(8,128)(2,1)S(1)}, bf16[2,8,256,128]{3,2,1,0:T(8,128)(2,1)S(1)}, u32[]{:S(2)}, u32[]{:S(2)}) collective-permute-start(bf16[2,8,256,128]{3,2,1,0:T(8,128)(2,1)S(1)} %collective-permute-done.2), channel_id=1, source_target_pairs={{0,1},{1,0},{2,3},{3,2},{4,5},{5,4},{6,7},{7,6},{8,9},{9,8},{10,11... | collective-permute-start | bytes 3145736 | tf_op jit(solution)/shard_map/gather/ppermute | solution.py:391
  118.8 2.8 %copy-start.13 = (bf16[2,8,256,128]{3,2,1,0:T(8,128)(2,1)}, bf16[2,8,256,128]{3,2,1,0:T(8,128)(2,1)S(1)}, u32[]{:S(2)}) copy-start(bf16[2,8,256,128]{3,2,1,0:T(8,128)(2,1)S(1)} %collective-permute-done.5) | copy-start | bytes 3145732
  118.8 2.8 %collective-permute-start.6 = (bf16[2,8,256,128]{3,2,1,0:T(8,128)(2,1)S(1)}, bf16[2,8,256,128]{3,2,1,0:T(8,128)(2,1)}, u32[]{:S(2)}, u32[]{:S(2)}) collective-permute-start(bf16[2,8,256,128]{3,2,1,0:T(8,128)(2,1)S(1)} %collective-permute-done.5), channel_id=1, source_target_pairs={{0,1},{1,0},{2,3},{3,2},{4,5},{5,4},{6,7},{7,6},{8,9},{9,8},{10,11... | collective-permute-start | bytes 3145736 | tf_op jit(solution)/shard_map/gather/ppermute | solution.py:391
  118.8 1.0 copy-start.14
  118.8 1.3 copy-start.15
  120.1 1.0 copy-start.16
  139.0 5.0 %collective-permute-start.8 = (bf16[2,16,128,128]{3,2,1,0:T(8,128)(2,1)}, bf16[2,16,128,128]{3,2,1,0:T(8,128)(2,1)S(1)}, u32[]{:S(2)}, u32[]{:S(2)}) collective-permute-start(bf16[2,16,128,128]{3,2,1,0:T(8,128)(2,1)} %get-tuple-element.41), channel_id=1, source_target_pairs={{0,1},{1,0},{2,3},{3,2},{4,5},{5,4},{6,7},{7,6},{8,9},{9,8},{10,11... | collective-permute-start | bytes 3145736 | tf_op jit(solution)/shard_map/return/ppermute | solution.py:391
  140.9 16.7 %collective-permute-start.10 = (bf16[2,16,128,128]{3,2,1,0:T(8,128)(2,1)}, bf16[2,16,128,128]{3,2,1,0:T(8,128)(2,1)}, u32[]{:S(2)}, u32[]{:S(2)}) collective-permute-start(bf16[2,16,128,128]{3,2,1,0:T(8,128)(2,1)} %get-tuple-element.46), channel_id=1, source_target_pairs={{0,1},{1,0},{2,3},{3,2},{4,5},{5,4},{6,7},{7,6},{8,9},{9,8},{10,11... | collective-permute-start | bytes 3145736 | tf_op jit(solution)/shard_map/return/ppermute | solution.py:391
  145.6 71.7 %all-to-all-start.2 = ((bf16[8,1040,128]{2,1,0:T(8,128)(2,1)}), bf16[8,1040,128]{2,1,0:T(8,128)(2,1)S(1)}, u32[]{:S(2)}, u32[]{:S(2)}) async-start(bf16[8,1040,128]{2,1,0:T(8,128)(2,1)} %get-tuple-element.42), calls=%async_computation.2 | async-start | bytes 4259840 | tf_op jit(solution)/shard_map/return/all_to_all | solution.py:387
  157.6 2.3 copy-start.11
  157.6 2.5 copy-start.9
  157.6 27.7 %copy-start.7 = (bf16[2,16,128,128]{3,2,1,0:T(8,128)(2,1)S(1)}, bf16[2,16,128,128]{3,2,1,0:T(8,128)(2,1)}, u32[]{:S(2)}) copy-start(bf16[2,16,128,128]{3,2,1,0:T(8,128)(2,1)} %get-tuple-element.49) | copy-start | bytes 3145732
  159.8 25.2 %collective-permute-start.11 = (bf16[2,16,128,128]{3,2,1,0:T(8,128)(2,1)S(1)}, bf16[2,16,128,128]{3,2,1,0:T(8,128)(2,1)S(1)}, u32[]{:S(2)}, u32[]{:S(2)}) collective-permute-start(bf16[2,16,128,128]{3,2,1,0:T(8,128)(2,1)S(1)} %add_convert_fusion.1), channel_id=1, source_target_pairs={{0,2},{1,3},{2,0},{3,1},{4,6},{5,7},{6,4},{7,5},{8,10},{9,11},{10,... | collective-permute-start | bytes 3145736 | tf_op jit(solution)/shard_map/return/ppermute | solution.py:391
  159.9 25.4 %collective-permute-start.13 = (bf16[2,16,128,128]{3,2,1,0:T(8,128)(2,1)S(1)}, bf16[2,16,128,128]{3,2,1,0:T(8,128)(2,1)S(1)}, u32[]{:S(2)}, u32[]{:S(2)}) collective-permute-start(bf16[2,16,128,128]{3,2,1,0:T(8,128)(2,1)S(1)} %copy-done.11), channel_id=1, source_target_pairs={{0,1},{1,0},{2,3},{3,2},{4,5},{5,4},{6,7},{7,6},{8,9},{9,8},{10,11... | collective-permute-start | bytes 3145736 | tf_op jit(solution)/shard_map/return/ppermute | solution.py:391
  160.1 25.8 %collective-permute-start.9 = (bf16[2,16,128,128]{3,2,1,0:T(8,128)(2,1)S(1)}, bf16[2,16,128,128]{3,2,1,0:T(8,128)(2,1)S(1)}, u32[]{:S(2)}, u32[]{:S(2)}) collective-permute-start(bf16[2,16,128,128]{3,2,1,0:T(8,128)(2,1)S(1)} %copy-done.9), channel_id=1, source_target_pairs={{0,1},{1,0},{2,3},{3,2},{4,5},{5,4},{6,7},{7,6},{8,9},{9,8},{10,11... | collective-permute-start | bytes 3145736 | tf_op jit(solution)/shard_map/return/ppermute | solution.py:391
  185.0 24.3 %collective-permute-start.12 = (bf16[2,16,128,128]{3,2,1,0:T(8,128)(2,1)S(1)}, bf16[2,16,128,128]{3,2,1,0:T(8,128)(2,1)S(1)}, u32[]{:S(2)}, u32[]{:S(2)}) collective-permute-start(bf16[2,16,128,128]{3,2,1,0:T(8,128)(2,1)S(1)} %add_convert_fusion.2), channel_id=1, source_target_pairs={{0,2},{1,3},{2,0},{3,1},{4,6},{5,7},{6,4},{7,5},{8,10},{9,11},{10,... | collective-permute-start | bytes 3145736 | tf_op jit(solution)/shard_map/return/ppermute | solution.py:391
  185.8 25.6 %collective-permute-start.14 = (bf16[2,16,128,128]{3,2,1,0:T(8,128)(2,1)S(1)}, bf16[2,16,128,128]{3,2,1,0:T(8,128)(2,1)S(1)}, u32[]{:S(2)}, u32[]{:S(2)}) collective-permute-start(bf16[2,16,128,128]{3,2,1,0:T(8,128)(2,1)S(1)} %add_convert_fusion), channel_id=1, source_target_pairs={{0,6},{1,7},{2,4},{3,5},{4,2},{5,3},{6,0},{7,1},{8,14},{9,15},{10,... | collective-permute-start | bytes 3145736 | tf_op jit(solution)/shard_map/return/ppermute | solution.py:391
  185.9 25.5 %copy-start.3 = (bf16[2,16,128,128]{3,2,1,0:T(8,128)(2,1)}, bf16[2,16,128,128]{3,2,1,0:T(8,128)(2,1)S(1)}, u32[]{:S(2)}) copy-start(bf16[2,16,128,128]{3,2,1,0:T(8,128)(2,1)S(1)} %collective-permute-done.9) | copy-start | bytes 3145732
  209.3 2.1 copy-start.4
  211.5 1.0 copy-start.5
  217.2 7.9 %copy-start.2 = (bf16[8,1040,128]{2,1,0:T(8,128)(2,1)}, bf16[8,1040,128]{2,1,0:T(8,128)(2,1)S(1)}, u32[]{:S(2)}) copy-start(bf16[8,1040,128]{2,1,0:T(8,128)(2,1)S(1)} %all-to-all-done.2.in_ref) | copy-start | bytes 6389764
  217.2 56.1 %all-to-all-start.3 = ((bf16[8,2,2,256,128]{4,3,2,1,0:T(8,128)(2,1)}), bf16[8,2,2,256,128]{4,3,2,1,0:T(8,128)(2,1)}, u32[]{:S(2)}, u32[]{:S(2)}) async-start(bf16[8,2,2,256,128]{4,3,2,1,0:T(8,128)(2,1)} %finish.1), calls=%async_computation.3 | async-start | bytes 4194304 | tf_op jit(solution)/shard_map/return/all_to_all | solution.py:387
  224.9 24.4 %collective-permute-start.15 = (bf16[8,512,128]{2,1,0:T(8,128)(2,1)}, bf16[8,512,128]{2,1,0:T(8,128)(2,1)S(1)}, u32[]{:S(2)}, u32[]{:S(2)}) collective-permute-start(bf16[8,512,128]{2,1,0:T(8,128)(2,1)} %slice.12), channel_id=1, source_target_pairs={{0,6},{1,7},{2,4},{3,5},{4,2},{5,3},{6,0},{7,1},{8,14},{9,15},{10,... | collective-permute-start | bytes 3145736 | tf_op jit(solution)/shard_map/return/ppermute | solution.py:391
  225.2 3.2 %collective-permute-start.18 = (f32[8,2,128]{2,0,1:T(8,128)S(1)}, f32[8,2,128]{2,0,1:T(8,128)S(1)}, u32[]{:S(2)}, u32[]{:S(2)}) collective-permute-start(f32[8,2,128]{2,0,1:T(8,128)S(1)} %reduce_sum.9), channel_id=1, source_target_pairs={{0,3},{1,2},{2,1},{3,0},{4,7},{5,6},{6,5},{7,4},{8,11},{9,10},{10,... | collective-permute-start | bytes 24584 | tf_op jit(solution)/shard_map/gains/ppermute | solution.py:400
  225.3 3.7 %collective-permute-start.17 = (f32[8,2,128]{2,0,1:T(8,128)S(1)}, f32[8,2,128]{2,0,1:T(8,128)S(1)}, u32[]{:S(2)}, u32[]{:S(2)}) collective-permute-start(f32[8,2,128]{2,0,1:T(8,128)S(1)} %reduce_sum.9), channel_id=1, source_target_pairs={{0,2},{1,3},{2,0},{3,1},{4,6},{5,7},{6,4},{7,5},{8,10},{9,11},{10,... | collective-permute-start | bytes 24584 | tf_op jit(solution)/shard_map/gains/ppermute | solution.py:400
  225.6 3.4 %collective-permute-start.16 = (f32[8,2,128]{2,0,1:T(8,128)S(1)}, f32[8,2,128]{2,0,1:T(8,128)S(1)}, u32[]{:S(2)}, u32[]{:S(2)}) collective-permute-start(f32[8,2,128]{2,0,1:T(8,128)S(1)} %reduce_sum.9), channel_id=1, source_target_pairs={{0,1},{1,0},{2,3},{3,2},{4,5},{5,4},{6,7},{7,6},{8,9},{9,8},{10,11... | collective-permute-start | bytes 24584 | tf_op jit(solution)/shard_map/gains/ppermute | solution.py:400
  229.1 5.3 %collective-permute-start.19 = (f32[8,2,128]{2,0,1:T(8,128)S(1)}, f32[8,2,128]{2,0,1:T(8,128)S(1)}, u32[]{:S(2)}, u32[]{:S(2)}) collective-permute-start(f32[8,2,128]{2,0,1:T(8,128)S(1)} %add_add_fusion.1), channel_id=1, source_target_pairs={{0,4},{1,5},{2,6},{3,7},{4,0},{5,1},{6,2},{7,3},{8,12},{9,13},{10,... | collective-permute-start | bytes 24584 | tf_op jit(solution)/shard_map/gains/ppermute | solution.py:391
  234.3 5.3 %collective-permute-start.21 = (f32[8,2,2,128]{3,1,0,2:T(2,128)S(1)}, f32[8,2,2,128]{3,1,0,2:T(2,128)S(1)}, u32[]{:S(2)}, u32[]{:S(2)}) collective-permute-start(f32[8,2,2,128]{3,1,0,2:T(2,128)S(1)} %pad_maximum_fusion), channel_id=1, source_target_pairs={{0,128},{64,192},{128,0},{192,64},{1,129},{65,193},{129,1},{193,65... | collective-permute-start | bytes 49160 | tf_op jit(solution)/shard_map/gains/ppermute | solution.py:400
  235.5 4.2 %collective-permute-start.22 = (f32[8,2,2,128]{3,1,0,2:T(2,128)S(1)}, f32[8,2,2,128]{3,1,0,2:T(2,128)S(1)}, u32[]{:S(2)}, u32[]{:S(2)}) collective-permute-start(f32[8,2,2,128]{3,1,0,2:T(2,128)S(1)} %pad_maximum_fusion), channel_id=1, source_target_pairs={{0,192},{64,128},{128,64},{192,0},{1,193},{65,129},{129,65},{193,1... | collective-permute-start | bytes 49160 | tf_op jit(solution)/shard_map/gains/ppermute | solution.py:400
  236.8 4.1 %collective-permute-start.20 = (f32[8,2,2,128]{3,1,0,2:T(2,128)S(1)}, f32[8,2,2,128]{3,1,0,2:T(2,128)S(1)}, u32[]{:S(2)}, u32[]{:S(2)}) collective-permute-start(f32[8,2,2,128]{3,1,0,2:T(2,128)S(1)} %pad_maximum_fusion), channel_id=1, source_target_pairs={{0,64},{64,0},{128,192},{192,128},{1,65},{65,1},{129,193},{193,129... | collective-permute-start | bytes 49160 | tf_op jit(solution)/shard_map/gains/ppermute | solution.py:400
  249.3 1.0 copy-start.6

commit v7 on v6

--- a/solution.py
+++ b/solution.py
@@ -430,7 +430,8 @@
     front, parts = outs[0], outs[1:9]
     with jax.named_scope("return"):
         far = wide_sum(parts[4], across(parts[5], 1))
-        side = wide_sum(parts[2], across(parts[3], 1))
+        far, side = lax.optimization_barrier((far, across(parts[3], 1)))
+        side = wide_sum(parts[2], side)
         far = across(far, 2)
         front, side = lax.optimization_barrier((front, side))
         front = along_z(front)

time: 278 us -> 279 us (level)
  Pallas kernels: 41.4 us -> 48.6 us
  starting transfers between devices: 50.9 us -> 45 us
    pallas_call x1, Pallas kernels: 17.4 us -> 24.6 us  [attend(): pl.pallas_call(attend_kernel, out_shape=(jax.ShapeDtypeStruct((8, 1040, 1...]
    all_to_all x4, starting transfers between devices: 31.5 us -> 25.7 us  [along_z(): lax.all_to_all(array, 'seq', split_axis=0, concat_axis=0, axis_index_grou...]
where the time goes in v7:
time: 279 us; the launch traced here: 276 us
  waiting for transfers between devices  167 us (60%)
  Pallas kernels  48.6 us (17%)
  starting transfers between devices  45 us (16%)
  local copies, waits for them, and re-layouts  8.93 us (3%)
  other arithmetic  5.95 us (2%)
    ppermute x17, waiting for transfers between devices, across(): return lax.ppermute(array, 'seq', [(i, i ^ flip) for i in range(64)])  126 us
    all_to_all x4, waiting for transfers between devices, along_z(): lax.all_to_all(array, 'seq', split_axis=0, concat_axis=0, axis_index_grou...  36.8 us
    all_to_all x4, starting transfers between devices, along_z(): lax.all_to_all(array, 'seq', split_axis=0, concat_axis=0, axis_index_grou...  25.7 us
    pallas_call x1, Pallas kernels, attend(): pl.pallas_call(attend_kernel, out_shape=(jax.ShapeDtypeStruct((8, 1040, 1...  24.6 us
    pallas_call x5, Pallas kernels, mover(): pl.pallas_call(kernel, out_shape=out_shape, in_specs=[smem if a.dtype ==...  15.3 us
    ppermute x17, starting transfers between devices, across(): return lax.ppermute(array, 'seq', [(i, i ^ flip) for i in range(64)])  12.6 us
    ppermute x6, starting transfers between devices, over_four(): lax.ppermute(array, axis, [(i, i ^ step * f) for i in range(size)])  6.71 us
  transfers between devices with their start and end apart: 27, of which 17 were waited for; matrix products, arithmetic and copies ran while one was open for 3% of the time, Pallas kernels for 7%

profile of v7, /device:TPU:16, one launch (start us, length us, event | category | flops | bytes accessed | tf_op | source)
XLA Modules:
  0.0 276.2 jit_solution(6003681318715606166)
XLA Ops:
  0.6 2.8 %pack.1 = bf16[8,2,2,256,128]{4,3,2,1,0:T(8,128)(2,1)} custom-call(bf16[256,2048]{1,0:T(8,128)(2,1)} %bitcast.47, bf16[256,2048]{1,0:T(8,128)(2,1)} %bitcast.48), custom_call_target="tpu_custom_call" | custom-call | bytes 4194304 | tf_op jit(solution)/shard_map/gather/pack/pallas_call | solution.py:274
  3.4 8.5 %all-to-all-start = ((bf16[8,2,2,256,128]{4,3,2,1,0:T(8,128)(2,1)}), bf16[8,2,2,256,128]{4,3,2,1,0:T(8,128)(2,1)S(1)}, u32[]{:S(2)}, u32[]{:S(2)}) async-start(bf16[8,2,2,256,128]{4,3,2,1,0:T(8,128)(2,1)} %pack.1), calls=%async_computation | async-start | bytes 4194304 | tf_op jit(solution)/shard_map/gather/all_to_all | solution.py:387
  11.9 0.6 pad_add_fusion.mine_ref
  12.5 3.0 %give.1 = bf16[8,2,256,128]{3,2,1,0:T(8,128)(2,1)} custom-call(s32[2]{0:T(128)} %pad_add_fusion.mine_ref, bf16[256,2048]{1,0:T(8,128)(2,1)} %bitcast.39, bf16[256,2048]{1,0:T(8,128)(2,1)} %bitcast.41), custom_call_target="tpu_custom_call" | custom-call | bytes 4194304 | tf_op jit(solution)/shard_map/gather/give/pallas_call | solution.py:274
  15.5 2.8 %collective-permute-start = (bf16[8,2,256,128]{3,2,1,0:T(8,128)(2,1)}, bf16[8,2,256,128]{3,2,1,0:T(8,128)(2,1)S(1)}, u32[]{:S(2)}, u32[]{:S(2)}) collective-permute-start(bf16[8,2,256,128]{3,2,1,0:T(8,128)(2,1)} %give.1), channel_id=1, source_target_pairs={{0,6},{1,7},{2,4},{3,5},{4,2},{5,3},{6,0},{7,1},{8,14},{9,15},{10,... | collective-permute-start | bytes 3145736 | tf_op jit(solution)/shard_map/gather/ppermute | solution.py:391
  18.4 0.1 copy.18
  18.5 0.7 reshape.70.list_ref
  19.2 1.3 dynamic-slice_bitcast_fusion.count_ref
  20.4 0.6 pad_add_fusion.1.info_ref
  21.0 20.6 %collective-permute-done.got_ref = bf16[8,2,256,128]{3,2,1,0:T(8,128)(2,1)S(1)} collective-permute-done((bf16[8,2,256,128]{3,2,1,0:T(8,128)(2,1)}, bf16[8,2,256,128]{3,2,1,0:T(8,128)(2,1)S(1)}, u32[]{:S(2)}, u32[]{:S(2)}) %collective-permute-start) | collective-permute-done | bytes 1048608 | tf_op jit(solution)/shard_map/gather/ppermute | solution.py:391
  41.6 1.0 copy-done.8
  42.6 3.4 %pack_pair.1 = bf16[8,2,2,256,128]{4,3,2,1,0:T(8,128)(2,1)} custom-call(s32[2]{0:T(128)} %pad_add_fusion.mine_ref, bf16[256,2048]{1,0:T(8,128)(2,1)} %bitcast.40, bf16[256,2048]{1,0:T(8,128)(2,1)} %bitcast.42, bf16[8,2,256,128]{3,2,1,0:T(8,128)(2,1)} %copy-done.8), custom_call_target="tpu_custom_call" | custom-call | bytes 4194304 | tf_op jit(solution)/shard_map/gather/pack_pair/pallas_call | solution.py:274
  46.0 17.1 %all-to-all-done.kv_hbm = bf16[8,2,2,256,128]{4,3,2,1,0:T(8,128)(2,1)S(1)} async-done(((bf16[8,2,2,256,128]{4,3,2,1,0:T(8,128)(2,1)}), bf16[8,2,2,256,128]{4,3,2,1,0:T(8,128)(2,1)S(1)}, u32[]{:S(2)}, u32[]{:S(2)}) %all-to-all-start) | async-done | bytes 2097184 | tf_op jit(solution)/shard_map/gather/all_to_all | solution.py:387
  63.1 4.4 %all-to-all-start.1 = ((bf16[8,2,2,256,128]{4,3,2,1,0:T(8,128)(2,1)}), bf16[8,2,2,256,128]{4,3,2,1,0:T(8,128)(2,1)}, u32[]{:S(2)}, u32[]{:S(2)}) async-start(bf16[8,2,2,256,128]{4,3,2,1,0:T(8,128)(2,1)} %pack_pair.1), calls=%async_computation.1 | async-start | bytes 4194304 | tf_op jit(solution)/shard_map/gather/all_to_all | solution.py:387
  67.5 3.9 %norm.1 = (bf16[2,8,256,128]{3,2,1,0:T(8,128)(2,1)}, bf16[2,8,256,128]{3,2,1,0:T(8,128)(2,1)}) custom-call(s32[2]{0:T(128)} %pad_add_fusion.mine_ref, bf16[8,2,2,256,128]{4,3,2,1,0:T(8,128)(2,1)} %copy-done.1, f32[16,128]{1,0:T(8,128)} %gain_ref.3), custom_call_target="tpu_custom_call" | custom-call | flops 10000000 | bytes 4194304 | tf_op jit(solution)/shard_map/gather/norm/pallas_call | solution.py:315
  71.4 2.8 %collective-permute-start.4 = (bf16[2,8,256,128]{3,2,1,0:T(8,128)(2,1)}, bf16[2,8,256,128]{3,2,1,0:T(8,128)(2,1)S(1)}, u32[]{:S(2)}, u32[]{:S(2)}) collective-permute-start(bf16[2,8,256,128]{3,2,1,0:T(8,128)(2,1)} %get-tuple-element.39), channel_id=1, source_target_pairs={{0,6},{1,7},{2,4},{3,5},{4,2},{5,3},{6,0},{7,1},{8,14},{9,15},{10,... | collective-permute-start | bytes 3145736 | tf_op jit(solution)/shard_map/gather/ppermute | solution.py:391
  74.3 0.2 collective-permute-start.2
  74.5 20.5 %collective-permute-done.4 = bf16[2,8,256,128]{3,2,1,0:T(8,128)(2,1)S(1)} collective-permute-done((bf16[2,8,256,128]{3,2,1,0:T(8,128)(2,1)}, bf16[2,8,256,128]{3,2,1,0:T(8,128)(2,1)S(1)}, u32[]{:S(2)}, u32[]{:S(2)}) %collective-permute-start.4) | collective-permute-done | bytes 1048608 | tf_op jit(solution)/shard_map/gather/ppermute | solution.py:391
  95.0 0.3 collective-permute-start.5
  95.3 0.5 collective-permute-start.7
  95.8 3.0 %collective-permute-done.2 = bf16[2,8,256,128]{3,2,1,0:T(8,128)(2,1)S(1)} collective-permute-done((bf16[2,8,256,128]{3,2,1,0:T(8,128)(2,1)}, bf16[2,8,256,128]{3,2,1,0:T(8,128)(2,1)S(1)}, u32[]{:S(2)}, u32[]{:S(2)}) %collective-permute-start.2) | collective-permute-done | bytes 1048608 | tf_op jit(solution)/shard_map/gather/ppermute | solution.py:391
  98.8 20.0 %collective-permute-done.5 = bf16[2,8,256,128]{3,2,1,0:T(8,128)(2,1)S(1)} collective-permute-done((bf16[2,8,256,128]{3,2,1,0:T(8,128)(2,1)S(1)}, bf16[2,8,256,128]{3,2,1,0:T(8,128)(2,1)S(1)}, u32[]{:S(2)}, u32[]{:S(2)}) %collective-permute-start.5) | collective-permute-done | bytes 1048608 | tf_op jit(solution)/shard_map/gather/ppermute | solution.py:391
  118.8 1.0 copy-done.12
  119.8 0.3 copy-done.13
  120.1 1.0 copy-done.14
  121.1 0.5 collective-permute-done.6
  121.6 24.6 %attend.1 = (bf16[8,1040,128]{2,1,0:T(8,128)(2,1)}, bf16[2,16,128,128]{3,2,1,0:T(8,128)(2,1)}, bf16[2,16,128,128]{3,2,1,0:T(8,128)(2,1)}, bf16[2,16,128,128]{3,2...) custom-call(s32[2]{0:T(128)} %pad_add_fusion.1.info_ref, ...), custom_call_target="tpu_custom_call" | custom-call | flops 6000000000 | bytes 20971520 | tf_op jit(solution)/shard_map/attend/attend/pallas_call | solution.py:180
  146.2 0.1 collective-permute-start.8
  146.3 0.5 collective-permute-start.9
  146.8 2.4 collective-permute-done.8
  149.2 2.6 add_convert_fusion.2
  151.8 0.4 add_convert_fusion.1
  152.2 6.2 %all-to-all-start.2 = ((bf16[8,1040,128]{2,1,0:T(8,128)(2,1)}), bf16[8,1040,128]{2,1,0:T(8,128)(2,1)S(1)}, u32[]{:S(2)}, u32[]{:S(2)}) async-start(bf16[8,1040,128]{2,1,0:T(8,128)(2,1)} %get-tuple-element.47), calls=%async_computation.2 | async-start | bytes 4259840 | tf_op jit(solution)/shard_map/return/all_to_all | solution.py:387
  158.4 0.2 collective-permute-start.13
  158.6 0.4 collective-permute-start.10
  159.0 24.7 %collective-permute-done.11 = bf16[2,16,128,128]{3,2,1,0:T(8,128)(2,1)S(1)} collective-permute-done((bf16[2,16,128,128]{3,2,1,0:T(8,128)(2,1)}, bf16[2,16,128,128]{3,2,1,0:T(8,128)(2,1)S(1)}, u32[]{:S(2)}, u32[]{:S(2)}) %collective-permute-start.11) | collective-permute-done | bytes 1048608 | tf_op jit(solution)/shard_map/return/ppermute | solution.py:391
  183.8 0.3 collective-permute-start.12
  184.1 1.7 add_convert_fusion
  185.8 1.6 collective-permute-start.14
  187.4 20.6 %collective-permute-done.12 = bf16[2,16,128,128]{3,2,1,0:T(8,128)(2,1)S(1)} collective-permute-done((bf16[2,16,128,128]{3,2,1,0:T(8,128)(2,1)S(1)}, bf16[2,16,128,128]{3,2,1,0:T(8,128)(2,1)S(1)}, u32[]{:S(2)}, u32[]{:S(2)}) %collective-permute-start.12) | collective-permute-done | bytes 1048608 | tf_op jit(solution)/shard_map/return/ppermute | solution.py:391
  208.1 3.3 %collective-permute-done.14 = bf16[2,16,128,128]{3,2,1,0:T(8,128)(2,1)S(1)} collective-permute-done((bf16[2,16,128,128]{3,2,1,0:T(8,128)(2,1)S(1)}, bf16[2,16,128,128]{3,2,1,0:T(8,128)(2,1)S(1)}, u32[]{:S(2)}, u32[]{:S(2)}) %collective-permute-start.14) | collective-permute-done | bytes 1048608 | tf_op jit(solution)/shard_map/return/ppermute | solution.py:391
  211.4 1.0 copy-done.6
  212.4 4.8 %finish.1 = bf16[8,2,2,256,128]{4,3,2,1,0:T(8,128)(2,1)} custom-call(s32[2]{0:T(128)} %pad_add_fusion.mine_ref, bf16[2,8,256,128]{3,2,1,0:T(8,128)(2,1)} %bitcast.43, bf16[2,8,256,128]{3,2,1,0:T(8,128)(2,1)} %bitcast.44, bf16[2,8,256,128]{3,2,1,0:T(8,128)(2,1)} %bitcast.45, bf16[2,8,256,128]{3,2,1,0:T(8,128)(2,1)} %bitcast.46, ...), custom_call_target="tpu_custom_call" | custom-call | flops 10000000 | bytes 8388608 | tf_op jit(solution)/shard_map/return/finish/pallas_call | solution.py:368
  217.2 6.6 %all-to-all-start.3 = ((bf16[8,2,2,256,128]{4,3,2,1,0:T(8,128)(2,1)}), bf16[8,2,2,256,128]{4,3,2,1,0:T(8,128)(2,1)}, u32[]{:S(2)}, u32[]{:S(2)}) async-start(bf16[8,2,2,256,128]{4,3,2,1,0:T(8,128)(2,1)} %finish.1), calls=%async_computation.3 | async-start | bytes 4194304 | tf_op jit(solution)/shard_map/return/all_to_all | solution.py:387
  223.8 1.0 slice.12
  224.9 1.2 collective-permute-start.15
  226.1 0.1 collective-permute-start.18
  226.2 0.1 collective-permute-start.17
  226.3 1.7 collective-permute-start.16
  228.1 1.2 collective-permute-done.18
  229.3 0.7 collective-permute-done.17
  230.0 1.5 collective-permute-start.19
  231.5 3.8 %collective-permute-done.19 = f32[8,2,128]{2,0,1:T(8,128)S(1)} collective-permute-done((f32[8,2,128]{2,0,1:T(8,128)S(1)}, f32[8,2,128]{2,0,1:T(8,128)S(1)}, u32[]{:S(2)}, u32[]{:S(2)}) %collective-permute-start.19) | collective-permute-done | bytes 8224 | tf_op jit(solution)/shard_map/gains/ppermute | solution.py:391
  235.4 0.1 collective-permute-start.21
  235.5 2.2 collective-permute-start.22
  237.7 2.5 collective-permute-start.20
  240.2 0.5 collective-permute-done.21
  240.7 1.2 collective-permute-done.20
  241.9 0.6 slice_bitcast_fusion
  242.5 6.8 %collective-permute-done.15.got_ref = bf16[8,512,128]{2,1,0:T(8,128)(2,1)S(1)} collective-permute-done((bf16[8,512,128]{2,1,0:T(8,128)(2,1)}, bf16[8,512,128]{2,1,0:T(8,128)(2,1)S(1)}, u32[]{:S(2)}, u32[]{:S(2)}) %collective-permute-start.15) | collective-permute-done | bytes 1048608 | tf_op jit(solution)/shard_map/return/ppermute | solution.py:391
  249.3 1.0 copy-done.7
  250.3 3.4 %unpack_front.1 = (bf16[256,2048]{1,0:T(8,128)(2,1)}, bf16[256,2048]{1,0:T(8,128)(2,1)}) custom-call(s32[2]{0:T(128)} %pad_add_fusion.mine_ref, bf16[8,1040,128]{2,1,0:T(8,128)(2,1)} %copy-done.2, bf16[8,512,128]{2,1,0:T(8,128)(2,1)} %copy-done.7), custom_call_target="tpu_custom_call" | custom-call | bytes 4194304 | tf_op jit(solution)/shard_map/return/unpack_front/pallas_call | solution.py:274
  253.6 19.7 %all-to-all-done.3.in_ref = bf16[8,2,2,256,128]{4,3,2,1,0:T(8,128)(2,1)} async-done(((bf16[8,2,2,256,128]{4,3,2,1,0:T(8,128)(2,1)}), bf16[8,2,2,256,128]{4,3,2,1,0:T(8,128)(2,1)}, u32[]{:S(2)}, u32[]{:S(2)}) %all-to-all-start.3) | async-done | bytes 2097184 | tf_op jit(solution)/shard_map/return/all_to_all | solution.py:387
  273.3 2.7 unpack.1
  (46 shorter events, 0.2 us)
Async XLA Ops:
  0.6 17.7 %copy-start = (s32[1,16,128,8]{2,3,1,0:T(8,128)S(1)}, s32[1,16,128,8]{2,3,1,0:T(8,128)}, u32[]{:S(2)}) copy-start(s32[1,16,128,8]{2,3,1,0:T(8,128)} %param.14) | copy-start | bytes 196612
  3.4 59.7 %all-to-all-start = ((bf16[8,2,2,256,128]{4,3,2,1,0:T(8,128)(2,1)}), bf16[8,2,2,256,128]{4,3,2,1,0:T(8,128)(2,1)S(1)}, u32[]{:S(2)}, u32[]{:S(2)}) async-start(bf16[8,2,2,256,128]{4,3,2,1,0:T(8,128)(2,1)} %pack.1), calls=%async_computation | async-start | bytes 4194304 | tf_op jit(solution)/shard_map/gather/all_to_all | solution.py:387
  15.5 26.1 %collective-permute-start = (bf16[8,2,256,128]{3,2,1,0:T(8,128)(2,1)}, bf16[8,2,256,128]{3,2,1,0:T(8,128)(2,1)S(1)}, u32[]{:S(2)}, u32[]{:S(2)}) collective-permute-start(bf16[8,2,256,128]{3,2,1,0:T(8,128)(2,1)} %give.1), channel_id=1, source_target_pairs={{0,6},{1,7},{2,4},{3,5},{4,2},{5,3},{6,0},{7,1},{8,14},{9,15},{10,... | collective-permute-start | bytes 3145736 | tf_op jit(solution)/shard_map/gather/ppermute | solution.py:391
  41.6 1.0 copy-start.8
  63.1 4.4 %copy-start.1 = (bf16[8,2,2,256,128]{4,3,2,1,0:T(8,128)(2,1)}, bf16[8,2,2,256,128]{4,3,2,1,0:T(8,128)(2,1)S(1)}, u32[]{:S(2)}) copy-start(bf16[8,2,2,256,128]{4,3,2,1,0:T(8,128)(2,1)S(1)} %all-to-all-done.kv_hbm) | copy-start | bytes 6291460
  63.1 58.4 %all-to-all-start.1 = ((bf16[8,2,2,256,128]{4,3,2,1,0:T(8,128)(2,1)}), bf16[8,2,2,256,128]{4,3,2,1,0:T(8,128)(2,1)}, u32[]{:S(2)}, u32[]{:S(2)}) async-start(bf16[8,2,2,256,128]{4,3,2,1,0:T(8,128)(2,1)} %pack_pair.1), calls=%async_computation.1 | async-start | bytes 4194304 | tf_op jit(solution)/shard_map/gather/all_to_all | solution.py:387
  71.4 23.6 %collective-permute-start.4 = (bf16[2,8,256,128]{3,2,1,0:T(8,128)(2,1)}, bf16[2,8,256,128]{3,2,1,0:T(8,128)(2,1)S(1)}, u32[]{:S(2)}, u32[]{:S(2)}) collective-permute-start(bf16[2,8,256,128]{3,2,1,0:T(8,128)(2,1)} %get-tuple-element.39), channel_id=1, source_target_pairs={{0,6},{1,7},{2,4},{3,5},{4,2},{5,3},{6,0},{7,1},{8,14},{9,15},{10,... | collective-permute-start | bytes 3145736 | tf_op jit(solution)/shard_map/gather/ppermute | solution.py:391
  74.3 24.5 %collective-permute-start.2 = (bf16[2,8,256,128]{3,2,1,0:T(8,128)(2,1)}, bf16[2,8,256,128]{3,2,1,0:T(8,128)(2,1)S(1)}, u32[]{:S(2)}, u32[]{:S(2)}) collective-permute-start(bf16[2,8,256,128]{3,2,1,0:T(8,128)(2,1)} %get-tuple-element.38), channel_id=1, source_target_pairs={{0,2},{1,3},{2,0},{3,1},{4,6},{5,7},{6,4},{7,5},{8,10},{9,11},{10,... | collective-permute-start | bytes 3145736 | tf_op jit(solution)/shard_map/gather/ppermute | solution.py:391
  95.0 26.5 %copy-start.9 = (bf16[2,8,256,128]{3,2,1,0:T(8,128)(2,1)}, bf16[2,8,256,128]{3,2,1,0:T(8,128)(2,1)S(1)}, u32[]{:S(2)}) copy-start(bf16[2,8,256,128]{3,2,1,0:T(8,128)(2,1)S(1)} %collective-permute-done.4) | copy-start | bytes 3145732
  95.0 23.7 %collective-permute-start.5 = (bf16[2,8,256,128]{3,2,1,0:T(8,128)(2,1)S(1)}, bf16[2,8,256,128]{3,2,1,0:T(8,128)(2,1)S(1)}, u32[]{:S(2)}, u32[]{:S(2)}) collective-permute-start(bf16[2,8,256,128]{3,2,1,0:T(8,128)(2,1)S(1)} %collective-permute-done.4), channel_id=1, source_target_pairs={{0,2},{1,3},{2,0},{3,1},{4,6},{5,7},{6,4},{7,5},{8,10},{9,11},{10,... | collective-permute-start | bytes 3145736 | tf_op jit(solution)/shard_map/gather/ppermute | solution.py:391
  95.3 23.5 %collective-permute-start.1 = (bf16[2,8,256,128]{3,2,1,0:T(8,128)(2,1)}, bf16[2,8,256,128]{3,2,1,0:T(8,128)(2,1)S(1)}, u32[]{:S(2)}, u32[]{:S(2)}) collective-permute-start(bf16[2,8,256,128]{3,2,1,0:T(8,128)(2,1)} %get-tuple-element.38), channel_id=1, source_target_pairs={{0,1},{1,0},{2,3},{3,2},{4,5},{5,4},{6,7},{7,6},{8,9},{9,8},{10,11... | collective-permute-start | bytes 3145736 | tf_op jit(solution)/shard_map/gather/ppermute | solution.py:391
  95.3 23.5 %collective-permute-start.7 = (bf16[2,8,256,128]{3,2,1,0:T(8,128)(2,1)S(1)}, bf16[2,8,256,128]{3,2,1,0:T(8,128)(2,1)S(1)}, u32[]{:S(2)}, u32[]{:S(2)}) collective-permute-start(bf16[2,8,256,128]{3,2,1,0:T(8,128)(2,1)S(1)} %collective-permute-done.4), channel_id=1, source_target_pairs={{0,1},{1,0},{2,3},{3,2},{4,5},{5,4},{6,7},{7,6},{8,9},{9,8},{10,11... | collective-permute-start | bytes 3145736 | tf_op jit(solution)/shard_map/gather/ppermute | solution.py:391
  98.8 22.8 %copy-start.10 = (bf16[2,8,256,128]{3,2,1,0:T(8,128)(2,1)}, bf16[2,8,256,128]{3,2,1,0:T(8,128)(2,1)S(1)}, u32[]{:S(2)}) copy-start(bf16[2,8,256,128]{3,2,1,0:T(8,128)(2,1)S(1)} %collective-permute-done.2) | copy-start | bytes 3145732
  98.8 20.0 %collective-permute-start.3 = (bf16[2,8,256,128]{3,2,1,0:T(8,128)(2,1)S(1)}, bf16[2,8,256,128]{3,2,1,0:T(8,128)(2,1)S(1)}, u32[]{:S(2)}, u32[]{:S(2)}) collective-permute-start(bf16[2,8,256,128]{3,2,1,0:T(8,128)(2,1)S(1)} %collective-permute-done.2), channel_id=1, source_target_pairs={{0,1},{1,0},{2,3},{3,2},{4,5},{5,4},{6,7},{7,6},{8,9},{9,8},{10,11... | collective-permute-start | bytes 3145736 | tf_op jit(solution)/shard_map/gather/ppermute | solution.py:391
  118.8 2.8 %copy-start.11 = (bf16[2,8,256,128]{3,2,1,0:T(8,128)(2,1)}, bf16[2,8,256,128]{3,2,1,0:T(8,128)(2,1)S(1)}, u32[]{:S(2)}) copy-start(bf16[2,8,256,128]{3,2,1,0:T(8,128)(2,1)S(1)} %collective-permute-done.5) | copy-start | bytes 3145732
  118.8 2.8 %collective-permute-start.6 = (bf16[2,8,256,128]{3,2,1,0:T(8,128)(2,1)S(1)}, bf16[2,8,256,128]{3,2,1,0:T(8,128)(2,1)}, u32[]{:S(2)}, u32[]{:S(2)}) collective-permute-start(bf16[2,8,256,128]{3,2,1,0:T(8,128)(2,1)S(1)} %collective-permute-done.5), channel_id=1, source_target_pairs={{0,1},{1,0},{2,3},{3,2},{4,5},{5,4},{6,7},{7,6},{8,9},{9,8},{10,11... | collective-permute-start | bytes 3145736 | tf_op jit(solution)/shard_map/gather/ppermute | solution.py:391
  118.8 1.0 copy-start.12
  118.8 1.3 copy-start.13
  120.1 1.0 copy-start.14
  146.2 5.5 %copy-start.3 = (bf16[2,16,128,128]{3,2,1,0:T(8,128)(2,1)S(1)}, bf16[2,16,128,128]{3,2,1,0:T(8,128)(2,1)}, u32[]{:S(2)}) copy-start(bf16[2,16,128,128]{3,2,1,0:T(8,128)(2,1)} %get-tuple-element.42) | copy-start | bytes 3145732
  146.2 3.0 %collective-permute-start.8 = (bf16[2,16,128,128]{3,2,1,0:T(8,128)(2,1)}, bf16[2,16,128,128]{3,2,1,0:T(8,128)(2,1)S(1)}, u32[]{:S(2)}, u32[]{:S(2)}) collective-permute-start(bf16[2,16,128,128]{3,2,1,0:T(8,128)(2,1)} %get-tuple-element.44), channel_id=1, source_target_pairs={{0,1},{1,0},{2,3},{3,2},{4,5},{5,4},{6,7},{7,6},{8,9},{9,8},{10,11... | collective-permute-start | bytes 3145736 | tf_op jit(solution)/shard_map/return/ppermute | solution.py:391
  146.3 5.4 %collective-permute-start.9 = (bf16[2,16,128,128]{3,2,1,0:T(8,128)(2,1)}, bf16[2,16,128,128]{3,2,1,0:T(8,128)(2,1)S(1)}, u32[]{:S(2)}, u32[]{:S(2)}) collective-permute-start(bf16[2,16,128,128]{3,2,1,0:T(8,128)(2,1)} %get-tuple-element.45), channel_id=1, source_target_pairs={{0,1},{1,0},{2,3},{3,2},{4,5},{5,4},{6,7},{7,6},{8,9},{9,8},{10,11... | collective-permute-start | bytes 3145736 | tf_op jit(solution)/shard_map/return/ppermute | solution.py:391
  152.2 65.0 %all-to-all-start.2 = ((bf16[8,1040,128]{2,1,0:T(8,128)(2,1)}), bf16[8,1040,128]{2,1,0:T(8,128)(2,1)S(1)}, u32[]{:S(2)}, u32[]{:S(2)}) async-start(bf16[8,1040,128]{2,1,0:T(8,128)(2,1)} %get-tuple-element.47), calls=%async_computation.2 | async-start | bytes 4259840 | tf_op jit(solution)/shard_map/return/all_to_all | solution.py:387
  158.4 25.4 %collective-permute-start.11 = (bf16[2,16,128,128]{3,2,1,0:T(8,128)(2,1)}, bf16[2,16,128,128]{3,2,1,0:T(8,128)(2,1)S(1)}, u32[]{:S(2)}, u32[]{:S(2)}) collective-permute-start(bf16[2,16,128,128]{3,2,1,0:T(8,128)(2,1)} %add_convert_fusion.2), channel_id=1, source_target_pairs={{0,2},{1,3},{2,0},{3,1},{4,6},{5,7},{6,4},{7,5},{8,10},{9,11},{10,... | collective-permute-start | bytes 3145736 | tf_op jit(solution)/shard_map/return/ppermute | solution.py:391
  158.4 25.6 %collective-permute-start.13 = (bf16[2,16,128,128]{3,2,1,0:T(8,128)(2,1)}, bf16[2,16,128,128]{3,2,1,0:T(8,128)(2,1)S(1)}, u32[]{:S(2)}, u32[]{:S(2)}) collective-permute-start(bf16[2,16,128,128]{3,2,1,0:T(8,128)(2,1)} %get-tuple-element.54), channel_id=1, source_target_pairs={{0,1},{1,0},{2,3},{3,2},{4,5},{5,4},{6,7},{7,6},{8,9},{9,8},{10,11... | collective-permute-start | bytes 3145736 | tf_op jit(solution)/shard_map/return/ppermute | solution.py:391
  158.6 28.8 %collective-permute-start.10 = (bf16[2,16,128,128]{3,2,1,0:T(8,128)(2,1)}, bf16[2,16,128,128]{3,2,1,0:T(8,128)(2,1)S(1)}, u32[]{:S(2)}, u32[]{:S(2)}) collective-permute-start(bf16[2,16,128,128]{3,2,1,0:T(8,128)(2,1)} %get-tuple-element.49), channel_id=1, source_target_pairs={{0,1},{1,0},{2,3},{3,2},{4,5},{5,4},{6,7},{7,6},{8,9},{9,8},{10,11... | collective-permute-start | bytes 3145736 | tf_op jit(solution)/shard_map/return/ppermute | solution.py:391
  183.8 24.3 %collective-permute-start.12 = (bf16[2,16,128,128]{3,2,1,0:T(8,128)(2,1)S(1)}, bf16[2,16,128,128]{3,2,1,0:T(8,128)(2,1)S(1)}, u32[]{:S(2)}, u32[]{:S(2)}) collective-permute-start(bf16[2,16,128,128]{3,2,1,0:T(8,128)(2,1)S(1)} %add_convert_fusion.1), channel_id=1, source_target_pairs={{0,2},{1,3},{2,0},{3,1},{4,6},{5,7},{6,4},{7,5},{8,10},{9,11},{10,... | collective-permute-start | bytes 3145736 | tf_op jit(solution)/shard_map/return/ppermute | solution.py:391
  185.8 25.6 %collective-permute-start.14 = (bf16[2,16,128,128]{3,2,1,0:T(8,128)(2,1)S(1)}, bf16[2,16,128,128]{3,2,1,0:T(8,128)(2,1)S(1)}, u32[]{:S(2)}, u32[]{:S(2)}) collective-permute-start(bf16[2,16,128,128]{3,2,1,0:T(8,128)(2,1)S(1)} %add_convert_fusion), channel_id=1, source_target_pairs={{0,6},{1,7},{2,4},{3,5},{4,2},{5,3},{6,0},{7,1},{8,14},{9,15},{10,... | collective-permute-start | bytes 3145736 | tf_op jit(solution)/shard_map/return/ppermute | solution.py:391
  187.4 24.0 %copy-start.4 = (bf16[2,16,128,128]{3,2,1,0:T(8,128)(2,1)}, bf16[2,16,128,128]{3,2,1,0:T(8,128)(2,1)S(1)}, u32[]{:S(2)}) copy-start(bf16[2,16,128,128]{3,2,1,0:T(8,128)(2,1)S(1)} %collective-permute-done.10) | copy-start | bytes 3145732
  208.1 3.3 %copy-start.5 = (bf16[2,16,128,128]{3,2,1,0:T(8,128)(2,1)}, bf16[2,16,128,128]{3,2,1,0:T(8,128)(2,1)S(1)}, u32[]{:S(2)}) copy-start(bf16[2,16,128,128]{3,2,1,0:T(8,128)(2,1)S(1)} %collective-permute-done.12) | copy-start | bytes 3145732
  211.4 1.0 copy-start.6
  217.2 8.9 %copy-start.2 = (bf16[8,1040,128]{2,1,0:T(8,128)(2,1)}, bf16[8,1040,128]{2,1,0:T(8,128)(2,1)S(1)}, u32[]{:S(2)}) copy-start(bf16[8,1040,128]{2,1,0:T(8,128)(2,1)S(1)} %all-to-all-done.2.in_ref) | copy-start | bytes 6389764
  217.2 56.1 %all-to-all-start.3 = ((bf16[8,2,2,256,128]{4,3,2,1,0:T(8,128)(2,1)}), bf16[8,2,2,256,128]{4,3,2,1,0:T(8,128)(2,1)}, u32[]{:S(2)}, u32[]{:S(2)}) async-start(bf16[8,2,2,256,128]{4,3,2,1,0:T(8,128)(2,1)} %finish.1), calls=%async_computation.3 | async-start | bytes 4194304 | tf_op jit(solution)/shard_map/return/all_to_all | solution.py:387
  224.9 24.4 %collective-permute-start.15 = (bf16[8,512,128]{2,1,0:T(8,128)(2,1)}, bf16[8,512,128]{2,1,0:T(8,128)(2,1)S(1)}, u32[]{:S(2)}, u32[]{:S(2)}) collective-permute-start(bf16[8,512,128]{2,1,0:T(8,128)(2,1)} %slice.12), channel_id=1, source_target_pairs={{0,6},{1,7},{2,4},{3,5},{4,2},{5,3},{6,0},{7,1},{8,14},{9,15},{10,... | collective-permute-start | bytes 3145736 | tf_op jit(solution)/shard_map/return/ppermute | solution.py:391
  226.1 3.2 %collective-permute-start.18 = (f32[8,2,128]{2,0,1:T(8,128)S(1)}, f32[8,2,128]{2,0,1:T(8,128)S(1)}, u32[]{:S(2)}, u32[]{:S(2)}) collective-permute-start(f32[8,2,128]{2,0,1:T(8,128)S(1)} %reduce_sum.9), channel_id=1, source_target_pairs={{0,3},{1,2},{2,1},{3,0},{4,7},{5,6},{6,5},{7,4},{8,11},{9,10},{10,... | collective-permute-start | bytes 24584 | tf_op jit(solution)/shard_map/gains/ppermute | solution.py:400
  226.2 3.7 %collective-permute-start.17 = (f32[8,2,128]{2,0,1:T(8,128)S(1)}, f32[8,2,128]{2,0,1:T(8,128)S(1)}, u32[]{:S(2)}, u32[]{:S(2)}) collective-permute-start(f32[8,2,128]{2,0,1:T(8,128)S(1)} %reduce_sum.9), channel_id=1, source_target_pairs={{0,2},{1,3},{2,0},{3,1},{4,6},{5,7},{6,4},{7,5},{8,10},{9,11},{10,... | collective-permute-start | bytes 24584 | tf_op jit(solution)/shard_map/gains/ppermute | solution.py:400
  226.3 3.6 %collective-permute-start.16 = (f32[8,2,128]{2,0,1:T(8,128)S(1)}, f32[8,2,128]{2,0,1:T(8,128)S(1)}, u32[]{:S(2)}, u32[]{:S(2)}) collective-permute-start(f32[8,2,128]{2,0,1:T(8,128)S(1)} %reduce_sum.9), channel_id=1, source_target_pairs={{0,1},{1,0},{2,3},{3,2},{4,5},{5,4},{6,7},{7,6},{8,9},{9,8},{10,11... | collective-permute-start | bytes 24584 | tf_op jit(solution)/shard_map/gains/ppermute | solution.py:400
  230.0 5.3 %collective-permute-start.19 = (f32[8,2,128]{2,0,1:T(8,128)S(1)}, f32[8,2,128]{2,0,1:T(8,128)S(1)}, u32[]{:S(2)}, u32[]{:S(2)}) collective-permute-start(f32[8,2,128]{2,0,1:T(8,128)S(1)} %add_add_fusion.1), channel_id=1, source_target_pairs={{0,4},{1,5},{2,6},{3,7},{4,0},{5,1},{6,2},{7,3},{8,12},{9,13},{10,... | collective-permute-start | bytes 24584 | tf_op jit(solution)/shard_map/gains/ppermute | solution.py:391
  235.4 5.3 %collective-permute-start.21 = (f32[8,2,2,128]{3,1,0,2:T(2,128)S(1)}, f32[8,2,2,128]{3,1,0,2:T(2,128)S(1)}, u32[]{:S(2)}, u32[]{:S(2)}) collective-permute-start(f32[8,2,2,128]{3,1,0,2:T(2,128)S(1)} %pad_maximum_fusion), channel_id=1, source_target_pairs={{0,128},{64,192},{128,0},{192,64},{1,129},{65,193},{129,1},{193,65... | collective-permute-start | bytes 49160 | tf_op jit(solution)/shard_map/gains/ppermute | solution.py:400
  235.5 5.2 %collective-permute-start.22 = (f32[8,2,2,128]{3,1,0,2:T(2,128)S(1)}, f32[8,2,2,128]{3,1,0,2:T(2,128)S(1)}, u32[]{:S(2)}, u32[]{:S(2)}) collective-permute-start(f32[8,2,2,128]{3,1,0,2:T(2,128)S(1)} %pad_maximum_fusion), channel_id=1, source_target_pairs={{0,192},{64,128},{128,64},{192,0},{1,193},{65,129},{129,65},{193,1... | collective-permute-start | bytes 49160 | tf_op jit(solution)/shard_map/gains/ppermute | solution.py:400
  237.7 4.2 %collective-permute-start.20 = (f32[8,2,2,128]{3,1,0,2:T(2,128)S(1)}, f32[8,2,2,128]{3,1,0,2:T(2,128)S(1)}, u32[]{:S(2)}, u32[]{:S(2)}) collective-permute-start(f32[8,2,2,128]{3,1,0,2:T(2,128)S(1)} %pad_maximum_fusion), channel_id=1, source_target_pairs={{0,64},{64,0},{128,192},{192,128},{1,65},{65,1},{129,193},{193,129... | collective-permute-start | bytes 49160 | tf_op jit(solution)/shard_map/gains/ppermute | solution.py:400
  249.3 1.0 copy-start.7
